TPU v7x, 1024 devices: a whole 8x8x8 slice. The times are simulated.
1024 devices in a mesh: pts: 64 (over x, y), cam: 16 (over z, core).
Axes of the slice: x: 8, y: 8, z: 8, core: 2. Of those that a mesh axis runs over, the one named last changes fastest.
Arguments:
- right_side: float32 [9, 8192], P(None, 'cam'), may hold values from -6 to 6
- camera_damping: float32 [9, 8192], P(None, 'cam'), may hold values from 0.5 to 4
- preconditioner: float32 [9, 8192], P(None, 'cam'), may hold values from 0.2 to 1
- jac_cam: float32 [1024, 18, 4096], P(('pts', 'cam')), may hold values from -0.25 to 0.25
- jac_pt: float32 [1024, 6, 4096], P(('pts', 'cam')), may hold values from -3 to 3
- camera_index: int32 [1024, 4096], P(('pts', 'cam')), may hold values from 0 to 8191, as said below
- point_index: int32 [1024, 4096], P(('pts', 'cam')), may hold values from 0 to 1023, never falling along the last dimension, each value on 1 to 16 neighbouring positions
- point_damping: float32 [1024, 3, 1024], P(('pts', 'cam')), may hold values from 0.5 to 2
- anchors: int32 [16], replicated, may hold values from 0 to 8191
Outputs:
- solution: float32 [9, 8192], P(None, 'cam')
- residual: float32 [9, 8192], P(None, 'cam')
Inputs may be any that keep to these rules, and one draw needn't show every extreme that they name: `point_index`: within each device's row the point numbers never fall, and every point 0 to 1023 has 1 to 16 observations. `camera_index`: row g holds the observations of device g = p * 16 + c (p its index along pts, c along cam). Its cameras lie in the covisible tiles of 64 cameras owned by cam indices c - 1, c, c + 1 (those that exist) and the index half the axis away; tiles are used unevenly.
All inputs are finite; a program needn't handle non-finite values.
Results may differ from a plain program's by a relative error of at most 0.0001.
Values sent between devices are 32-bit elements; how exact they have to be, the bound alone decides.
No kernel may reach another device: no remote copies, remote signals or barrier semaphores. Data moves between devices by JAX's collectives and lax.ppermute only.
A program may use at most 32 MiB of HBM per device.

v0:
```python
import jax
import jax.numpy as jnp
from jax import lax
from jax.sharding import PartitionSpec as P

ITERS = 2


def point_inverse(jac_pt, point_id, damping, segments):
    rows = jac_pt.reshape(2, 3, -1)
    pairs = [(0, 0), (0, 1), (0, 2), (1, 1), (1, 2), (2, 2)]
    prods = jnp.stack(
        [jnp.sum(rows[:, first] * rows[:, second], axis=0) for first, second in pairs]
    )
    summed = jax.ops.segment_sum(prods.T, point_id, segments).T
    sym_xx = summed[0] + damping[0]
    sym_xy = summed[1]
    sym_xz = summed[2]
    sym_yy = summed[3] + damping[1]
    sym_yz = summed[4]
    sym_zz = summed[5] + damping[2]
    cof_xx = sym_yy * sym_zz - sym_yz * sym_yz
    cof_xy = sym_xz * sym_yz - sym_xy * sym_zz
    cof_xz = sym_xy * sym_yz - sym_xz * sym_yy
    cof_yy = sym_xx * sym_zz - sym_xz * sym_xz
    cof_yz = sym_xy * sym_xz - sym_xx * sym_yz
    cof_zz = sym_xx * sym_yy - sym_xy * sym_xy
    determinant = sym_xx * cof_xx + sym_xy * cof_xy + sym_xz * cof_xz
    return (
        jnp.stack([cof_xx, cof_xy, cof_xz, cof_xy, cof_yy, cof_yz, cof_xz, cof_yz, cof_zz])
        / determinant
    )


def schur_terms(whole, jac_cam, jac_pt, cam_id, point_id, inverse, segments, camera_count):
    cam_rows = jac_cam.reshape(2, 9, -1)
    pt_rows = jac_pt.reshape(2, 3, -1)
    picked = whole[:, cam_id]
    predicted = jnp.sum(cam_rows * picked[None], axis=1)
    pulled = jnp.sum(pt_rows * predicted[:, None], axis=0)
    gathered = jax.ops.segment_sum(pulled.T, point_id, segments).T
    solved = jnp.sum(inverse.reshape(3, 3, -1) * gathered[None], axis=1)
    spread = solved[:, point_id]
    leftover = predicted - jnp.sum(pt_rows * spread[None], axis=1)
    pushed = jnp.sum(cam_rows * leftover[:, None], axis=0)
    return jax.ops.segment_sum(pushed.T, cam_id, camera_count).T


def residual_inner(residual, precond):
    return lax.psum(jnp.sum(residual * precond), "cam")


def on_device(
    right_side,
    camera_damping,
    preconditioner,
    jac_cam,
    jac_pt,
    camera_index,
    point_index,
    point_damping,
    anchors,
):
    width = right_side.shape[1]
    owners = lax.axis_size("cam")
    camera_count = width * owners
    segments = point_damping.shape[2]
    cam_id = camera_index[0]
    point_id = point_index[0]
    inverse = point_inverse(jac_pt[0], point_id, point_damping[0], segments)
    first_camera = lax.axis_index("cam") * width
    owned_ids = first_camera + jnp.arange(width, dtype=jnp.int32)
    keep = 1.0 - jnp.any(anchors[:, None] == owned_ids[None, :], axis=0).astype(jnp.float32)
    solution = jnp.zeros_like(right_side)
    residual = right_side * keep
    precond = preconditioner * residual
    direction = precond
    gamma = residual_inner(residual, precond)
    for iteration in range(ITERS):
        masked = direction * keep
        whole = lax.all_gather(masked, "cam", axis=1, tiled=True)
        terms = schur_terms(
            whole, jac_cam[0], jac_pt[0], cam_id, point_id, inverse, segments, camera_count
        )
        partial_sum = lax.psum_scatter(terms, "cam", scatter_dimension=1, tiled=True)
        summed = lax.psum(partial_sum, "pts")
        image = keep * (camera_damping * masked + summed)
        alpha = gamma / lax.psum(jnp.sum(direction * image), "cam")
        solution = solution + alpha * direction
        residual = residual - alpha * image
        precond = preconditioner * residual
        fresh = residual_inner(residual, precond)
        direction = precond + fresh / gamma * direction
        gamma = fresh
    return (solution, residual)


def solution(mesh):
    return jax.shard_map(
        on_device,
        mesh=mesh,
        in_specs=(
            P(None, "cam"),
            P(None, "cam"),
            P(None, "cam"),
            P(("pts", "cam"), None, None),
            P(("pts", "cam"), None, None),
            P(("pts", "cam"), None),
            P(("pts", "cam"), None),
            P(("pts", "cam"), None, None),
            P(),
        ),
        out_specs=(P(None, "cam"), P(None, "cam")),
        check_vma=False,
    )
```

profile of v0, /device:TPU:1, one launch (start us, length us, event | category | flops | bytes accessed | tf_op | source)
XLA Modules:
  0.0 1013.4 jit_solution(234468097029168855)
XLA Ops:
  11.1 1.7 reduce.6
  12.8 32.3 %all_gather.6 = f32[9,8192]{1,0:T(8,128)S(1)} all-gather(f32[9,512]{1,0:T(8,128)S(1)} %get-tuple-element.28), channel_id=1, replica_groups=mesh['pts'=64,'cam'=16] {'cam'}, dimensions={1}, use_global_device_ids=true | all-gather | bytes 313344 | tf_op jit(solution)/shard_map/all_gather | solution.py:81
  45.9 24.9 %scatter_custom_fusion = f32[1024,6]{1,0:T(8,128)} fusion(s32[4096]{0:T(1024)} %bitcast.77, f32[4096,6]{1,0:T(8,128)S(1)} %copy.116, f32[]{:T(128)} %constant.1.clone.1), kind=kCustom, calls=%fused_computation.21 | custom fusion | flops 24576 | bytes 25088 | tf_op jit(solution)/shard_map/scatter-add | solution.py:15
  70.8 1.2 copy.117
  73.7 2.6 copy.114
  76.3 13.0 %gather_fusion = f32[4096,9]{1,0:T(8,128)S(1)} fusion(f32[9,8192]{0,1:T(8,128)} %copy.114, s32[4096]{0:T(1024)S(1)} %broadcast_clamp_fusion.1), kind=kCustom, calls=%fused_computation | custom fusion | bytes 311296 | tf_op jit(solution)/shard_map/gather | solution.py:38
  90.7 24.3 %scatter_custom_fusion.1 = f32[1024,3]{1,0:T(8,128)S(1)} fusion(s32[4096]{0:T(1024)} %bitcast.78, f32[4096,3]{1,0:T(8,128)S(1)} %copy.118, f32[]{:T(128)} %constant.1.clone.1), kind=kCustom, calls=%fused_computation.19 | custom fusion | flops 12288 | bytes 12800 | tf_op jit(solution)/shard_map/scatter-add | solution.py:41
  115.4 10.8 %gather_fusion.1 = f32[4096,3]{1,0:T(8,128)S(1)} fusion(f32[3,1024]{0,1:T(8,128)S(1)} %copy.120, s32[4096]{0:T(1024)S(1)} %broadcast_clamp_fusion), kind=kCustom, calls=%fused_computation.1 | custom fusion | bytes 114688 | tf_op jit(solution)/shard_map/gather | solution.py:43
  127.7 24.6 %scatter_custom_fusion.2 = f32[8192,9]{1,0:T(8,128)} fusion(s32[4096]{0:T(1024)} %bitcast.80, f32[4096,9]{1,0:T(8,128)S(1)} %copy.122, f32[]{:T(128)} %constant.1.clone.1), kind=kCustom, calls=%fused_computation.11 | custom fusion | flops 36864 | bytes 295424 | tf_op jit(solution)/shard_map/scatter-add | solution.py:46
  152.3 3.6 copy.123
  155.9 57.9 %reduce-scatter.3.cloned.1.call-done = f32[9,512]{1,0:T(8,128)} async-done(((f32[9,8192]{1,0:T(8,128)}), f32[9,512]{1,0:T(8,128)}) %reduce-scatter.3.cloned.1.call-update) | async-done | bytes 18448 | tf_op jit(solution)/shard_map/reduce_scatter | solution.py:85
  213.8 224.1 %psum.43 = f32[9,512]{1,0:T(8,128)S(1)} all-reduce(f32[9,512]{1,0:T(8,128)} %reduce-scatter.3.cloned.1.call-done), channel_id=1, replica_groups=mesh['pts'=64,'cam'=16] {'pts'}, use_global_device_ids=true, to_apply=%region_18.0 | all-reduce | flops 4608 | bytes 36864 | tf_op jit(solution)/shard_map/psum | solution.py:86
  438.6 81.9 %all-reduce = (f32[]{:T(128)}, f32[]{:T(128)}) all-reduce(f32[]{:T(128)} %get-tuple-element.17, f32[]{:T(128)} %get-tuple-element.16), channel_id=1, replica_groups=mesh['pts'=64,'cam'=16] {'cam'}, use_global_device_ids=true, to_apply=%region_2.0 | all-reduce | flops 2 | bytes 16 | tf_op jit(solution)/shard_map/psum | solution.py:50
  522.5 24.2 %psum.45 = f32[]{:T(128)} all-reduce(f32[]{:T(128)} %get-tuple-element.20), channel_id=1, replica_groups=mesh['pts'=64,'cam'=16] {'cam'}, use_global_device_ids=true, to_apply=%region_22.0 | all-reduce | flops 1 | bytes 8 | tf_op jit(solution)/shard_map/psum | solution.py:50
  548.0 16.2 %all_gather.7 = f32[9,8192]{1,0:T(8,128)S(1)} all-gather(f32[9,512]{1,0:T(8,128)S(1)} %broadcast_multiply_fusion), channel_id=1, replica_groups=mesh['pts'=64,'cam'=16] {'cam'}, dimensions={1}, use_global_device_ids=true | all-gather | bytes 313344 | tf_op jit(solution)/shard_map/all_gather | solution.py:81
  564.2 2.6 copy.124
  566.8 13.0 %gather_fusion.2 = f32[4096,9]{1,0:T(8,128)S(1)} fusion(f32[9,8192]{0,1:T(8,128)} %copy.124, s32[4096]{0:T(1024)S(1)} %broadcast_clamp_fusion.1), kind=kCustom, calls=%fused_computation.2 | custom fusion | bytes 311296 | tf_op jit(solution)/shard_map/gather | solution.py:38
  581.3 24.3 %scatter_custom_fusion.3 = f32[1024,3]{1,0:T(8,128)S(1)} fusion(s32[4096]{0:T(1024)} %bitcast.79, f32[4096,3]{1,0:T(8,128)S(1)} %copy.126, f32[]{:T(128)} %constant.1.clone.1), kind=kCustom, calls=%fused_computation.17 | custom fusion | flops 12288 | bytes 12800 | tf_op jit(solution)/shard_map/scatter-add | solution.py:41
  606.0 10.8 %gather_fusion.3 = f32[4096,3]{1,0:T(8,128)S(1)} fusion(f32[3,1024]{0,1:T(8,128)S(1)} %copy.128, s32[4096]{0:T(1024)S(1)} %broadcast_clamp_fusion), kind=kCustom, calls=%fused_computation.3 | custom fusion | bytes 114688 | tf_op jit(solution)/shard_map/gather | solution.py:43
  618.2 24.6 %scatter_custom_fusion.4 = f32[8192,9]{1,0:T(8,128)} fusion(s32[4096]{0:T(1024)} %bitcast.81, f32[4096,9]{1,0:T(8,128)S(1)} %copy.130, f32[]{:T(128)} %constant.1.clone.1), kind=kCustom, calls=%fused_computation.9 | custom fusion | flops 36864 | bytes 295424 | tf_op jit(solution)/shard_map/scatter-add | solution.py:46
  642.9 3.5 copy.131
  646.4 51.7 %reduce-scatter.5.cloned.1.call-done = f32[9,512]{1,0:T(8,128)} async-done(((f32[9,8192]{1,0:T(8,128)}), f32[9,512]{1,0:T(8,128)}) %reduce-scatter.5.cloned.1.call-update) | async-done | bytes 18448 | tf_op jit(solution)/shard_map/reduce_scatter | solution.py:85
  698.2 223.9 %psum.46 = f32[9,512]{1,0:T(8,128)S(1)} all-reduce(f32[9,512]{1,0:T(8,128)} %reduce-scatter.5.cloned.1.call-done), channel_id=1, replica_groups=mesh['pts'=64,'cam'=16] {'pts'}, use_global_device_ids=true, to_apply=%region_31.0 | all-reduce | flops 4608 | bytes 36864 | tf_op jit(solution)/shard_map/psum | solution.py:86
  922.7 81.9 %psum.47 = f32[]{:T(128)} all-reduce(f32[]{:T(128)} %multiply_reduce_fusion.10), channel_id=1, replica_groups=mesh['pts'=64,'cam'=16] {'cam'}, use_global_device_ids=true, to_apply=%region_33.0 | all-reduce | flops 1 | bytes 8 | tf_op jit(solution)/shard_map/psum | solution.py:88
  (59 shorter events, 15.5 us)
Async XLA Ops:
  7.2 5.6 copy-start.1
  7.2 5.6 copy-start.2
  7.2 206.6 %reduce-scatter.3.cloned.1.call-start = ((), (), s32[]{:S(2)}) async-start(), calls=%async_computation.2 | async-start | bytes 557056 | tf_op jit(solution)/shard_map/reduce_scatter | solution.py:85
  152.3 285.7 %copy-start = (f32[9,512]{1,0:T(8,128)S(1)}, f32[9,512]{1,0:T(8,128)}, u32[]{:S(2)}) copy-start(f32[9,512]{1,0:T(8,128)} %param.10) | copy-start | bytes 55300
  152.3 369.6 %copy-start.3 = (f32[9,512]{1,0:T(8,128)S(1)}, f32[9,512]{1,0:T(8,128)}, u32[]{:S(2)}) copy-start(f32[9,512]{1,0:T(8,128)} %param.11) | copy-start | bytes 55300
  155.9 542.3 %reduce-scatter.5.cloned.1.call-start = ((), (), s32[]{:S(2)}) async-start(), calls=%async_computation.3 | async-start | bytes 557056 | tf_op jit(solution)/shard_map/reduce_scatter | solution.py:85
Sparse Core Ops, SparseCore 0:
  156.0 57.7 reduce-scatter.2
  646.6 51.5 reduce-scatter.4
where the time goes:
time: 1010 us
  blocking collectives  685 us (68%)
  other arithmetic  133 us (13%)
  waiting for transfers between devices  110 us (11%)
  local copies, waits for them, and re-layouts  67.8 us (7%)
  between operations  18.4 us (2%)
    psum x2, blocking collectives, on_device(): summed = lax.psum(partial_sum, 'pts')  448 us
    reduce_scatter x2, waiting for transfers between devices, on_device(): lax.psum_scatter(terms, 'cam', scatter_dimension=1, tiled=True)  110 us
    psum x2, blocking collectives, residual_inner(): return lax.psum(jnp.sum(residual * precond), 'cam')  106 us
    psum x1, blocking collectives, on_device(): alpha = gamma / lax.psum(jnp.sum(direction * image), 'cam')  81.9 us
    scatter-add x2, other arithmetic, schur_terms(): return jax.ops.segment_sum(pushed.T, cam_id, camera_count).T  49.2 us
    all_gather x2, blocking collectives, on_device(): whole = lax.all_gather(masked, 'cam', axis=1, tiled=True)  48.5 us
    scatter-add x2, other arithmetic, schur_terms(): gathered = jax.ops.segment_sum(pulled.T, point_id, segments).T  48.5 us
    gather x4, local copies, waits for them, and re-layouts, schur_terms(): picked = whole[:, cam_id]  27.1 us
  transfers between devices with their start and end apart: 2, of which 2 were waited for; matrix products, arithmetic and copies ran while one was open for 0% of the time, Pallas kernels for 0%

commit v1 on v0

v1 whole, which is shorter than its diff:
```python
import functools

import jax
import jax.numpy as jnp
from jax import lax
from jax.experimental import pallas as pl
from jax.experimental.pallas import tpu as pltpu
from jax.sharding import PartitionSpec as P

LANES = 128
BLOCKS = 4
F32, BF16 = jnp.float32, jnp.bfloat16
VMEM = pl.BlockSpec(memory_space=pltpu.VMEM)
SMEM = pl.BlockSpec(memory_space=pltpu.SMEM)
PARAMS = pltpu.CompilerParams(vmem_limit_bytes=40 * 1024 * 1024)


def split(value):
    high = value.astype(BF16)
    low = (value - high.astype(F32)).astype(BF16)
    return high, low


def one_hot(row, count):
    ids = lax.broadcasted_iota(jnp.int32, (count, row.shape[1]), 0)
    return jnp.where(ids == row, 1.0, 0.0)


def same_before(point, step):
    return jnp.where(pltpu.roll(point, step, 1) == point, 1.0, 0.0)


def point_totals(value, point, steps):
    count = point.shape[1]
    before = value
    after = value
    for step in steps:
        mask = same_before(point, step)
        before = before + mask * pltpu.roll(before, step, 1)
        mask_after = pltpu.roll(mask, count - step, 1)
        after = after + mask_after * pltpu.roll(after, count - step, 1)
    return before + (after - value)


def setup_kernel(steps, width, owners, position, jac_pt, point_ref, damping, camera_ref, inverse, local):
    camera = camera_ref[...]
    shift = (camera // width - position[0] + owners) % owners
    block = jnp.where(shift == 1, 1, jnp.where(shift == owners - 1, 2, 3))
    block = jnp.where(shift == 0, 0, block)
    local[...] = block * width + camera % width

    point = point_ref[...]
    count = point.shape[1]
    tiles = damping.shape[1] // LANES
    rows = [jac_pt[r : r + 1, :] for r in range(6)]
    pairs = [(0, 0), (0, 1), (0, 2), (1, 1), (1, 2), (2, 2)]
    prods = [rows[a] * rows[b] + rows[3 + a] * rows[3 + b] for a, b in pairs]
    prods = jnp.concatenate(prods + [jnp.zeros((2, count), F32)], axis=0)
    summed = point_totals(prods, point, steps)

    hot = one_hot(point % LANES, LANES).astype(BF16)
    tile_mask = one_hot(point // LANES, tiles)
    table = jnp.concatenate(
        [damping[k : k + 1, t * LANES : (t + 1) * LANES] for k in range(3) for t in range(tiles)],
        axis=0,
    )
    high = table.astype(BF16)
    rest = table - high.astype(F32)
    mid = rest.astype(BF16)
    low = (rest - mid.astype(F32)).astype(BF16)
    picked = sum(
        jnp.dot(part, hot, preferred_element_type=F32) for part in (high, mid, low)
    )
    damp = [
        jnp.sum(picked[k * tiles : (k + 1) * tiles] * tile_mask, axis=0, keepdims=True)
        for k in range(3)
    ]
    xx = summed[0:1] + damp[0]
    xy = summed[1:2]
    xz = summed[2:3]
    yy = summed[3:4] + damp[1]
    yz = summed[4:5]
    zz = summed[5:6] + damp[2]
    cof_xx = yy * zz - yz * yz
    cof_xy = xz * yz - xy * zz
    cof_xz = xy * yz - xz * yy
    cof_yy = xx * zz - xz * xz
    cof_yz = xy * xz - xx * yz
    cof_zz = xx * yy - xy * xy
    det = xx * cof_xx + xy * cof_xy + xz * cof_xz
    inverse[0:1] = cof_xx / det
    inverse[1:2] = cof_xy / det
    inverse[2:3] = cof_xz / det
    inverse[3:4] = cof_yy / det
    inverse[4:5] = cof_yz / det
    inverse[5:6] = cof_zz / det
    inverse[6:8] = jnp.zeros((2, count), F32)


def own_rows(value):
    ids = lax.broadcasted_iota(jnp.int32, value.shape, 0)
    return jnp.where(ids % BLOCKS == 0, value, 0.0)


def lane_sums(value):
    return jnp.sum(value, axis=0, keepdims=True)


def schur(vector, where, jac_cam, jac_pt, camera, point_ref, inverse, hot, error, chunk, params, half, steps):
    count = camera.shape[1]
    slots = 2 * BLOCKS
    table = vector.reshape(params, half, slots, LANES)
    table = jnp.concatenate(
        [table[:, h].reshape(params * slots, LANES) for h in range(half)], axis=1
    )
    high, low = split(table)
    rows = params * slots

    def masks(span):
        camera_row = camera[:, span]
        tile = (camera_row // LANES) % (2 * half)
        slot = (tile % 2) * BLOCKS + camera_row // (2 * half * LANES)
        lane = (tile // 2) * LANES + camera_row % LANES
        return slot, lane

    def predict(i, _):
        span = pl.ds(pl.multiple_of(i * chunk, chunk), chunk)
        slot, lane = masks(span)
        spot = one_hot(lane, half * LANES).astype(BF16)
        hot[:, span] = spot
        got = jnp.dot(high, spot, preferred_element_type=F32)
        got = got + jnp.dot(low, spot, preferred_element_type=F32)
        mask = one_hot(slot, slots)
        for r in range(2):
            total = jnp.zeros((slots, chunk), F32)
            for a in range(params):
                jac = jac_cam[r * params + a : r * params + a + 1, span]
                total = total + jac * got[a * slots : (a + 1) * slots]
            error[r : r + 1, span] = lane_sums(total * mask)
        return 0

    lax.fori_loop(0, count // chunk, predict, 0)

    e0, e1 = error[0:1, :], error[1:2, :]
    jp = [jac_pt[r : r + 1, :] for r in range(6)]
    pulled = [jp[k] * e0 + jp[3 + k] * e1 for k in range(3)]
    pulled = jnp.concatenate(pulled + [jnp.zeros((5, count), F32)], axis=0)
    sums = point_totals(pulled, point_ref[...], steps)
    y0, y1, y2 = sums[0:1], sums[1:2], sums[2:3]
    inv = [inverse[r : r + 1, :] for r in range(6)]
    z = (
        inv[0] * y0 + inv[1] * y1 + inv[2] * y2,
        inv[1] * y0 + inv[3] * y1 + inv[4] * y2,
        inv[2] * y0 + inv[4] * y1 + inv[5] * y2,
    )
    left0 = e0 - (jp[0] * z[0] + jp[1] * z[1] + jp[2] * z[2])
    left1 = e1 - (jp[3] * z[0] + jp[4] * z[1] + jp[5] * z[2])
    energy = e0 * left0 + e1 * left1
    error[0:1, :] = left0
    error[1:2, :] = left1

    def push(i, total):
        span = pl.ds(pl.multiple_of(i * chunk, chunk), chunk)
        slot, _ = masks(span)
        mask = one_hot(slot, slots)
        first, second = error[0:1, span], error[1:2, span]
        highs, lows = [], []
        for a in range(params):
            value = jac_cam[a : a + 1, span] * first
            value = value + jac_cam[params + a : params + a + 1, span] * second
            near = value.astype(BF16).astype(F32)
            highs.append(near * mask)
            lows.append((value - near) * mask)
        both = jnp.concatenate(highs + lows, axis=0).astype(BF16)
        return total + lax.dot_general(
            both, hot[:, span], (((1,), (1,)), ((), ())), preferred_element_type=F32
        )

    total = lax.fori_loop(
        0, count // chunk, push, jnp.zeros((2 * rows, half * LANES), F32)
    )
    total = total[:rows] + total[rows:]
    for a in range(params):
        for h in range(half):
            start = (a * half + h) * slots
            where[start : start + slots, :] = total[
                a * slots : (a + 1) * slots, h * LANES : (h + 1) * LANES
            ]
    return sum(energy[:, t * LANES : (t + 1) * LANES] for t in range(count // LANES))


def prepare_kernel(position, anchors, right_side, camera_damping, preconditioner, bundle, kept):
    params, width = right_side.shape
    tiles = width // LANES
    ids = position[0] * width + lax.broadcasted_iota(jnp.int32, (1, width), 1)
    keep = jnp.ones((1, width), F32)
    for index in range(anchors.shape[0]):
        keep = jnp.where(ids == anchors[index], 0.0, keep)
    weights = preconditioner[...] * keep
    kept[...] = jnp.broadcast_to(keep, kept.shape)
    for t in range(tiles):
        lanes = slice(t * LANES, (t + 1) * LANES)
        for which, value in enumerate((right_side[...], weights, camera_damping[...])):
            place = pl.ds(which * params * tiles + t, params, stride=tiles)
            bundle[place, :] = value[:, lanes]


def send_rows(send, data_rows, rows):
    rest = send.shape[0] - data_rows
    send[data_rows:, :] = jnp.zeros((rest, LANES), F32)
    for index, row in enumerate(rows):
        send[data_rows + index : data_rows + index + 1, :] = row


def first_kernel(sizes, share, own, after, before, across, jac_cam, jac_pt, camera, point,
                 inverse, send, state, hot, error):
    chunk, params, half, steps = sizes
    data_rows = params * 2 * half * BLOCKS
    per = params * 2 * half
    for block, bundle in enumerate((own, after, before, across)):
        for which in range(3):
            place = pl.ds(which * data_rows + block, per, stride=BLOCKS)
            state[place, :] = bundle[which * per : (which + 1) * per, :]
    right = state[0:data_rows, :]
    vector = state[data_rows : 2 * data_rows, :] * right
    damping = state[2 * data_rows :, :]
    energy = schur(vector, send, jac_cam, jac_pt, camera, point, inverse, hot, error,
                   chunk, params, half, steps)
    energy = energy + share * lane_sums(own_rows(damping * vector * vector))
    gamma = share * lane_sums(own_rows(right * vector))
    send_rows(send, data_rows, (energy, gamma))


def scalar(ref, row):
    return jnp.sum(ref[row : row + 1, :], axis=1, keepdims=True)


def second_kernel(sizes, share, received, state, jac_cam, jac_pt, camera, point, inverse,
                  send, hot, error):
    chunk, params, half, steps = sizes
    data_rows = params * 2 * half * BLOCKS
    right = state[0:data_rows, :]
    weights = state[data_rows : 2 * data_rows, :]
    damping = state[2 * data_rows :, :]
    alpha = scalar(received, data_rows + 1) / scalar(received, data_rows)
    image = damping * (weights * right) + received[0:data_rows, :]
    residual = right - alpha * image
    vector = weights * residual
    energy = schur(vector, send, jac_cam, jac_pt, camera, point, inverse, hot, error,
                   chunk, params, half, steps)
    energy = energy + share * lane_sums(own_rows(damping * vector * vector))
    fresh = share * lane_sums(own_rows(residual * vector))
    cross = share * lane_sums(own_rows(image * vector))
    send_rows(send, data_rows, (energy, fresh, cross))


def last_kernel(half, first, second, state, kept, solution, residual):
    params, width = solution.shape
    tiles = 2 * half
    data_rows = params * tiles * BLOCKS
    curve, gamma = scalar(first, data_rows), scalar(first, data_rows + 1)
    alpha = gamma / curve
    energy, fresh = scalar(second, data_rows), scalar(second, data_rows + 1)
    cross = scalar(second, data_rows + 2)
    beta = fresh / gamma
    alpha_next = fresh / (energy + 2.0 * beta * cross + beta * beta * curve)
    for t in range(tiles):
        def own(ref, base):
            return ref[pl.ds(base + t * BLOCKS, params, stride=tiles * BLOCKS), :]

        right, weights, damping = (own(state, which * data_rows) for which in range(3))
        start = weights * right
        image = damping * start + own(first, 0)
        left = right - alpha * image
        vector = weights * left
        direction = vector + beta * start
        image_next = damping * vector + own(second, 0) + beta * image
        lanes = slice(t * LANES, (t + 1) * LANES)
        keep = kept[0:1, lanes]
        solution[:, lanes] = alpha * start + alpha_next * direction
        residual[:, lanes] = keep * (left - alpha_next * image_next)


def spread_kernel(received, send):
    total = received[0:8, :]
    for start in range(8, received.shape[0], 8):
        total = total + received[start : start + 8, :]
    total = total[0:BLOCKS] + total[BLOCKS:]
    total = jnp.concatenate([total, total], axis=0)
    for start in range(0, send.shape[0], 8):
        send[start : start + 8, :] = total


def combine_kernel(position, received, send):
    owners = received.shape[0] // BLOCKS
    me = position[0]

    def row(owner, block):
        spot = lax.rem(owner + 2 * owners, owners) * BLOCKS + block
        return received[pl.ds(spot, 1), :]

    def block_sum(owner):
        return (row(owner, 0) + row(owner - 1, 1)) + (
            row(owner + 1, 2) + row(owner + owners // 2, 3)
        )

    blocks = [block_sum(me + shift) for shift in (0, 1, -1, owners // 2)]
    joined = jnp.concatenate(blocks, axis=0)
    total = received[0:BLOCKS, :]
    for owner in range(1, owners):
        total = total + received[owner * BLOCKS : (owner + 1) * BLOCKS, :]
    joined = jnp.where(position[1] == 1, total, joined)
    joined = jnp.concatenate([joined, joined], axis=0)
    for start in range(0, send.shape[0], 8):
        send[start : start + 8, :] = joined


def call(kernel, outs, specs, *args, scratch=(), name=None):
    shapes = [jax.ShapeDtypeStruct(shape, dtype) for shape, dtype in outs]
    single = len(shapes) == 1
    return pl.pallas_call(
        kernel,
        out_shape=shapes[0] if single else shapes,
        in_specs=specs,
        out_specs=VMEM if single else [VMEM] * len(shapes),
        scratch_shapes=list(scratch),
        compiler_params=PARAMS,
        name=name,
    )(*args)


def swap(value, axis, size):
    value = value.reshape(size, BLOCKS, LANES)
    return lax.all_to_all(value, axis, 0, 0).reshape(size * BLOCKS, LANES)


def on_device(right_side, camera_damping, preconditioner, jac_cam, jac_pt, camera_index,
              point_index, point_damping, anchors):
    params, width = right_side.shape
    owners, rows = lax.axis_size("cam"), lax.axis_size("pts")
    tiles = width // LANES
    half = tiles // 2
    per = params * tiles
    data_rows = per * BLOCKS
    count = camera_index.shape[1]
    me = lax.axis_index("cam").astype(jnp.int32)
    position = jnp.stack([me, (lax.axis_index("pts") == per).astype(jnp.int32)])
    jac_cam, jac_pt = jac_cam[0], jac_pt[0]
    steps = (1, 2, 4, 8)
    sizes = (512, params, half, steps)
    share = 1.0 / rows

    bundle, kept = call(
        prepare_kernel, [((3 * per, LANES), F32), ((8, width), F32)],
        [SMEM, SMEM] + [VMEM] * 3, position, anchors, right_side, camera_damping,
        preconditioner, name="prepare",
    )
    after, before, across = (
        lax.ppermute(bundle, "cam", [(i, (i - d) % owners) for i in range(owners)])
        for d in (1, -1, owners // 2)
    )
    inverse, local = call(
        functools.partial(setup_kernel, steps, width, owners),
        [((8, count), F32), ((1, count), jnp.int32)],
        [SMEM] + [VMEM] * 4, position, jac_pt, point_index, point_damping[0], camera_index,
        name="invert",
    )
    scratch = (pltpu.VMEM((half * LANES, count), BF16), pltpu.VMEM((8, count), F32))
    send, state = call(
        functools.partial(first_kernel, sizes, share),
        [((rows * BLOCKS, LANES), F32), ((3 * data_rows, LANES), F32)],
        [VMEM] * 9, bundle, after, before, across, jac_cam, jac_pt, local, point_index,
        inverse, scratch=scratch, name="apply_first",
    )

    def reduce(send):
        chunks = swap(send, "pts", rows)
        chunks = call(spread_kernel, [((owners * BLOCKS, LANES), F32)], [VMEM], chunks, name="spread")
        chunks = swap(chunks, "cam", owners)
        chunks = call(
            combine_kernel, [((rows * BLOCKS, LANES), F32)], [SMEM, VMEM], position, chunks,
            name="combine",
        )
        return swap(chunks, "pts", rows)

    first = reduce(send)
    send = call(
        functools.partial(second_kernel, sizes, share), [((rows * BLOCKS, LANES), F32)],
        [VMEM] * 7, first, state, jac_cam, jac_pt, local, point_index, inverse,
        scratch=scratch, name="apply_second",
    )
    second = reduce(send)
    return tuple(
        call(
            functools.partial(last_kernel, half), [((params, width), F32)] * 2, [VMEM] * 4,
            first, second, state, kept, name="finish",
        )
    )


def solution(mesh):
    return jax.shard_map(
        on_device,
        mesh=mesh,
        in_specs=(
            P(None, "cam"),
            P(None, "cam"),
            P(None, "cam"),
            P(("pts", "cam"), None, None),
            P(("pts", "cam"), None, None),
            P(("pts", "cam"), None),
            P(("pts", "cam"), None),
            P(("pts", "cam"), None, None),
            P(),
        ),
        out_specs=(P(None, "cam"), P(None, "cam")),
        check_vma=False,
    )
```

time: 1010 us -> 138 us (0.14)
  blocking collectives: 685 us -> 99.4 us
  other arithmetic: 133 us -> 0.08 us
  waiting for transfers between devices: 110 us -> 0.06 us
  local copies, waits for them, and re-layouts: 67.8 us -> 4.53 us
  starting transfers between devices: 0.08 us -> 18.1 us
  between operations: 18.4 us -> 0.76 us
  Pallas kernels: 0 us -> 14.6 us
    psum x5 -> x0, blocking collectives: 636 us -> none  [the longest x2 448 us: on_device(): summed = lax.psum(partial_sum, 'pts')]
    scatter-add x5 -> x0, other arithmetic: 123 us -> none  [the longest x2 49.2 us: schur_terms(): return jax.ops.segment_sum(pushed.T, cam_id, camera_count).T]
    reduce_scatter x2 -> x0, waiting for transfers between devices: 110 us -> none  [on_device(): lax.psum_scatter(terms, 'cam', scatter_dimension=1, tiled=True)]
    all_to_all x0 -> x6, blocking collectives: none -> 99.4 us  [swap(): return lax.all_to_all(value, axis, 0, 0).reshape(size * BLOCKS, LANES)]
    gather x8 -> x0, local copies, waits for them, and re-layouts: 49.9 us -> none  [the longest x4 27.1 us: schur_terms(): picked = whole[:, cam_id]]
    all_gather x2 -> x0, blocking collectives: 48.5 us -> none  [on_device(): whole = lax.all_gather(masked, 'cam', axis=1, tiled=True)]
    ppermute x0 -> x3, starting transfers between devices: none -> 18.1 us  [on_device(): lax.ppermute(bundle, 'cam', [(i, (i - d) % owners) for i in range(owners)])]
    pallas_call x0 -> x9, Pallas kernels: none -> 14.6 us  [call(): pl.pallas_call(kernel, out_shape=shapes[0] if single else shapes, in_spec...]
  transfers between devices with their start and end apart: 2 -> 3, of which waited for: 2 -> 1; matrix products, arithmetic and copies ran while one was open for 0% -> 1% of each run, Pallas kernels for 0% -> 1%
where the time goes in v1:
time: 138 us
  blocking collectives  99.4 us (72%)
  starting transfers between devices  18.1 us (13%)
  Pallas kernels  14.6 us (11%)
  local copies, waits for them, and re-layouts  4.53 us (3%)
    all_to_all x6, blocking collectives, swap(): return lax.all_to_all(value, axis, 0, 0).reshape(size * BLOCKS, LANES)  99.4 us
    ppermute x3, starting transfers between devices, on_device(): lax.ppermute(bundle, 'cam', [(i, (i - d) % owners) for i in range(owners)])  18.1 us
    pallas_call x9, Pallas kernels, call(): pl.pallas_call(kernel, out_shape=shapes[0] if single else shapes, in_spec...  14.6 us
    unnamed x19, local copies, waits for them, and re-layouts  4.53 us
  transfers between devices with their start and end apart: 3, of which 1 were waited for; matrix products, arithmetic and copies ran while one was open for 1% of the time, Pallas kernels for 1%

profile of v1, /device:TPU:1, one launch (start us, length us, event | category | flops | bytes accessed | tf_op | source)
XLA Modules:
  0.0 137.5 jit_solution(15133141174446813398)
XLA Ops:
  0.7 0.1 pad_add_fusion.position
  0.7 0.6 copy-done.5
  1.3 0.8 copy-done.1
  2.1 0.8 copy-done.2
  2.8 0.8 copy-done.3
  3.6 0.6 prepare.1
  4.2 15.1 %collective-permute-start.2 = (f32[108,128]{1,0:T(8,128)S(1)}, f32[108,128]{1,0:T(8,128)S(1)}, u32[]{:S(2)}, u32[]{:S(2)}) collective-permute-start(f32[108,128]{1,0:T(8,128)S(1)} %get-tuple-element.8.own), channel_id=1, source_target_pairs={{0,8},{1,9},{2,10},{3,11},{4,12},{5,13},{6,14},{7,15},{8,0},{9,1},... | collective-permute-start | bytes 165896 | tf_op jit(solution)/shard_map/ppermute | solution.py:359
  19.3 3.0 %collective-permute-start.1 = (f32[108,128]{1,0:T(8,128)S(1)}, f32[108,128]{1,0:T(8,128)S(1)}, u32[]{:S(2)}, u32[]{:S(2)}) collective-permute-start(f32[108,128]{1,0:T(8,128)S(1)} %get-tuple-element.8.own), channel_id=1, source_target_pairs={{0,1},{1,2},{2,3},{3,4},{4,5},{5,6},{6,7},{7,8},{8,9},{9,10},{10,1... | collective-permute-start | bytes 165896 | tf_op jit(solution)/shard_map/ppermute | solution.py:359
  22.2 1.0 copy.18
  23.2 0.2 copy.17
  23.4 0.5 copy-done
  23.9 1.8 %invert.1 = (f32[8,4096]{1,0:T(8,128)S(1)}, s32[1,4096]{1,0:T(1,128)S(1)}) custom-call(s32[2]{0:T(128)S(1)} %pad_add_fusion.position, f32[6,4096]{1,0:T(8,128)S(1)} %bitcast.25, s32[1,4096]{1,0:T(1,128)S(1)} %copy-done, f32[3,1024]{1,0:T(4,128)S(1)} %bitcast.41, s32[1,4096]{1,0:T(1,128)S(1)} %copy-done.4), custom_call_target="tpu_custom_call" | custom-call | tf_op jit(solution)/shard_map/invert/pallas_call | solution.py:321
  25.8 0.1 collective-permute-done.after
  25.8 5.1 %apply_first.1 = (f32[256,128]{1,0:T(8,128)S(1)}, f32[432,128]{1,0:T(8,128)S(1)}) custom-call(f32[108,128]{1,0:T(8,128)S(1)} %get-tuple-element.8.own, f32[108,128]{1,0:T(8,128)S(1)} %collective-permute-done.after, f32[108,128]{1,0:T(8,128)S(1)} %collective-permute-done.1.before, f32[108,128]{1,0:T(8,128)S(1)} %collective-permute-done.2.across, ...), custom_call_target="tpu_custom_call" | custom-call | tf_op jit(solution)/shard_map/apply_first/pallas_call | solution.py:321
  30.9 24.6 %all_to_all.30 = f32[64,4,128]{2,1,0:T(4,128)S(1)} all-to-all(f32[64,4,128]{2,1,0:T(4,128)S(1)} %bitcast.40), channel_id=1, replica_groups=mesh['pts'=64,'cam'=16] {'pts'}, dimensions={0} | all-to-all | bytes 262144 | tf_op jit(solution)/shard_map/all_to_all | solution.py:334
  55.6 15.6 %all_to_all.31 = f32[16,4,128]{2,1,0:T(4,128)S(1)} all-to-all(f32[16,4,128]{2,1,0:T(4,128)S(1)} %bitcast.37), channel_id=1, replica_groups=mesh['pts'=64,'cam'=16] {'cam'}, dimensions={0} | all-to-all | bytes 65536 | tf_op jit(solution)/shard_map/all_to_all | solution.py:334
  71.2 0.6 combine.2
  71.8 15.3 %all_to_all.32 = f32[64,4,128]{2,1,0:T(4,128)S(1)} all-to-all(f32[64,4,128]{2,1,0:T(4,128)S(1)} %bitcast.33), channel_id=1, replica_groups=mesh['pts'=64,'cam'=16] {'pts'}, dimensions={0} | all-to-all | bytes 262144 | tf_op jit(solution)/shard_map/all_to_all | solution.py:334
  87.1 5.2 %apply_second.1 = f32[256,128]{1,0:T(8,128)S(1)} custom-call(f32[256,128]{1,0:T(8,128)S(1)} %bitcast.28, f32[432,128]{1,0:T(8,128)S(1)} %get-tuple-element.12.state, f32[18,4096]{1,0:T(8,128)S(1)} %bitcast.24, f32[6,4096]{1,0:T(8,128)S(1)} %bitcast.27, s32[1,4096]{1,0:T(1,128)S(1)} %get-tuple-element.9.camera, s32[1,4096]{1,0:T(1,128)S(1)} %copy-done, ...), custom_call_target="tpu_custom_call" | custom-call | tf_op jit(solution)/shard_map/apply_second/pallas_call | solution.py:321
  92.3 15.7 %all_to_all.33 = f32[64,4,128]{2,1,0:T(4,128)S(1)} all-to-all(f32[64,4,128]{2,1,0:T(4,128)S(1)} %bitcast.30), channel_id=1, replica_groups=mesh['pts'=64,'cam'=16] {'pts'}, dimensions={0} | all-to-all | bytes 262144 | tf_op jit(solution)/shard_map/all_to_all | solution.py:334
  108.0 12.9 %all_to_all.34 = f32[16,4,128]{2,1,0:T(4,128)S(1)} all-to-all(f32[16,4,128]{2,1,0:T(4,128)S(1)} %bitcast.39), channel_id=1, replica_groups=mesh['pts'=64,'cam'=16] {'cam'}, dimensions={0} | all-to-all | bytes 65536 | tf_op jit(solution)/shard_map/all_to_all | solution.py:334
  120.9 0.6 combine.3
  121.5 15.3 %all_to_all.35 = f32[64,4,128]{2,1,0:T(4,128)S(1)} all-to-all(f32[64,4,128]{2,1,0:T(4,128)S(1)} %bitcast.31), channel_id=1, replica_groups=mesh['pts'=64,'cam'=16] {'pts'}, dimensions={0} | all-to-all | bytes 262144 | tf_op jit(solution)/shard_map/all_to_all | solution.py:334
  136.8 0.7 finish.1
  (17 shorter events, 0.1 us)
Async XLA Ops:
  0.6 21.6 %copy-start.7 = (f32[1,3,1024]{2,0,1:T(1,128)S(1)}, f32[1,3,1024]{2,0,1:T(1,128)}, u32[]{:S(2)}) copy-start(f32[1,3,1024]{2,0,1:T(1,128)} %param.16) | copy-start | bytes 36868
  0.6 0.7 copy-start.5
  1.3 0.8 copy-start.1
  2.1 0.8 copy-start.2
  2.8 0.8 copy-start.3
  3.6 19.6 %copy-start.6 = (f32[1,18,4096]{2,0,1:T(1,128)S(1)}, f32[1,18,4096]{2,0,1:T(1,128)}, u32[]{:S(2)}) copy-start(f32[1,18,4096]{2,0,1:T(1,128)} %param.12) | copy-start | bytes 884740
  4.2 21.6 %collective-permute-start.2 = (f32[108,128]{1,0:T(8,128)S(1)}, f32[108,128]{1,0:T(8,128)S(1)}, u32[]{:S(2)}, u32[]{:S(2)}) collective-permute-start(f32[108,128]{1,0:T(8,128)S(1)} %get-tuple-element.8.own), channel_id=1, source_target_pairs={{0,8},{1,9},{2,10},{3,11},{4,12},{5,13},{6,14},{7,15},{8,0},{9,1},... | collective-permute-start | bytes 165896 | tf_op jit(solution)/shard_map/ppermute | solution.py:359
  19.3 6.5 %collective-permute-start.1 = (f32[108,128]{1,0:T(8,128)S(1)}, f32[108,128]{1,0:T(8,128)S(1)}, u32[]{:S(2)}, u32[]{:S(2)}) collective-permute-start(f32[108,128]{1,0:T(8,128)S(1)} %get-tuple-element.8.own), channel_id=1, source_target_pairs={{0,1},{1,2},{2,3},{3,4},{4,5},{5,6},{6,7},{7,8},{8,9},{9,10},{10,1... | collective-permute-start | bytes 165896 | tf_op jit(solution)/shard_map/ppermute | solution.py:359
  22.2 3.6 %collective-permute-start = (f32[108,128]{1,0:T(8,128)S(1)}, f32[108,128]{1,0:T(8,128)S(1)}, u32[]{:S(2)}, u32[]{:S(2)}) collective-permute-start(f32[108,128]{1,0:T(8,128)S(1)} %get-tuple-element.8.own), channel_id=1, source_target_pairs={{0,15},{1,0},{2,1},{3,2},{4,3},{5,4},{6,5},{7,6},{8,7},{9,8},{10,9... | collective-permute-start | bytes 165896 | tf_op jit(solution)/shard_map/ppermute | solution.py:359
  23.2 0.7 copy-start
  23.2 0.7 copy-start.4

commit v2 on v1

v2 whole, which is shorter than its diff:
```python
import functools

import jax
import jax.numpy as jnp
from jax import lax
from jax.experimental import pallas as pl
from jax.experimental.pallas import tpu as pltpu
from jax.sharding import PartitionSpec as P

LANES = 128
BLOCKS = 4
STEPS = (1, 2, 4, 8)
CHUNK = 512
F32, BF16 = jnp.float32, jnp.bfloat16
VMEM = pl.BlockSpec(memory_space=pltpu.VMEM)
SMEM = pl.BlockSpec(memory_space=pltpu.SMEM)
HBM = pl.BlockSpec(memory_space=pltpu.HBM)
PARAMS = pltpu.CompilerParams(vmem_limit_bytes=40 * 1024 * 1024)


def one_hot(row, count):
    ids = lax.broadcasted_iota(jnp.int32, (count, row.shape[1]), 0)
    return jnp.where(ids == row, 1.0, 0.0)


def short_one_hot(row, count):
    ids = lax.broadcasted_iota(jnp.int16, (count, row.shape[1]), 0)
    return jnp.where(ids == row.astype(jnp.int16), BF16(1), BF16(0))


def neighbour_masks(point):
    count = point.shape[1]
    before = [jnp.where(pltpu.roll(point, s, 1) == point, 1.0, 0.0) for s in STEPS]
    after = [pltpu.roll(mask, count - s, 1) for mask, s in zip(before, STEPS)]
    return jnp.concatenate(before + after, axis=0)


def point_totals(value, masks):
    count = value.shape[1]
    before = value
    after = value
    for i, step in enumerate(STEPS):
        j = len(STEPS) + i
        before = before + masks[i : i + 1] * pltpu.roll(before, step, 1)
        after = after + masks[j : j + 1] * pltpu.roll(after, count - step, 1)
    return before + (after - value)


def setup_kernel(width, owners, position, jac_pt, point_ref, damping, camera_ref,
                 inverse, masks, lane, slot):
    camera = camera_ref[...]
    shift = lax.rem(lax.div(camera, width) - position[0] + owners, owners)
    block = jnp.where(shift == 1, 1, jnp.where(shift == owners - 1, 2, 3))
    block = jnp.where(shift == 0, 0, block)
    inner = lax.rem(camera, width)
    tile = lax.div(inner, LANES)
    lane[...] = lax.div(tile, 2) * LANES + lax.rem(inner, LANES)
    slot[...] = lax.rem(tile, 2) * BLOCKS + block

    point = point_ref[...]
    count = point.shape[1]
    tiles = damping.shape[1] // LANES
    masks[...] = neighbour_masks(point)
    rows = [jac_pt[r : r + 1, :] for r in range(6)]
    pairs = [(0, 0), (0, 1), (0, 2), (1, 1), (1, 2), (2, 2)]
    prods = [rows[a] * rows[b] + rows[3 + a] * rows[3 + b] for a, b in pairs]
    prods = jnp.concatenate(prods + [jnp.zeros((2, count), F32)], axis=0)
    summed = point_totals(prods, masks[...])

    hot = one_hot(lax.rem(point, LANES), LANES).astype(BF16)
    tile_mask = one_hot(lax.div(point, LANES), tiles)
    table = jnp.concatenate(
        [damping[k : k + 1, t * LANES : (t + 1) * LANES] for k in range(3) for t in range(tiles)],
        axis=0,
    )
    high = table.astype(BF16)
    rest = table - high.astype(F32)
    mid = rest.astype(BF16)
    low = (rest - mid.astype(F32)).astype(BF16)
    picked = sum(
        jnp.dot(part, hot, preferred_element_type=F32) for part in (high, mid, low)
    )
    damp = [
        jnp.sum(picked[k * tiles : (k + 1) * tiles] * tile_mask, axis=0, keepdims=True)
        for k in range(3)
    ]
    xx = summed[0:1] + damp[0]
    xy = summed[1:2]
    xz = summed[2:3]
    yy = summed[3:4] + damp[1]
    yz = summed[4:5]
    zz = summed[5:6] + damp[2]
    cof_xx = yy * zz - yz * yz
    cof_xy = xz * yz - xy * zz
    cof_xz = xy * yz - xz * yy
    cof_yy = xx * zz - xz * xz
    cof_yz = xy * xz - xx * yz
    cof_zz = xx * yy - xy * xy
    det = xx * cof_xx + xy * cof_xy + xz * cof_xz
    inverse[0:1] = cof_xx / det
    inverse[1:2] = cof_xy / det
    inverse[2:3] = cof_xz / det
    inverse[3:4] = cof_yy / det
    inverse[4:5] = cof_yz / det
    inverse[5:6] = cof_zz / det
    inverse[6:8] = jnp.zeros((2, count), F32)


def lane_sums(value):
    return jnp.sum(value, axis=0, keepdims=True)


def schur(vector, send, jac_cam, jac_pt, lane, slot, masks, inverse, hot, error):
    count = lane.shape[1]
    params = jac_cam.shape[0] // 2
    slots = 2 * BLOCKS
    half = hot.shape[0] // LANES
    rows = params * slots
    table = vector.reshape(params, half, slots, LANES)
    table = jnp.concatenate([table[:, h].reshape(rows, LANES) for h in range(half)], axis=1)
    high = table.astype(BF16)
    low = (table - high.astype(F32)).astype(BF16)
    table = jnp.concatenate([high, low], axis=0)

    def predict(i, _):
        span = pl.ds(pl.multiple_of(i * CHUNK, CHUNK), CHUNK)
        spot = short_one_hot(lane[:, span], half * LANES)
        hot[:, span] = spot
        got = jnp.dot(table, spot, preferred_element_type=F32)
        got = got[:rows] + got[rows:]
        mask = one_hot(slot[:, span], slots)
        for r in range(2):
            total = jnp.zeros((slots, CHUNK), F32)
            for a in range(params):
                jac = jac_cam[r * params + a : r * params + a + 1, span]
                total = total + jac * got[a * slots : (a + 1) * slots]
            error[r : r + 1, span] = lane_sums(total * mask)
        return 0

    lax.fori_loop(0, count // CHUNK, predict, 0, unroll=count // CHUNK)

    e0, e1 = error[0:1, :], error[1:2, :]
    jp = [jac_pt[r : r + 1, :] for r in range(6)]
    pulled = [jp[k] * e0 + jp[3 + k] * e1 for k in range(3)]
    pulled = jnp.concatenate(pulled + [jnp.zeros((5, count), F32)], axis=0)
    sums = point_totals(pulled, masks[...])
    y0, y1, y2 = sums[0:1], sums[1:2], sums[2:3]
    inv = [inverse[r : r + 1, :] for r in range(6)]
    z = (
        inv[0] * y0 + inv[1] * y1 + inv[2] * y2,
        inv[1] * y0 + inv[3] * y1 + inv[4] * y2,
        inv[2] * y0 + inv[4] * y1 + inv[5] * y2,
    )
    left0 = e0 - (jp[0] * z[0] + jp[1] * z[1] + jp[2] * z[2])
    left1 = e1 - (jp[3] * z[0] + jp[4] * z[1] + jp[5] * z[2])
    energy = e0 * left0 + e1 * left1
    error[0:1, :] = left0
    error[1:2, :] = left1

    def push(i, total):
        span = pl.ds(pl.multiple_of(i * CHUNK, CHUNK), CHUNK)
        mask = one_hot(slot[:, span], slots)
        first, second = error[0:1, span], error[1:2, span]
        highs, lows = [], []
        for a in range(params):
            value = jac_cam[a : a + 1, span] * first
            value = value + jac_cam[params + a : params + a + 1, span] * second
            near = value.astype(BF16).astype(F32)
            highs.append(near * mask)
            lows.append((value - near) * mask)
        both = jnp.concatenate(highs + lows, axis=0).astype(BF16)
        return total + lax.dot_general(
            both, hot[:, span], (((1,), (1,)), ((), ())), preferred_element_type=F32
        )

    total = jnp.zeros((2 * rows, half * LANES), F32)
    total = lax.fori_loop(0, count // CHUNK, push, total, unroll=count // CHUNK)
    total = total[:rows] + total[rows:]
    for a in range(params):
        for h in range(half):
            start = (a * half + h) * slots
            send[start : start + slots, :] = total[
                a * slots : (a + 1) * slots, h * LANES : (h + 1) * LANES
            ]
    return sum(energy[:, t * LANES : (t + 1) * LANES] for t in range(count // LANES))


RIGHT, DAMPING, WEIGHTS, PULL, UNWEIGH = range(5)


def own_part(own, which):
    per = own.shape[0] // 5
    return own[which * per : (which + 1) * per, :]


def prepare_kernel(position, anchors, right_side, camera_damping, preconditioner, start,
                   own, right, damping, precond, sems):
    params, width = right.shape
    tiles = width // LANES
    pairs = ((right_side, right), (camera_damping, damping), (preconditioner, precond))
    copies = [
        pltpu.make_async_copy(source, target, sems.at[i])
        for i, (source, target) in enumerate(pairs)
    ]
    for copy in copies:
        copy.start()
    ids = position[0] * width + lax.broadcasted_iota(jnp.int32, (1, width), 1)
    keep = jnp.ones((1, width), F32)
    for index in range(anchors.shape[0]):
        keep = jnp.where(ids == anchors[index], 0.0, keep)
    for copy in copies:
        copy.wait()
    weights = precond[...] * keep
    vector = weights * right[...]
    parts = [right[...], damping[...], weights, weights * damping[...] * vector]
    parts.append(keep / precond[...])
    for t in range(tiles):
        lanes = slice(t * LANES, (t + 1) * LANES)
        start[pl.ds(t, params, stride=tiles), :] = vector[:, lanes]
        for which, value in enumerate(parts):
            place = pl.ds(which * params * tiles + t, params, stride=tiles)
            own[place, :] = value[:, lanes]


def send_scalars(send, data_rows, rows):
    rest = send.shape[0] - data_rows
    send[data_rows:, :] = jnp.zeros((rest, LANES), F32)
    for index, row in enumerate(rows):
        at = data_rows + index * BLOCKS
        send[at : at + 1, :] = row


def scalar(ref, row):
    return jnp.sum(ref[row : row + 1, :], axis=1, keepdims=True)


def first_kernel(share, mine, after, before, across, own, jac_cam, jac_pt, lane, slot,
                 masks, inverse, send, start, hot, error):
    per = mine.shape[0]
    for block, part in enumerate((mine, after, before, across)):
        start[pl.ds(block, per, stride=BLOCKS), :] = part[...]
    energy = schur(start[...], send, jac_cam, jac_pt, lane, slot, masks, inverse, hot, error)
    vector = mine[...]
    energy = energy + share * lane_sums(own_part(own, DAMPING) * vector * vector)
    gamma = share * lane_sums(own_part(own, RIGHT) * vector)
    send_scalars(send, start.shape[0], (energy, gamma))


def second_kernel(share, received, start, own, jac_cam, jac_pt, lane, slot, masks, inverse,
                  send, step, hot, error):
    data_rows = start.shape[0]
    per = data_rows // BLOCKS
    alpha = scalar(received, data_rows + BLOCKS) / scalar(received, data_rows)
    step[...] = start[...] - alpha * received[0:data_rows, :]
    energy = schur(step[...], send, jac_cam, jac_pt, lane, slot, masks, inverse, hot, error)
    vector = step[pl.ds(0, per, stride=BLOCKS), :]
    change = received[pl.ds(0, per, stride=BLOCKS), :]
    residual = own_part(own, UNWEIGH) * vector
    energy = energy + share * lane_sums(own_part(own, DAMPING) * vector * vector)
    fresh = share * lane_sums(residual * vector)
    cross = share * lane_sums(residual * change)
    send_scalars(send, data_rows, (energy, fresh, cross))


def last_kernel(first, second, start, step, own, solution, residual):
    params, width = solution.shape
    tiles = width // LANES
    per = params * tiles
    data_rows = per * BLOCKS
    curve, gamma = scalar(first, data_rows), scalar(first, data_rows + BLOCKS)
    energy, fresh, cross = (scalar(second, per + i) for i in range(3))
    alpha = gamma / curve
    beta = fresh / gamma
    alpha_next = fresh / (energy + 2.0 * beta * cross + beta * beta * curve)
    for t in range(tiles):
        spread = pl.ds(t * BLOCKS, params, stride=tiles * BLOCKS)
        begin, vector, change = start[spread, :], step[spread, :], first[spread, :]
        terms = second[pl.ds(t, params, stride=tiles), :]
        damping, unweigh = (
            own[pl.ds(which * per + t, params, stride=tiles), :] for which in (DAMPING, UNWEIGH)
        )
        direction = vector + beta * begin
        image = jnp.where(unweigh > 0.0, damping * vector + terms, 0.0)
        image = image + beta * (unweigh * change)
        lanes = slice(t * LANES, (t + 1) * LANES)
        solution[:, lanes] = alpha * begin + alpha_next * direction
        residual[:, lanes] = unweigh * vector - alpha_next * image


def chunk_sum(received):
    total = received[0:8, :]
    for at in range(8, received.shape[0], 8):
        total = total + received[at : at + 8, :]
    return total[0:BLOCKS] + total[BLOCKS:]


def spread_kernel(position, received, own, send):
    total = chunk_sum(received)
    per = own.shape[0] // 5
    rows = [own[pl.ds(which * per + position[2], 1), :] for which in (WEIGHTS, PULL)]
    total = jnp.concatenate([total, *rows, jnp.zeros((2, LANES), F32)], axis=0)
    for at in range(0, send.shape[0], 8):
        send[at : at + 8, :] = total


def combine_kernel(position, received, send):
    owners = received.shape[0] // 8
    me = position[0]

    def row(owner, at):
        spot = lax.rem(owner + 2 * owners, owners) * 8 + at
        return received[pl.ds(spot, 1), :]

    def block_change(owner):
        terms = (row(owner, 0) + row(owner - 1, 1)) + (
            row(owner + 1, 2) + row(owner + owners // 2, 3)
        )
        return row(owner, BLOCKS + 1) + row(owner, BLOCKS) * terms

    joined = [block_change(me + shift) for shift in (0, 1, -1, owners // 2)]
    joined = jnp.concatenate(joined, axis=0)
    total = received[0:8, :]
    for owner in range(1, owners):
        total = total + received[owner * 8 : (owner + 1) * 8, :]
    joined = jnp.where(position[1] == 1, total[0:BLOCKS], joined)
    joined = jnp.concatenate([joined, joined], axis=0)
    for at in range(0, send.shape[0], 8):
        send[at : at + 8, :] = joined


def spread_own_kernel(position, received, send):
    total = chunk_sum(received)
    owners = send.shape[0]
    scalars = jnp.broadcast_to(total[0:1], send.shape)
    send[...] = jnp.where(position[1] == 1, scalars, 0.0)

    @pl.when(position[1] == 0)
    def _():
        for block, shift in enumerate((0, 1, -1, owners // 2)):
            spot = lax.rem(position[0] + shift + owners, owners)
            send[pl.ds(spot, 1), :] = total[block : block + 1]


def combine_own_kernel(received, send):
    total = received[0:8, :]
    for at in range(8, received.shape[0], 8):
        total = total + received[at : at + 8, :]
    send[...] = jnp.broadcast_to(lane_sums(total), send.shape)


def call(kernel, outs, specs, *args, scratch=(), name=None):
    shapes = [jax.ShapeDtypeStruct(shape, dtype) for shape, dtype in outs]
    single = len(shapes) == 1
    return pl.pallas_call(
        kernel,
        out_shape=shapes[0] if single else shapes,
        in_specs=specs,
        out_specs=VMEM if single else [VMEM] * len(shapes),
        scratch_shapes=list(scratch),
        compiler_params=PARAMS,
        name=name,
    )(*args)


def swap(value, axis, size):
    rows = value.shape[0] // size
    value = value.reshape(size, rows, LANES)
    return lax.all_to_all(value, axis, 0, 0).reshape(size * rows, LANES)


def on_device(right_side, camera_damping, preconditioner, jac_cam, jac_pt, camera_index,
              point_index, point_damping, anchors):
    params, width = right_side.shape
    owners, rows = lax.axis_size("cam"), lax.axis_size("pts")
    per = params * width // LANES
    count = camera_index.shape[1]
    me = lax.axis_index("cam").astype(jnp.int32)
    spot = lax.axis_index("pts").astype(jnp.int32)
    position = jnp.stack([me, (spot >= per).astype(jnp.int32), jnp.minimum(spot, per - 1)])
    jac_cam, jac_pt = jac_cam[0], jac_pt[0]
    share = 1.0 / rows

    mine, own = call(
        prepare_kernel, [((per, LANES), F32), ((5 * per, LANES), F32)],
        [SMEM, SMEM] + [HBM] * 3, position, anchors, right_side, camera_damping, preconditioner,
        scratch=[pltpu.VMEM((params, width), F32)] * 3 + [pltpu.SemaphoreType.DMA((3,))],
        name="prepare",
    )
    after, before, across = (
        lax.ppermute(mine, "cam", [(i, (i - d) % owners) for i in range(owners)])
        for d in (1, -1, owners // 2)
    )
    inverse, masks, lane, slot = call(
        functools.partial(setup_kernel, width, owners),
        [((8, count), F32), ((8, count), F32), ((1, count), jnp.int32), ((1, count), jnp.int32)],
        [SMEM] + [VMEM] * 4, position, jac_pt, point_index, point_damping[0], camera_index,
        name="invert",
    )
    fixed = (jac_cam, jac_pt, lane, slot, masks, inverse)
    half = width // (2 * LANES)
    scratch = (pltpu.VMEM((half * LANES, count), BF16), pltpu.VMEM((8, count), F32))
    sums = ((rows * BLOCKS, LANES), F32)
    vector = ((per * BLOCKS, LANES), F32)

    send, start = call(
        functools.partial(first_kernel, share), [sums, vector], [VMEM] * 11,
        mine, after, before, across, own, *fixed, scratch=scratch, name="apply_first",
    )
    chunks = swap(send, "pts", rows)
    chunks = call(
        spread_kernel, [((owners * 8, LANES), F32)], [SMEM, VMEM, VMEM], position, chunks, own,
        name="spread",
    )
    chunks = swap(chunks, "cam", owners)
    chunks = call(combine_kernel, [sums], [SMEM, VMEM], position, chunks, name="combine")
    first = swap(chunks, "pts", rows)

    send, step = call(
        functools.partial(second_kernel, share), [sums, vector], [VMEM] * 9,
        first, start, own, *fixed, scratch=scratch, name="apply_second",
    )
    chunks = swap(send, "pts", rows)
    chunks = call(
        spread_own_kernel, [((owners, LANES), F32)], [SMEM, VMEM], position, chunks,
        name="spread_own",
    )
    chunks = swap(chunks, "cam", owners)
    chunks = call(
        combine_own_kernel, [((rows, LANES), F32)], [VMEM], chunks, name="combine_own"
    )
    second = swap(chunks, "pts", rows)
    return tuple(
        call(
            last_kernel, [((params, width), F32)] * 2, [VMEM] * 5, first, second, start, step,
            own, name="finish",
        )
    )


def solution(mesh):
    return jax.shard_map(
        on_device,
        mesh=mesh,
        in_specs=(
            P(None, "cam"),
            P(None, "cam"),
            P(None, "cam"),
            P(("pts", "cam"), None, None),
            P(("pts", "cam"), None, None),
            P(("pts", "cam"), None),
            P(("pts", "cam"), None),
            P(("pts", "cam"), None, None),
            P(),
        ),
        out_specs=(P(None, "cam"), P(None, "cam")),
        check_vma=False,
    )
```

time: 138 us -> 132 us (0.957)
  Pallas kernels: 14.6 us -> 8.85 us
    pallas_call x9, Pallas kernels: 14.6 us -> 8.85 us  [call(): pl.pallas_call(kernel, out_shape=shapes[0] if single else shapes, in_spec...]
  transfers between devices with their start and end apart: 3 -> 3, of which waited for: 1 -> 0; matrix products, arithmetic and copies ran while one was open for 1% -> 1% of each run, Pallas kernels for 1% -> 2%
where the time goes in v2:
time: 132 us; the launch traced here: 131 us
  blocking collectives  98.8 us (75%)
  starting transfers between devices  18.1 us (14%)
  Pallas kernels  8.85 us (7%)
  local copies, waits for them, and re-layouts  4.53 us (3%)
    all_to_all x6, blocking collectives, swap(): return lax.all_to_all(value, axis, 0, 0).reshape(size * rows, LANES)  98.8 us
    ppermute x3, starting transfers between devices, on_device(): lax.ppermute(mine, 'cam', [(i, (i - d) % owners) for i in range(owners)])  18.1 us
    pallas_call x9, Pallas kernels, call(): pl.pallas_call(kernel, out_shape=shapes[0] if single else shapes, in_spec...  8.85 us
    unnamed x19, local copies, waits for them, and re-layouts  4.53 us
  transfers between devices with their start and end apart: 3, of which 0 were waited for; matrix products, arithmetic and copies ran while one was open for 1% of the time, Pallas kernels for 2%

profile of v2, /device:TPU:1, one launch (start us, length us, event | category | flops | bytes accessed | tf_op | source)
XLA Modules:
  0.0 131.1 jit_solution(17547998397974990179)
XLA Ops:
  0.7 0.1 pad_add_fusion.position
  0.7 0.6 copy-done.5
  1.3 0.8 copy-done
  2.1 0.8 copy-done.1
  2.8 0.8 copy-done.2
  3.6 0.7 prepare.1
  4.3 15.1 %collective-permute-start.2 = (f32[36,128]{1,0:T(8,128)S(1)}, f32[36,128]{1,0:T(8,128)S(1)}, u32[]{:S(2)}, u32[]{:S(2)}) collective-permute-start(f32[36,128]{1,0:T(8,128)S(1)} %get-tuple-element.12.mine), channel_id=1, source_target_pairs={{0,8},{1,9},{2,10},{3,11},{4,12},{5,13},{6,14},{7,15},{8,0},{9,1},... | collective-permute-start | bytes 55304 | tf_op jit(solution)/shard_map/ppermute | solution.py:390
  19.4 3.0 %collective-permute-start.1 = (f32[36,128]{1,0:T(8,128)S(1)}, f32[36,128]{1,0:T(8,128)S(1)}, u32[]{:S(2)}, u32[]{:S(2)}) collective-permute-start(f32[36,128]{1,0:T(8,128)S(1)} %get-tuple-element.12.mine), channel_id=1, source_target_pairs={{0,1},{1,2},{2,3},{3,4},{4,5},{5,6},{6,7},{7,8},{8,9},{9,10},{10,1... | collective-permute-start | bytes 55304 | tf_op jit(solution)/shard_map/ppermute | solution.py:390
  22.4 1.0 copy.20
  23.4 0.2 copy.19
  23.6 0.5 copy-done.3
  24.1 2.0 %invert.1 = (f32[8,4096]{1,0:T(8,128)S(1)}, f32[8,4096]{1,0:T(8,128)S(1)}, s32[1,4096]{1,0:T(1,128)S(1)}, s32[1,4096]{1,0:T(1,128)S(1)}) custom-call(s32[3]{0:T(128)S(1)} %pad_add_fusion.position, f32[6,4096]{1,0:T(8,128)S(1)} %bitcast.30, s32[1,4096]{1,0:T(1,128)S(1)} %copy-done.3, f32[3,1024]{1,0:T(4,128)S(1)} %bitcast.44, s32[1,4096]{1,0:T(1,128)S(1)} %copy-done.4), custom_call_target="tpu_custom_call" | custom-call | tf_op jit(solution)/shard_map/invert/pallas_call | solution.py:354
  26.2 1.8 %apply_first.1 = (f32[256,128]{1,0:T(8,128)S(1)}, f32[144,128]{1,0:T(8,128)S(1)}) custom-call(f32[36,128]{1,0:T(8,128)S(1)} %get-tuple-element.12.mine, f32[36,128]{1,0:T(8,128)S(1)} %collective-permute-done.after, f32[36,128]{1,0:T(8,128)S(1)} %collective-permute-done.1.before, f32[36,128]{1,0:T(8,128)S(1)} %collective-permute-done.2.across, ...), custom_call_target="tpu_custom_call" | custom-call | tf_op jit(solution)/shard_map/apply_first/pallas_call | solution.py:354
  27.9 24.5 %all_to_all.30 = f32[64,4,128]{2,1,0:T(4,128)S(1)} all-to-all(f32[64,4,128]{2,1,0:T(4,128)S(1)} %bitcast.43), channel_id=1, replica_groups=mesh['pts'=64,'cam'=16] {'pts'}, dimensions={0} | all-to-all | bytes 262144 | tf_op jit(solution)/shard_map/all_to_all | solution.py:368
  52.5 0.6 spread.1
  53.0 16.2 %all_to_all.31 = f32[16,8,128]{2,1,0:T(8,128)S(1)} all-to-all(f32[16,8,128]{2,1,0:T(8,128)S(1)} %bitcast.39), channel_id=1, replica_groups=mesh['pts'=64,'cam'=16] {'cam'}, dimensions={0} | all-to-all | bytes 131072 | tf_op jit(solution)/shard_map/all_to_all | solution.py:368
  69.2 0.6 combine.1
  69.8 15.6 %all_to_all.32 = f32[64,4,128]{2,1,0:T(4,128)S(1)} all-to-all(f32[64,4,128]{2,1,0:T(4,128)S(1)} %bitcast.37), channel_id=1, replica_groups=mesh['pts'=64,'cam'=16] {'pts'}, dimensions={0} | all-to-all | bytes 262144 | tf_op jit(solution)/shard_map/all_to_all | solution.py:368
  85.4 1.9 %apply_second.1 = (f32[256,128]{1,0:T(8,128)S(1)}, f32[144,128]{1,0:T(8,128)S(1)}) custom-call(f32[256,128]{1,0:T(8,128)S(1)} %bitcast.33, f32[144,128]{1,0:T(8,128)S(1)} %get-tuple-element.19.start, f32[180,128]{1,0:T(8,128)S(1)} %get-tuple-element.13.own, f32[18,4096]{1,0:T(8,128)S(1)} %bitcast.29, f32[6,4096]{1,0:T(8,128)S(1)} %bitcast.32, ...), custom_call_target="tpu_custom_call" | custom-call | tf_op jit(solution)/shard_map/apply_second/pallas_call | solution.py:354
  87.3 15.4 %all_to_all.33 = f32[64,4,128]{2,1,0:T(4,128)S(1)} all-to-all(f32[64,4,128]{2,1,0:T(4,128)S(1)} %bitcast.42), channel_id=1, replica_groups=mesh['pts'=64,'cam'=16] {'pts'}, dimensions={0} | all-to-all | bytes 262144 | tf_op jit(solution)/shard_map/all_to_all | solution.py:368
  102.7 0.6 spread_own.1
  103.3 12.5 %all_to_all.34 = f32[16,1,128]{2,1,0:T(1,128)S(1)} all-to-all(f32[16,1,128]{2,1,0:T(1,128)S(1)} %bitcast.45), channel_id=1, replica_groups=mesh['pts'=64,'cam'=16] {'cam'}, dimensions={0} | all-to-all | bytes 16384 | tf_op jit(solution)/shard_map/all_to_all | solution.py:368
  115.7 14.6 %all_to_all.35 = f32[64,1,128]{2,1,0:T(1,128)S(1)} all-to-all(f32[64,1,128]{2,1,0:T(1,128)S(1)} %bitcast.41), channel_id=1, replica_groups=mesh['pts'=64,'cam'=16] {'pts'}, dimensions={0} | all-to-all | bytes 65536 | tf_op jit(solution)/shard_map/all_to_all | solution.py:368
  130.3 0.7 finish.1
  (17 shorter events, 0.1 us)
Async XLA Ops:
  0.6 21.8 %copy-start.7 = (f32[1,3,1024]{2,0,1:T(1,128)S(1)}, f32[1,3,1024]{2,0,1:T(1,128)}, u32[]{:S(2)}) copy-start(f32[1,3,1024]{2,0,1:T(1,128)} %param.16) | copy-start | bytes 36868
  0.6 0.7 copy-start.5
  1.3 0.8 copy-start
  2.1 0.8 copy-start.1
  2.8 0.8 copy-start.2
  3.6 19.8 %copy-start.6 = (f32[1,18,4096]{2,0,1:T(1,128)S(1)}, f32[1,18,4096]{2,0,1:T(1,128)}, u32[]{:S(2)}) copy-start(f32[1,18,4096]{2,0,1:T(1,128)} %param.12) | copy-start | bytes 884740
  4.3 21.8 %collective-permute-start.2 = (f32[36,128]{1,0:T(8,128)S(1)}, f32[36,128]{1,0:T(8,128)S(1)}, u32[]{:S(2)}, u32[]{:S(2)}) collective-permute-start(f32[36,128]{1,0:T(8,128)S(1)} %get-tuple-element.12.mine), channel_id=1, source_target_pairs={{0,8},{1,9},{2,10},{3,11},{4,12},{5,13},{6,14},{7,15},{8,0},{9,1},... | collective-permute-start | bytes 55304 | tf_op jit(solution)/shard_map/ppermute | solution.py:390
  19.4 6.7 %collective-permute-start.1 = (f32[36,128]{1,0:T(8,128)S(1)}, f32[36,128]{1,0:T(8,128)S(1)}, u32[]{:S(2)}, u32[]{:S(2)}) collective-permute-start(f32[36,128]{1,0:T(8,128)S(1)} %get-tuple-element.12.mine), channel_id=1, source_target_pairs={{0,1},{1,2},{2,3},{3,4},{4,5},{5,6},{6,7},{7,8},{8,9},{9,10},{10,1... | collective-permute-start | bytes 55304 | tf_op jit(solution)/shard_map/ppermute | solution.py:390
  22.4 3.7 %collective-permute-start = (f32[36,128]{1,0:T(8,128)S(1)}, f32[36,128]{1,0:T(8,128)S(1)}, u32[]{:S(2)}, u32[]{:S(2)}) collective-permute-start(f32[36,128]{1,0:T(8,128)S(1)} %get-tuple-element.12.mine), channel_id=1, source_target_pairs={{0,15},{1,0},{2,1},{3,2},{4,3},{5,4},{6,5},{7,6},{8,7},{9,8},{10,9... | collective-permute-start | bytes 55304 | tf_op jit(solution)/shard_map/ppermute | solution.py:390
  23.4 0.7 copy-start.3
  23.4 0.7 copy-start.4

commit v3 on v2

--- a/solution.py
+++ b/solution.py
@@ -13,8 +13,6 @@
 CHUNK = 512
 F32, BF16 = jnp.float32, jnp.bfloat16
 VMEM = pl.BlockSpec(memory_space=pltpu.VMEM)
-SMEM = pl.BlockSpec(memory_space=pltpu.SMEM)
-HBM = pl.BlockSpec(memory_space=pltpu.HBM)
 PARAMS = pltpu.CompilerParams(vmem_limit_bytes=40 * 1024 * 1024)
 
 
@@ -46,10 +44,12 @@
     return before + (after - value)
 
 
-def setup_kernel(width, owners, position, jac_pt, point_ref, damping, camera_ref,
-                 inverse, masks, lane, slot):
+def setup_kernel(owners, jac_pt, point_ref, damping, camera_ref, right_side, camera_damping,
+                 preconditioner, keep, inverse, masks, lane, slot, own):
+    width = right_side.shape[1]
+    own_arrays(right_side[...], camera_damping[...], preconditioner[...], keep[...], own)
     camera = camera_ref[...]
-    shift = lax.rem(lax.div(camera, width) - position[0] + owners, owners)
+    shift = lax.rem(lax.div(camera, width) - lax.axis_index("cam") + owners, owners)
     block = jnp.where(shift == 1, 1, jnp.where(shift == owners - 1, 2, 3))
     block = jnp.where(shift == 0, 0, block)
     inner = lax.rem(camera, width)
@@ -193,30 +193,13 @@
     return own[which * per : (which + 1) * per, :]
 
 
-def prepare_kernel(position, anchors, right_side, camera_damping, preconditioner, start,
-                   own, right, damping, precond, sems):
+def own_arrays(right, damping, precond, keep, own):
     params, width = right.shape
     tiles = width // LANES
-    pairs = ((right_side, right), (camera_damping, damping), (preconditioner, precond))
-    copies = [
-        pltpu.make_async_copy(source, target, sems.at[i])
-        for i, (source, target) in enumerate(pairs)
-    ]
-    for copy in copies:
-        copy.start()
-    ids = position[0] * width + lax.broadcasted_iota(jnp.int32, (1, width), 1)
-    keep = jnp.ones((1, width), F32)
-    for index in range(anchors.shape[0]):
-        keep = jnp.where(ids == anchors[index], 0.0, keep)
-    for copy in copies:
-        copy.wait()
-    weights = precond[...] * keep
-    vector = weights * right[...]
-    parts = [right[...], damping[...], weights, weights * damping[...] * vector]
-    parts.append(keep / precond[...])
+    weights = precond * keep
+    parts = (right, damping, weights, weights * damping * weights * right, keep / precond)
     for t in range(tiles):
         lanes = slice(t * LANES, (t + 1) * LANES)
-        start[pl.ds(t, params, stride=tiles), :] = vector[:, lanes]
         for which, value in enumerate(parts):
             place = pl.ds(which * params * tiles + t, params, stride=tiles)
             own[place, :] = value[:, lanes]
@@ -236,11 +219,14 @@
 
 def first_kernel(share, mine, after, before, across, own, jac_cam, jac_pt, lane, slot,
                  masks, inverse, send, start, hot, error):
-    per = mine.shape[0]
+    params, width = mine.shape
+    tiles = width // LANES
     for block, part in enumerate((mine, after, before, across)):
-        start[pl.ds(block, per, stride=BLOCKS), :] = part[...]
+        for t in range(tiles):
+            place = pl.ds(t * BLOCKS + block, params, stride=tiles * BLOCKS)
+            start[place, :] = part[:, t * LANES : (t + 1) * LANES]
     energy = schur(start[...], send, jac_cam, jac_pt, lane, slot, masks, inverse, hot, error)
-    vector = mine[...]
+    vector = start[pl.ds(0, params * tiles, stride=BLOCKS), :]
     energy = energy + share * lane_sums(own_part(own, DAMPING) * vector * vector)
     gamma = share * lane_sums(own_part(own, RIGHT) * vector)
     send_scalars(send, start.shape[0], (energy, gamma))
@@ -294,18 +280,19 @@
     return total[0:BLOCKS] + total[BLOCKS:]
 
 
-def spread_kernel(position, received, own, send):
+def spread_kernel(received, own, send):
     total = chunk_sum(received)
     per = own.shape[0] // 5
-    rows = [own[pl.ds(which * per + position[2], 1), :] for which in (WEIGHTS, PULL)]
+    at = jnp.minimum(lax.axis_index("pts"), per - 1)
+    rows = [own[pl.ds(which * per + at, 1), :] for which in (WEIGHTS, PULL)]
     total = jnp.concatenate([total, *rows, jnp.zeros((2, LANES), F32)], axis=0)
     for at in range(0, send.shape[0], 8):
         send[at : at + 8, :] = total
 
 
-def combine_kernel(position, received, send):
+def combine_kernel(per, received, send):
     owners = received.shape[0] // 8
-    me = position[0]
+    me = lax.axis_index("cam")
 
     def row(owner, at):
         spot = lax.rem(owner + 2 * owners, owners) * 8 + at
@@ -322,22 +309,23 @@
     total = received[0:8, :]
     for owner in range(1, owners):
         total = total + received[owner * 8 : (owner + 1) * 8, :]
-    joined = jnp.where(position[1] == 1, total[0:BLOCKS], joined)
+    joined = jnp.where(lax.axis_index("pts") >= per, total[0:BLOCKS], joined)
     joined = jnp.concatenate([joined, joined], axis=0)
     for at in range(0, send.shape[0], 8):
         send[at : at + 8, :] = joined
 
 
-def spread_own_kernel(position, received, send):
+def spread_own_kernel(per, received, send):
     total = chunk_sum(received)
     owners = send.shape[0]
     scalars = jnp.broadcast_to(total[0:1], send.shape)
-    send[...] = jnp.where(position[1] == 1, scalars, 0.0)
-
-    @pl.when(position[1] == 0)
+    chunk = lax.axis_index("pts")
+    send[...] = jnp.where(chunk >= per, scalars, 0.0)
+
+    @pl.when(chunk < per)
     def _():
         for block, shift in enumerate((0, 1, -1, owners // 2)):
-            spot = lax.rem(position[0] + shift + owners, owners)
+            spot = lax.rem(lax.axis_index("cam") + shift + owners, owners)
             send[pl.ds(spot, 1), :] = total[block : block + 1]
 
 
@@ -348,14 +336,13 @@
     send[...] = jnp.broadcast_to(lane_sums(total), send.shape)
 
 
-def call(kernel, outs, specs, *args, scratch=(), name=None):
-    shapes = [jax.ShapeDtypeStruct(shape, dtype) for shape, dtype in outs]
-    single = len(shapes) == 1
+def call(kernel, outs, *args, scratch=(), name=None):
+    single = not isinstance(outs, list)
     return pl.pallas_call(
         kernel,
-        out_shape=shapes[0] if single else shapes,
-        in_specs=specs,
-        out_specs=VMEM if single else [VMEM] * len(shapes),
+        out_shape=outs,
+        in_specs=[VMEM] * len(args),
+        out_specs=VMEM if single else [VMEM] * len(outs),
         scratch_shapes=list(scratch),
         compiler_params=PARAMS,
         name=name,
@@ -374,67 +361,54 @@
     owners, rows = lax.axis_size("cam"), lax.axis_size("pts")
     per = params * width // LANES
     count = camera_index.shape[1]
-    me = lax.axis_index("cam").astype(jnp.int32)
-    spot = lax.axis_index("pts").astype(jnp.int32)
-    position = jnp.stack([me, (spot >= per).astype(jnp.int32), jnp.minimum(spot, per - 1)])
     jac_cam, jac_pt = jac_cam[0], jac_pt[0]
     share = 1.0 / rows
 
-    mine, own = call(
-        prepare_kernel, [((per, LANES), F32), ((5 * per, LANES), F32)],
-        [SMEM, SMEM] + [HBM] * 3, position, anchors, right_side, camera_damping, preconditioner,
-        scratch=[pltpu.VMEM((params, width), F32)] * 3 + [pltpu.SemaphoreType.DMA((3,))],
-        name="prepare",
-    )
+    ids = lax.axis_index("cam") * width + jnp.arange(width, dtype=jnp.int32)
+    keep = 1.0 - jnp.any(anchors[:, None] == ids[None, :], axis=0).astype(F32)
+    mine = keep * (preconditioner * right_side)
     after, before, across = (
         lax.ppermute(mine, "cam", [(i, (i - d) % owners) for i in range(owners)])
         for d in (1, -1, owners // 2)
     )
-    inverse, masks, lane, slot = call(
-        functools.partial(setup_kernel, width, owners),
-        [((8, count), F32), ((8, count), F32), ((1, count), jnp.int32), ((1, count), jnp.int32)],
-        [SMEM] + [VMEM] * 4, position, jac_pt, point_index, point_damping[0], camera_index,
-        name="invert",
+    whole = jax.ShapeDtypeStruct((8, count), F32)
+    index = jax.ShapeDtypeStruct((1, count), jnp.int32)
+    inverse, masks, lane, slot, own = call(
+        functools.partial(setup_kernel, owners),
+        [whole, whole, index, index, jax.ShapeDtypeStruct((5 * per, LANES), F32)],
+        jac_pt, point_index, point_damping[0], camera_index, right_side, camera_damping,
+        preconditioner, keep[None], name="invert",
     )
     fixed = (jac_cam, jac_pt, lane, slot, masks, inverse)
     half = width // (2 * LANES)
     scratch = (pltpu.VMEM((half * LANES, count), BF16), pltpu.VMEM((8, count), F32))
-    sums = ((rows * BLOCKS, LANES), F32)
-    vector = ((per * BLOCKS, LANES), F32)
+    sums = jax.ShapeDtypeStruct((rows * BLOCKS, LANES), F32)
+    vector = jax.ShapeDtypeStruct((per * BLOCKS, LANES), F32)
 
     send, start = call(
-        functools.partial(first_kernel, share), [sums, vector], [VMEM] * 11,
+        functools.partial(first_kernel, share), [sums, vector],
         mine, after, before, across, own, *fixed, scratch=scratch, name="apply_first",
     )
     chunks = swap(send, "pts", rows)
-    chunks = call(
-        spread_kernel, [((owners * 8, LANES), F32)], [SMEM, VMEM, VMEM], position, chunks, own,
-        name="spread",
-    )
+    shape = jax.ShapeDtypeStruct((owners * 8, LANES), F32)
+    chunks = call(spread_kernel, shape, chunks, own, name="spread")
     chunks = swap(chunks, "cam", owners)
-    chunks = call(combine_kernel, [sums], [SMEM, VMEM], position, chunks, name="combine")
+    chunks = call(functools.partial(combine_kernel, per), sums, chunks, name="combine")
     first = swap(chunks, "pts", rows)
 
     send, step = call(
-        functools.partial(second_kernel, share), [sums, vector], [VMEM] * 9,
+        functools.partial(second_kernel, share), [sums, vector],
         first, start, own, *fixed, scratch=scratch, name="apply_second",
     )
     chunks = swap(send, "pts", rows)
-    chunks = call(
-        spread_own_kernel, [((owners, LANES), F32)], [SMEM, VMEM], position, chunks,
-        name="spread_own",
-    )
+    shape = jax.ShapeDtypeStruct((owners, LANES), F32)
+    chunks = call(functools.partial(spread_own_kernel, per), shape, chunks, name="spread_own")
     chunks = swap(chunks, "cam", owners)
-    chunks = call(
-        combine_own_kernel, [((rows, LANES), F32)], [VMEM], chunks, name="combine_own"
-    )
+    shape = jax.ShapeDtypeStruct((rows, LANES), F32)
+    chunks = call(combine_own_kernel, shape, chunks, name="combine_own")
     second = swap(chunks, "pts", rows)
-    return tuple(
-        call(
-            last_kernel, [((params, width), F32)] * 2, [VMEM] * 5, first, second, start, step,
-            own, name="finish",
-        )
-    )
+    shape = jax.ShapeDtypeStruct((params, width), F32)
+    return tuple(call(last_kernel, [shape, shape], first, second, start, step, own, name="finish"))
 
 
 def solution(mesh):

time: 132 us -> 128 us (0.970)
  Pallas kernels: 8.85 us -> 5.95 us
  local copies, waits for them, and re-layouts: 4.53 us -> 2.42 us
  other arithmetic: 0.08 us -> 1.59 us
    pallas_call x9 -> x8, Pallas kernels: 8.85 us -> 5.95 us  [call(): pl.pallas_call(kernel, out_shape=outs, in_specs=[VMEM] * len(args), out_s...]
    unnamed x19 -> x15, local copies, waits for them, and re-layouts: 4.53 us -> 2.42 us
  transfers between devices with their start and end apart: 3 -> 3, of which waited for: 0 -> 0; matrix products, arithmetic and copies ran while one was open for 1% -> 1% of each run, Pallas kernels for 2% -> 1%
where the time goes in v3:
time: 128 us
  blocking collectives  98.8 us (77%)
  starting transfers between devices  18.1 us (14%)
  Pallas kernels  5.95 us (5%)
  local copies, waits for them, and re-layouts  2.42 us (2%)
  other arithmetic  1.59 us (1%)
    all_to_all x6, blocking collectives, swap(): return lax.all_to_all(value, axis, 0, 0).reshape(size * rows, LANES)  98.8 us
    ppermute x3, starting transfers between devices, on_device(): lax.ppermute(mine, 'cam', [(i, (i - d) % owners) for i in range(owners)])  18.1 us
    pallas_call x8, Pallas kernels, call(): pl.pallas_call(kernel, out_shape=outs, in_specs=[VMEM] * len(args), out_s...  5.95 us
  transfers between devices with their start and end apart: 3, of which 0 were waited for; matrix products, arithmetic and copies ran while one was open for 1% of the time, Pallas kernels for 1%

profile of v3, /device:TPU:1, one launch (start us, length us, event | category | flops | bytes accessed | tf_op | source)
XLA Modules:
  0.0 127.6 jit_solution(10509694986730097426)
XLA Ops:
  0.7 0.8 compare_reduce_fusion
  1.5 0.8 multiply_multiply_fusion.mine
  2.2 15.1 %collective-permute-start.2 = (f32[9,512]{1,0:T(8,128)S(1)}, f32[9,512]{1,0:T(8,128)S(1)}, u32[]{:S(2)}, u32[]{:S(2)}) collective-permute-start(f32[9,512]{1,0:T(8,128)S(1)} %multiply_multiply_fusion.mine), channel_id=1, source_target_pairs={{0,8},{1,9},{2,10},{3,11},{4,12},{5,13},{6,14},{7,15},{8,0},{9,1},... | collective-permute-start | bytes 55304 | tf_op jit(solution)/shard_map/ppermute | solution.py:371
  17.3 3.0 %collective-permute-start.1 = (f32[9,512]{1,0:T(8,128)S(1)}, f32[9,512]{1,0:T(8,128)S(1)}, u32[]{:S(2)}, u32[]{:S(2)}) collective-permute-start(f32[9,512]{1,0:T(8,128)S(1)} %multiply_multiply_fusion.mine), channel_id=1, source_target_pairs={{0,1},{1,2},{2,3},{3,4},{4,5},{5,6},{6,7},{7,8},{8,9},{9,10},{10,1... | collective-permute-start | bytes 55304 | tf_op jit(solution)/shard_map/ppermute | solution.py:371
  20.3 0.7 copy.23
  21.0 1.0 copy.22
  22.0 0.0 copy-start
  22.0 0.0 copy-start.1
  22.0 0.0 copy-start.2
  22.0 0.0 copy-start.3
  22.0 0.2 copy.21
  22.2 0.5 copy-done
  22.7 0.0 copy-done.1
  22.8 0.0 copy-done.2
  22.8 1.4 %invert.1 = (f32[8,4096]{1,0:T(8,128)S(1)}, f32[8,4096]{1,0:T(8,128)S(1)}, s32[1,4096]{1,0:T(1,128)S(1)}, s32[1,4096]{1,0:T(1,128)S(1)}, f32[180,128]{1,0:T(8,128)S(1)}) custom-call(f32[6,4096]{1,0:T(8,128)S(1)} %bitcast.28, s32[1,4096]{1,0:T(1,128)S(1)} %copy-done.3, f32[3,1024]{1,0:T(4,128)S(1)} %bitcast.42, s32[1,4096]{1,0:T(1,128)S(1)} %copy-done.4, ...), custom_call_target="tpu_custom_call" | custom-call | tf_op jit(solution)/shard_map/invert/pallas_call | solution.py:341
  24.3 1.8 %apply_first.1 = (f32[256,128]{1,0:T(8,128)S(1)}, f32[144,128]{1,0:T(8,128)S(1)}) custom-call(f32[9,512]{1,0:T(8,128)S(1)} %multiply_multiply_fusion.mine, f32[9,512]{1,0:T(8,128)S(1)} %collective-permute-done.after, f32[9,512]{1,0:T(8,128)S(1)} %collective-permute-done.1.before, f32[9,512]{1,0:T(8,128)S(1)} %collective-permute-done.2.across, ...), custom_call_target="tpu_custom_call" | custom-call | tf_op jit(solution)/shard_map/apply_first/pallas_call | solution.py:341
  26.1 24.5 %all_to_all.30 = f32[64,4,128]{2,1,0:T(4,128)S(1)} all-to-all(f32[64,4,128]{2,1,0:T(4,128)S(1)} %bitcast.41), channel_id=1, replica_groups=mesh['pts'=64,'cam'=16] {'pts'}, dimensions={0} | all-to-all | bytes 262144 | tf_op jit(solution)/shard_map/all_to_all | solution.py:355
  50.6 16.2 %all_to_all.31 = f32[16,8,128]{2,1,0:T(8,128)S(1)} all-to-all(f32[16,8,128]{2,1,0:T(8,128)S(1)} %bitcast.37), channel_id=1, replica_groups=mesh['pts'=64,'cam'=16] {'cam'}, dimensions={0} | all-to-all | bytes 131072 | tf_op jit(solution)/shard_map/all_to_all | solution.py:355
  66.9 15.6 %all_to_all.32 = f32[64,4,128]{2,1,0:T(4,128)S(1)} all-to-all(f32[64,4,128]{2,1,0:T(4,128)S(1)} %bitcast.34), channel_id=1, replica_groups=mesh['pts'=64,'cam'=16] {'pts'}, dimensions={0} | all-to-all | bytes 262144 | tf_op jit(solution)/shard_map/all_to_all | solution.py:355
  82.5 1.8 %apply_second.1 = (f32[256,128]{1,0:T(8,128)S(1)}, f32[144,128]{1,0:T(8,128)S(1)}) custom-call(f32[256,128]{1,0:T(8,128)S(1)} %bitcast.31, f32[144,128]{1,0:T(8,128)S(1)} %get-tuple-element.17.start, f32[180,128]{1,0:T(8,128)S(1)} %get-tuple-element.11.own, f32[18,4096]{1,0:T(8,128)S(1)} %bitcast.27, f32[6,4096]{1,0:T(8,128)S(1)} %bitcast.30, ...), custom_call_target="tpu_custom_call" | custom-call | tf_op jit(solution)/shard_map/apply_second/pallas_call | solution.py:341
  84.3 15.4 %all_to_all.33 = f32[64,4,128]{2,1,0:T(4,128)S(1)} all-to-all(f32[64,4,128]{2,1,0:T(4,128)S(1)} %bitcast.40), channel_id=1, replica_groups=mesh['pts'=64,'cam'=16] {'pts'}, dimensions={0} | all-to-all | bytes 262144 | tf_op jit(solution)/shard_map/all_to_all | solution.py:355
  99.8 12.5 %all_to_all.34 = f32[16,1,128]{2,1,0:T(1,128)S(1)} all-to-all(f32[16,1,128]{2,1,0:T(1,128)S(1)} %bitcast.43), channel_id=1, replica_groups=mesh['pts'=64,'cam'=16] {'cam'}, dimensions={0} | all-to-all | bytes 16384 | tf_op jit(solution)/shard_map/all_to_all | solution.py:355
  112.2 14.6 %all_to_all.35 = f32[64,1,128]{2,1,0:T(1,128)S(1)} all-to-all(f32[64,1,128]{2,1,0:T(1,128)S(1)} %bitcast.39), channel_id=1, replica_groups=mesh['pts'=64,'cam'=16] {'pts'}, dimensions={0} | all-to-all | bytes 65536 | tf_op jit(solution)/shard_map/all_to_all | solution.py:355
  126.9 0.7 finish.1
  (15 shorter events, 0.2 us)
Async XLA Ops:
  0.6 21.3 %copy-start.5 = (f32[1,18,4096]{2,0,1:T(1,128)S(1)}, f32[1,18,4096]{2,0,1:T(1,128)}, u32[]{:S(2)}) copy-start(f32[1,18,4096]{2,0,1:T(1,128)} %param.12) | copy-start | bytes 884740
  2.2 22.0 %collective-permute-start.2 = (f32[9,512]{1,0:T(8,128)S(1)}, f32[9,512]{1,0:T(8,128)S(1)}, u32[]{:S(2)}, u32[]{:S(2)}) collective-permute-start(f32[9,512]{1,0:T(8,128)S(1)} %multiply_multiply_fusion.mine), channel_id=1, source_target_pairs={{0,8},{1,9},{2,10},{3,11},{4,12},{5,13},{6,14},{7,15},{8,0},{9,1},... | collective-permute-start | bytes 55304 | tf_op jit(solution)/shard_map/ppermute | solution.py:371
  17.3 6.9 %collective-permute-start.1 = (f32[9,512]{1,0:T(8,128)S(1)}, f32[9,512]{1,0:T(8,128)S(1)}, u32[]{:S(2)}, u32[]{:S(2)}) collective-permute-start(f32[9,512]{1,0:T(8,128)S(1)} %multiply_multiply_fusion.mine), channel_id=1, source_target_pairs={{0,1},{1,2},{2,3},{3,4},{4,5},{5,6},{6,7},{7,8},{8,9},{9,10},{10,1... | collective-permute-start | bytes 55304 | tf_op jit(solution)/shard_map/ppermute | solution.py:371
  20.3 4.0 %collective-permute-start = (f32[9,512]{1,0:T(8,128)S(1)}, f32[9,512]{1,0:T(8,128)S(1)}, u32[]{:S(2)}, u32[]{:S(2)}) collective-permute-start(f32[9,512]{1,0:T(8,128)S(1)} %multiply_multiply_fusion.mine), channel_id=1, source_target_pairs={{0,15},{1,0},{2,1},{3,2},{4,3},{5,4},{6,5},{7,6},{8,7},{9,8},{10,9... | collective-permute-start | bytes 55304 | tf_op jit(solution)/shard_map/ppermute | solution.py:371
  22.0 0.8 copy-start
  22.0 0.8 copy-start.1
  22.0 0.8 copy-start.2
  22.0 0.8 copy-start.3
  22.0 0.8 copy-start.4

commit v4 on v3

--- a/solution.py
+++ b/solution.py
@@ -11,6 +11,7 @@
 BLOCKS = 4
 STEPS = (1, 2, 4, 8)
 CHUNK = 512
+FOLDS = 8
 F32, BF16 = jnp.float32, jnp.bfloat16
 VMEM = pl.BlockSpec(memory_space=pltpu.VMEM)
 PARAMS = pltpu.CompilerParams(vmem_limit_bytes=40 * 1024 * 1024)
@@ -26,29 +27,37 @@
     return jnp.where(ids == row.astype(jnp.int16), BF16(1), BF16(0))
 
 
-def neighbour_masks(point):
-    count = point.shape[1]
-    before = [jnp.where(pltpu.roll(point, s, 1) == point, 1.0, 0.0) for s in STEPS]
-    after = [pltpu.roll(mask, count - s, 1) for mask, s in zip(before, STEPS)]
-    return jnp.concatenate(before + after, axis=0)
+def fold(ref, row):
+    parts = [ref[row : row + 1, i * CHUNK : (i + 1) * CHUNK] for i in range(FOLDS)]
+    return jnp.concatenate(parts, axis=0)
+
+
+def shifted(value, step):
+    ids = lax.broadcasted_iota(jnp.int32, value.shape, 1)
+    rolled = pltpu.roll(value, step % CHUNK, 1)
+    if step > 0:
+        return jnp.where(ids < step, pltpu.roll(rolled, 1, 0), rolled)
+    return jnp.where(ids >= CHUNK + step, pltpu.roll(rolled, FOLDS - 1, 0), rolled)
+
+
+def part(ref, index):
+    return ref[index * FOLDS : (index + 1) * FOLDS, :]
 
 
 def point_totals(value, masks):
-    count = value.shape[1]
     before = value
     after = value
     for i, step in enumerate(STEPS):
-        j = len(STEPS) + i
-        before = before + masks[i : i + 1] * pltpu.roll(before, step, 1)
-        after = after + masks[j : j + 1] * pltpu.roll(after, count - step, 1)
+        before = before + part(masks, i) * shifted(before, step)
+        after = after + part(masks, len(STEPS) + i) * shifted(after, -step)
     return before + (after - value)
 
 
 def setup_kernel(owners, jac_pt, point_ref, damping, camera_ref, right_side, camera_damping,
-                 preconditioner, keep, inverse, masks, lane, slot, own):
+                 preconditioner, keep, inverse, masks, folded, lane, slot, own):
     width = right_side.shape[1]
     own_arrays(right_side[...], camera_damping[...], preconditioner[...], keep[...], own)
-    camera = camera_ref[...]
+    camera = fold(camera_ref, 0)
     shift = lax.rem(lax.div(camera, width) - lax.axis_index("cam") + owners, owners)
     block = jnp.where(shift == 1, 1, jnp.where(shift == owners - 1, 2, 3))
     block = jnp.where(shift == 0, 0, block)
@@ -57,18 +66,19 @@
     lane[...] = lax.div(tile, 2) * LANES + lax.rem(inner, LANES)
     slot[...] = lax.rem(tile, 2) * BLOCKS + block
 
-    point = point_ref[...]
-    count = point.shape[1]
+    point = fold(point_ref, 0)
+    for i, step in enumerate(STEPS + tuple(-step for step in STEPS)):
+        same = jnp.where(shifted(point, step) == point, 1.0, 0.0)
+        masks[i * FOLDS : (i + 1) * FOLDS, :] = same
+    rows = [fold(jac_pt, r) for r in range(6)]
+    for r in range(6):
+        folded[r * FOLDS : (r + 1) * FOLDS, :] = rows[r]
+    pairs = [(0, 0), (0, 1), (0, 2), (1, 1), (1, 2), (2, 2)]
+    xx, xy, xz, yy, yz, zz = (
+        point_totals(rows[a] * rows[b] + rows[3 + a] * rows[3 + b], masks) for a, b in pairs
+    )
+
     tiles = damping.shape[1] // LANES
-    masks[...] = neighbour_masks(point)
-    rows = [jac_pt[r : r + 1, :] for r in range(6)]
-    pairs = [(0, 0), (0, 1), (0, 2), (1, 1), (1, 2), (2, 2)]
-    prods = [rows[a] * rows[b] + rows[3 + a] * rows[3 + b] for a, b in pairs]
-    prods = jnp.concatenate(prods + [jnp.zeros((2, count), F32)], axis=0)
-    summed = point_totals(prods, masks[...])
-
-    hot = one_hot(lax.rem(point, LANES), LANES).astype(BF16)
-    tile_mask = one_hot(lax.div(point, LANES), tiles)
     table = jnp.concatenate(
         [damping[k : k + 1, t * LANES : (t + 1) * LANES] for k in range(3) for t in range(tiles)],
         axis=0,
@@ -77,19 +87,16 @@
     rest = table - high.astype(F32)
     mid = rest.astype(BF16)
     low = (rest - mid.astype(F32)).astype(BF16)
-    picked = sum(
-        jnp.dot(part, hot, preferred_element_type=F32) for part in (high, mid, low)
-    )
-    damp = [
-        jnp.sum(picked[k * tiles : (k + 1) * tiles] * tile_mask, axis=0, keepdims=True)
-        for k in range(3)
-    ]
-    xx = summed[0:1] + damp[0]
-    xy = summed[1:2]
-    xz = summed[2:3]
-    yy = summed[3:4] + damp[1]
-    yz = summed[4:5]
-    zz = summed[5:6] + damp[2]
+    damp = [[], [], []]
+    for i in range(FOLDS):
+        spot = point[i : i + 1]
+        hot = short_one_hot(lax.rem(spot, LANES), LANES)
+        mask = one_hot(lax.div(spot, LANES), tiles)
+        picked = sum(jnp.dot(piece, hot, preferred_element_type=F32) for piece in (high, mid, low))
+        for k in range(3):
+            damp[k].append(lane_sums(picked[k * tiles : (k + 1) * tiles] * mask))
+    damp = [jnp.concatenate(rows_of, axis=0) for rows_of in damp]
+    xx, yy, zz = xx + damp[0], yy + damp[1], zz + damp[2]
     cof_xx = yy * zz - yz * yz
     cof_xy = xz * yz - xy * zz
     cof_xz = xy * yz - xz * yy
@@ -97,21 +104,15 @@
     cof_yz = xy * xz - xx * yz
     cof_zz = xx * yy - xy * xy
     det = xx * cof_xx + xy * cof_xy + xz * cof_xz
-    inverse[0:1] = cof_xx / det
-    inverse[1:2] = cof_xy / det
-    inverse[2:3] = cof_xz / det
-    inverse[3:4] = cof_yy / det
-    inverse[4:5] = cof_yz / det
-    inverse[5:6] = cof_zz / det
-    inverse[6:8] = jnp.zeros((2, count), F32)
+    for r, cof in enumerate((cof_xx, cof_xy, cof_xz, cof_yy, cof_yz, cof_zz)):
+        inverse[r * FOLDS : (r + 1) * FOLDS, :] = cof / det
 
 
 def lane_sums(value):
     return jnp.sum(value, axis=0, keepdims=True)
 
 
-def schur(vector, send, jac_cam, jac_pt, lane, slot, masks, inverse, hot, error):
-    count = lane.shape[1]
+def schur(vector, send, jac_cam, folded, lane, slot, masks, inverse, hot, error):
     params = jac_cam.shape[0] // 2
     slots = 2 * BLOCKS
     half = hot.shape[0] // LANES
@@ -122,30 +123,24 @@
     low = (table - high.astype(F32)).astype(BF16)
     table = jnp.concatenate([high, low], axis=0)
 
-    def predict(i, _):
-        span = pl.ds(pl.multiple_of(i * CHUNK, CHUNK), CHUNK)
-        spot = short_one_hot(lane[:, span], half * LANES)
+    for i in range(FOLDS):
+        span = slice(i * CHUNK, (i + 1) * CHUNK)
+        spot = short_one_hot(lane[i : i + 1, :], half * LANES)
         hot[:, span] = spot
         got = jnp.dot(table, spot, preferred_element_type=F32)
         got = got[:rows] + got[rows:]
-        mask = one_hot(slot[:, span], slots)
+        mask = one_hot(slot[i : i + 1, :], slots)
         for r in range(2):
             total = jnp.zeros((slots, CHUNK), F32)
             for a in range(params):
                 jac = jac_cam[r * params + a : r * params + a + 1, span]
                 total = total + jac * got[a * slots : (a + 1) * slots]
-            error[r : r + 1, span] = lane_sums(total * mask)
-        return 0
-
-    lax.fori_loop(0, count // CHUNK, predict, 0, unroll=count // CHUNK)
-
-    e0, e1 = error[0:1, :], error[1:2, :]
-    jp = [jac_pt[r : r + 1, :] for r in range(6)]
-    pulled = [jp[k] * e0 + jp[3 + k] * e1 for k in range(3)]
-    pulled = jnp.concatenate(pulled + [jnp.zeros((5, count), F32)], axis=0)
-    sums = point_totals(pulled, masks[...])
-    y0, y1, y2 = sums[0:1], sums[1:2], sums[2:3]
-    inv = [inverse[r : r + 1, :] for r in range(6)]
+            error[r * FOLDS + i : r * FOLDS + i + 1, :] = lane_sums(total * mask)
+
+    e0, e1 = part(error, 0), part(error, 1)
+    jp = [part(folded, r) for r in range(6)]
+    inv = [part(inverse, r) for r in range(6)]
+    y0, y1, y2 = (point_totals(jp[k] * e0 + jp[3 + k] * e1, masks) for k in range(3))
     z = (
         inv[0] * y0 + inv[1] * y1 + inv[2] * y2,
         inv[1] * y0 + inv[3] * y1 + inv[4] * y2,
@@ -154,27 +149,23 @@
     left0 = e0 - (jp[0] * z[0] + jp[1] * z[1] + jp[2] * z[2])
     left1 = e1 - (jp[3] * z[0] + jp[4] * z[1] + jp[5] * z[2])
     energy = e0 * left0 + e1 * left1
-    error[0:1, :] = left0
-    error[1:2, :] = left1
-
-    def push(i, total):
-        span = pl.ds(pl.multiple_of(i * CHUNK, CHUNK), CHUNK)
-        mask = one_hot(slot[:, span], slots)
-        first, second = error[0:1, span], error[1:2, span]
+
+    total = jnp.zeros((2 * rows, half * LANES), F32)
+    for i in range(FOLDS):
+        span = slice(i * CHUNK, (i + 1) * CHUNK)
+        mask = one_hot(slot[i : i + 1, :], slots)
+        first, second = mask * left0[i : i + 1], mask * left1[i : i + 1]
         highs, lows = [], []
         for a in range(params):
             value = jac_cam[a : a + 1, span] * first
             value = value + jac_cam[params + a : params + a + 1, span] * second
-            near = value.astype(BF16).astype(F32)
-            highs.append(near * mask)
-            lows.append((value - near) * mask)
-        both = jnp.concatenate(highs + lows, axis=0).astype(BF16)
-        return total + lax.dot_general(
+            near = value.astype(BF16)
+            highs.append(near)
+            lows.append((value - near.astype(F32)).astype(BF16))
+        both = jnp.concatenate(highs + lows, axis=0)
+        total = total + lax.dot_general(
             both, hot[:, span], (((1,), (1,)), ((), ())), preferred_element_type=F32
         )
-
-    total = jnp.zeros((2 * rows, half * LANES), F32)
-    total = lax.fori_loop(0, count // CHUNK, push, total, unroll=count // CHUNK)
     total = total[:rows] + total[rows:]
     for a in range(params):
         for h in range(half):
@@ -182,7 +173,7 @@
             send[start : start + slots, :] = total[
                 a * slots : (a + 1) * slots, h * LANES : (h + 1) * LANES
             ]
-    return sum(energy[:, t * LANES : (t + 1) * LANES] for t in range(count // LANES))
+    return lane_sums(sum(energy[:, t * LANES : (t + 1) * LANES] for t in range(CHUNK // LANES)))
 
 
 RIGHT, DAMPING, WEIGHTS, PULL, UNWEIGH = range(5)
@@ -217,28 +208,29 @@
     return jnp.sum(ref[row : row + 1, :], axis=1, keepdims=True)
 
 
-def first_kernel(share, mine, after, before, across, own, jac_cam, jac_pt, lane, slot,
+def first_kernel(share, mine, after, before, across, keep, own, jac_cam, folded, lane, slot,
                  masks, inverse, send, start, hot, error):
     params, width = mine.shape
     tiles = width // LANES
-    for block, part in enumerate((mine, after, before, across)):
+    for block, ref in enumerate((mine, after, before, across)):
+        value = ref[...] * keep[block : block + 1, :]
         for t in range(tiles):
             place = pl.ds(t * BLOCKS + block, params, stride=tiles * BLOCKS)
-            start[place, :] = part[:, t * LANES : (t + 1) * LANES]
-    energy = schur(start[...], send, jac_cam, jac_pt, lane, slot, masks, inverse, hot, error)
+            start[place, :] = value[:, t * LANES : (t + 1) * LANES]
+    energy = schur(start[...], send, jac_cam, folded, lane, slot, masks, inverse, hot, error)
     vector = start[pl.ds(0, params * tiles, stride=BLOCKS), :]
     energy = energy + share * lane_sums(own_part(own, DAMPING) * vector * vector)
     gamma = share * lane_sums(own_part(own, RIGHT) * vector)
     send_scalars(send, start.shape[0], (energy, gamma))
 
 
-def second_kernel(share, received, start, own, jac_cam, jac_pt, lane, slot, masks, inverse,
+def second_kernel(share, received, start, own, jac_cam, folded, lane, slot, masks, inverse,
                   send, step, hot, error):
     data_rows = start.shape[0]
     per = data_rows // BLOCKS
     alpha = scalar(received, data_rows + BLOCKS) / scalar(received, data_rows)
     step[...] = start[...] - alpha * received[0:data_rows, :]
-    energy = schur(step[...], send, jac_cam, jac_pt, lane, slot, masks, inverse, hot, error)
+    energy = schur(step[...], send, jac_cam, folded, lane, slot, masks, inverse, hot, error)
     vector = step[pl.ds(0, per, stride=BLOCKS), :]
     change = received[pl.ds(0, per, stride=BLOCKS), :]
     residual = own_part(own, UNWEIGH) * vector
@@ -364,30 +356,34 @@
     jac_cam, jac_pt = jac_cam[0], jac_pt[0]
     share = 1.0 / rows
 
-    ids = lax.axis_index("cam") * width + jnp.arange(width, dtype=jnp.int32)
-    keep = 1.0 - jnp.any(anchors[:, None] == ids[None, :], axis=0).astype(F32)
-    mine = keep * (preconditioner * right_side)
+    mine = preconditioner * right_side
+    shifts = (0, 1, -1, owners // 2)
     after, before, across = (
         lax.ppermute(mine, "cam", [(i, (i - d) % owners) for i in range(owners)])
-        for d in (1, -1, owners // 2)
-    )
-    whole = jax.ShapeDtypeStruct((8, count), F32)
-    index = jax.ShapeDtypeStruct((1, count), jnp.int32)
-    inverse, masks, lane, slot, own = call(
+        for d in shifts[1:]
+    )
+    firsts = (lax.axis_index("cam") + jnp.array(shifts) + owners) % owners * width
+    ids = firsts[:, None] + jnp.arange(width, dtype=jnp.int32)[None]
+    keep = 1.0 - jnp.any(anchors[:, None, None] == ids[None], axis=0).astype(F32)
+    folds = [
+        jax.ShapeDtypeStruct((count_of * FOLDS, CHUNK), kind)
+        for count_of, kind in ((6, F32), (8, F32), (6, F32), (1, jnp.int32), (1, jnp.int32))
+    ]
+    inverse, masks, folded, lane, slot, own = call(
         functools.partial(setup_kernel, owners),
-        [whole, whole, index, index, jax.ShapeDtypeStruct((5 * per, LANES), F32)],
+        folds + [jax.ShapeDtypeStruct((5 * per, LANES), F32)],
         jac_pt, point_index, point_damping[0], camera_index, right_side, camera_damping,
-        preconditioner, keep[None], name="invert",
-    )
-    fixed = (jac_cam, jac_pt, lane, slot, masks, inverse)
+        preconditioner, keep[:1], name="invert",
+    )
+    fixed = (jac_cam, folded, lane, slot, masks, inverse)
     half = width // (2 * LANES)
-    scratch = (pltpu.VMEM((half * LANES, count), BF16), pltpu.VMEM((8, count), F32))
+    scratch = (pltpu.VMEM((half * LANES, count), BF16), pltpu.VMEM((2 * FOLDS, CHUNK), F32))
     sums = jax.ShapeDtypeStruct((rows * BLOCKS, LANES), F32)
     vector = jax.ShapeDtypeStruct((per * BLOCKS, LANES), F32)
 
     send, start = call(
         functools.partial(first_kernel, share), [sums, vector],
-        mine, after, before, across, own, *fixed, scratch=scratch, name="apply_first",
+        mine, after, before, across, keep, own, *fixed, scratch=scratch, name="apply_first",
     )
     chunks = swap(send, "pts", rows)
     shape = jax.ShapeDtypeStruct((owners * 8, LANES), F32)

time: 128 us -> 127 us (level)
  transfers between devices with their start and end apart: 3 -> 3, of which waited for: 0 -> 0; matrix products, arithmetic and copies ran while one was open for 1% -> 2% of each run, Pallas kernels for 1% -> 1%
where the time goes in v4:
time: 127 us
  blocking collectives  98.8 us (78%)
  starting transfers between devices  18 us (14%)
  Pallas kernels  5.23 us (4%)
  other arithmetic  2.34 us (2%)
  local copies, waits for them, and re-layouts  1.54 us (1%)
    all_to_all x6, blocking collectives, swap(): return lax.all_to_all(value, axis, 0, 0).reshape(size * rows, LANES)  98.8 us
    ppermute x3, starting transfers between devices, on_device(): lax.ppermute(mine, 'cam', [(i, (i - d) % owners) for i in range(owners)])  18 us
    pallas_call x8, Pallas kernels, call(): pl.pallas_call(kernel, out_shape=outs, in_specs=[VMEM] * len(args), out_s...  5.23 us
  transfers between devices with their start and end apart: 3, of which 0 were waited for; matrix products, arithmetic and copies ran while one was open for 2% of the time, Pallas kernels for 1%

profile of v4, /device:TPU:1, one launch (start us, length us, event | category | flops | bytes accessed | tf_op | source)
XLA Modules:
  0.0 126.8 jit_solution(7946172376537841085)
XLA Ops:
  0.6 0.8 mul.6.mine
  1.5 15.1 %collective-permute-start.2 = (f32[9,512]{1,0:T(8,128)S(1)}, f32[9,512]{1,0:T(8,128)S(1)}, u32[]{:S(2)}, u32[]{:S(2)}) collective-permute-start(f32[9,512]{1,0:T(8,128)S(1)} %mul.6.mine), channel_id=1, source_target_pairs={{0,8},{1,9},{2,10},{3,11},{4,12},{5,13},{6,14},{7,15},{8,0},{9,1},... | collective-permute-start | bytes 55304 | tf_op jit(solution)/shard_map/ppermute | solution.py:362
  16.6 3.0 %collective-permute-start.1 = (f32[9,512]{1,0:T(8,128)S(1)}, f32[9,512]{1,0:T(8,128)S(1)}, u32[]{:S(2)}, u32[]{:S(2)}) collective-permute-start(f32[9,512]{1,0:T(8,128)S(1)} %mul.6.mine), channel_id=1, source_target_pairs={{0,1},{1,2},{2,3},{3,4},{4,5},{5,6},{6,7},{7,8},{8,9},{9,10},{10,1... | collective-permute-start | bytes 55304 | tf_op jit(solution)/shard_map/ppermute | solution.py:362
  19.5 0.7 fusion
  20.2 0.1 iota_add_fusion
  20.3 0.8 compare_reduce_fusion
  21.1 0.7 copy.24
  21.8 0.1 copy.23
  21.9 0.0 copy-start
  21.9 0.0 copy-start.3
  21.9 0.2 copy.22
  22.1 0.5 copy-done
  22.6 0.0 copy-done.1
  22.6 0.0 copy-done.2
  22.7 0.7 invert.1
  23.4 1.8 %apply_first.1 = (f32[256,128]{1,0:T(8,128)S(1)}, f32[144,128]{1,0:T(8,128)S(1)}) custom-call(f32[9,512]{1,0:T(8,128)S(1)} %mul.6.mine, f32[9,512]{1,0:T(8,128)S(1)} %collective-permute-done.after, f32[9,512]{1,0:T(8,128)S(1)} %collective-permute-done.1.before, f32[9,512]{1,0:T(8,128)S(1)} %collective-permute-done.2.across, ...), custom_call_target="tpu_custom_call" | custom-call | tf_op jit(solution)/shard_map/apply_first/pallas_call | solution.py:333
  25.2 24.5 %all_to_all.30 = f32[64,4,128]{2,1,0:T(4,128)S(1)} all-to-all(f32[64,4,128]{2,1,0:T(4,128)S(1)} %bitcast.38), channel_id=1, replica_groups=mesh['pts'=64,'cam'=16] {'pts'}, dimensions={0} | all-to-all | bytes 262144 | tf_op jit(solution)/shard_map/all_to_all | solution.py:347
  49.8 16.2 %all_to_all.31 = f32[16,8,128]{2,1,0:T(8,128)S(1)} all-to-all(f32[16,8,128]{2,1,0:T(8,128)S(1)} %bitcast.34), channel_id=1, replica_groups=mesh['pts'=64,'cam'=16] {'cam'}, dimensions={0} | all-to-all | bytes 131072 | tf_op jit(solution)/shard_map/all_to_all | solution.py:347
  66.0 15.6 %all_to_all.32 = f32[64,4,128]{2,1,0:T(4,128)S(1)} all-to-all(f32[64,4,128]{2,1,0:T(4,128)S(1)} %bitcast.31), channel_id=1, replica_groups=mesh['pts'=64,'cam'=16] {'pts'}, dimensions={0} | all-to-all | bytes 262144 | tf_op jit(solution)/shard_map/all_to_all | solution.py:347
  81.6 1.9 %apply_second.1 = (f32[256,128]{1,0:T(8,128)S(1)}, f32[144,128]{1,0:T(8,128)S(1)}) custom-call(f32[256,128]{1,0:T(8,128)S(1)} %bitcast.27, f32[144,128]{1,0:T(8,128)S(1)} %get-tuple-element.19.start, f32[180,128]{1,0:T(8,128)S(1)} %get-tuple-element.12.own, f32[18,4096]{1,0:T(8,128)S(1)} %bitcast.26, f32[48,512]{1,0:T(8,128)S(1)} %get-tuple-element.13.folded, ...), custom_call_target="tpu_custom_call" | custom-call | tf_op jit(solution)/shard_map/apply_second/pallas_call | solution.py:333
  83.5 15.4 %all_to_all.33 = f32[64,4,128]{2,1,0:T(4,128)S(1)} all-to-all(f32[64,4,128]{2,1,0:T(4,128)S(1)} %bitcast.37), channel_id=1, replica_groups=mesh['pts'=64,'cam'=16] {'pts'}, dimensions={0} | all-to-all | bytes 262144 | tf_op jit(solution)/shard_map/all_to_all | solution.py:347
  98.9 12.5 %all_to_all.34 = f32[16,1,128]{2,1,0:T(1,128)S(1)} all-to-all(f32[16,1,128]{2,1,0:T(1,128)S(1)} %bitcast.40), channel_id=1, replica_groups=mesh['pts'=64,'cam'=16] {'cam'}, dimensions={0} | all-to-all | bytes 16384 | tf_op jit(solution)/shard_map/all_to_all | solution.py:347
  111.4 14.6 %all_to_all.35 = f32[64,1,128]{2,1,0:T(1,128)S(1)} all-to-all(f32[64,1,128]{2,1,0:T(1,128)S(1)} %bitcast.36), channel_id=1, replica_groups=mesh['pts'=64,'cam'=16] {'pts'}, dimensions={0} | all-to-all | bytes 65536 | tf_op jit(solution)/shard_map/all_to_all | solution.py:347
  126.0 0.7 finish.1
  (19 shorter events, 0.2 us)
Async XLA Ops:
  0.6 21.2 %copy-start.6 = (f32[1,6,4096]{2,0,1:T(1,128)S(1)}, f32[1,6,4096]{2,0,1:T(1,128)}, u32[]{:S(2)}) copy-start(f32[1,6,4096]{2,0,1:T(1,128)} %param.14) | copy-start | bytes 294916
  0.6 21.2 %copy-start.5 = (f32[1,18,4096]{2,0,1:T(1,128)S(1)}, f32[1,18,4096]{2,0,1:T(1,128)}, u32[]{:S(2)}) copy-start(f32[1,18,4096]{2,0,1:T(1,128)} %param.13) | copy-start | bytes 884740
  1.5 21.8 %collective-permute-start.2 = (f32[9,512]{1,0:T(8,128)S(1)}, f32[9,512]{1,0:T(8,128)S(1)}, u32[]{:S(2)}, u32[]{:S(2)}) collective-permute-start(f32[9,512]{1,0:T(8,128)S(1)} %mul.6.mine), channel_id=1, source_target_pairs={{0,8},{1,9},{2,10},{3,11},{4,12},{5,13},{6,14},{7,15},{8,0},{9,1},... | collective-permute-start | bytes 55304 | tf_op jit(solution)/shard_map/ppermute | solution.py:362
  16.6 6.8 %collective-permute-start.1 = (f32[9,512]{1,0:T(8,128)S(1)}, f32[9,512]{1,0:T(8,128)S(1)}, u32[]{:S(2)}, u32[]{:S(2)}) collective-permute-start(f32[9,512]{1,0:T(8,128)S(1)} %mul.6.mine), channel_id=1, source_target_pairs={{0,1},{1,2},{2,3},{3,4},{4,5},{5,6},{6,7},{7,8},{8,9},{9,10},{10,1... | collective-permute-start | bytes 55304 | tf_op jit(solution)/shard_map/ppermute | solution.py:362
  19.5 3.8 %collective-permute-start = (f32[9,512]{1,0:T(8,128)S(1)}, f32[9,512]{1,0:T(8,128)S(1)}, u32[]{:S(2)}, u32[]{:S(2)}) collective-permute-start(f32[9,512]{1,0:T(8,128)S(1)} %mul.6.mine), channel_id=1, source_target_pairs={{0,15},{1,0},{2,1},{3,2},{4,3},{5,4},{6,5},{7,6},{8,7},{9,8},{10,9... | collective-permute-start | bytes 55304 | tf_op jit(solution)/shard_map/ppermute | solution.py:362
  21.9 0.8 copy-start
  21.9 0.8 copy-start.1
  21.9 0.8 copy-start.2
  21.9 0.8 copy-start.3
  21.9 0.8 copy-start.4

commit v5 on v4

--- a/solution.py
+++ b/solution.py
@@ -5,13 +5,15 @@
 from jax import lax
 from jax.experimental import pallas as pl
 from jax.experimental.pallas import tpu as pltpu
-from jax.sharding import PartitionSpec as P
+from jax.sharding import Mesh, PartitionSpec as P
 
 LANES = 128
 BLOCKS = 4
 STEPS = (1, 2, 4, 8)
 CHUNK = 512
 FOLDS = 8
+PAIR = 5
+SCALARS = 64
 F32, BF16 = jnp.float32, jnp.bfloat16
 VMEM = pl.BlockSpec(memory_space=pltpu.VMEM)
 PARAMS = pltpu.CompilerParams(vmem_limit_bytes=40 * 1024 * 1024)
@@ -20,6 +22,14 @@
 def one_hot(row, count):
     ids = lax.broadcasted_iota(jnp.int32, (count, row.shape[1]), 0)
     return jnp.where(ids == row, 1.0, 0.0)
+
+
+def cam_index():
+    return lax.axis_index("z") * 2 + lax.axis_index("core")
+
+
+def pts_index():
+    return lax.axis_index("x") * lax.axis_size("y") + lax.axis_index("y")
 
 
 def short_one_hot(row, count):
@@ -58,7 +68,7 @@
     width = right_side.shape[1]
     own_arrays(right_side[...], camera_damping[...], preconditioner[...], keep[...], own)
     camera = fold(camera_ref, 0)
-    shift = lax.rem(lax.div(camera, width) - lax.axis_index("cam") + owners, owners)
+    shift = lax.rem(lax.div(camera, width) - cam_index() + owners, owners)
     block = jnp.where(shift == 1, 1, jnp.where(shift == owners - 1, 2, 3))
     block = jnp.where(shift == 0, 0, block)
     inner = lax.rem(camera, width)
@@ -224,36 +234,119 @@
     send_scalars(send, start.shape[0], (energy, gamma))
 
 
+def lane_ids(rows=1):
+    return lax.broadcasted_iota(jnp.int32, (rows, LANES), 1)
+
+
 def second_kernel(share, received, start, own, jac_cam, folded, lane, slot, masks, inverse,
-                  send, step, hot, error):
+                  send, step, sums, hot, error):
     data_rows = start.shape[0]
     per = data_rows // BLOCKS
     alpha = scalar(received, data_rows + BLOCKS) / scalar(received, data_rows)
     step[...] = start[...] - alpha * received[0:data_rows, :]
-    energy = schur(step[...], send, jac_cam, folded, lane, slot, masks, inverse, hot, error)
+    energy = schur(step[...], sums, jac_cam, folded, lane, slot, masks, inverse, hot, error)
     vector = step[pl.ds(0, per, stride=BLOCKS), :]
     change = received[pl.ds(0, per, stride=BLOCKS), :]
     residual = own_part(own, UNWEIGH) * vector
     energy = energy + share * lane_sums(own_part(own, DAMPING) * vector * vector)
     fresh = share * lane_sums(residual * vector)
     cross = share * lane_sums(residual * change)
-    send_scalars(send, data_rows, (energy, fresh, cross))
-
-
-def last_kernel(first, second, start, step, own, solution, residual):
+    ids = lane_ids(BLOCKS)
+    extra = jnp.zeros((BLOCKS, LANES), F32)
+    for index, row in enumerate((energy, fresh, cross)):
+        extra = jnp.where(ids == SCALARS + index, jnp.sum(row, axis=1, keepdims=True), extra)
+    extra = jnp.where(lax.broadcasted_iota(jnp.int32, extra.shape, 0) == 0, extra, 0.0)
+    for chunk in range(16):
+        base = chunk * 3 * BLOCKS
+        send[base : base + 2 * BLOCKS, :] = sums[chunk * 2 * BLOCKS : (chunk + 1) * 2 * BLOCKS, :]
+        third = (32 + chunk // 4) * BLOCKS
+        third = sums[third : third + BLOCKS, :]
+        if chunk % 4:
+            third = pltpu.roll(third, LANES - 32 * (chunk % 4), 1)
+        send[base + 2 * BLOCKS : base + 3 * BLOCKS, :] = jnp.where(ids < 32, third, extra)
+
+
+def pair_kernel(received, send):
+    rows = 3 * BLOCKS
+    first = received[0:rows, :]
+    second = received[rows : 2 * rows, :]
+    for source in range(2, received.shape[0] // rows, 2):
+        first = first + received[source * rows : (source + 1) * rows, :]
+        second = second + received[(source + 1) * rows : (source + 2) * rows, :]
+
+    def rows_of(value, block):
+        return [value[r * BLOCKS + block : r * BLOCKS + block + 1] for r in range(3)]
+
+    zero = [jnp.zeros((1, LANES), F32)] * 3
+    ids = lane_ids()
+    scalars = first[2 * BLOCKS : 2 * BLOCKS + 1] + second[2 * BLOCKS : 2 * BLOCKS + 1]
+    own_even = [a + b for a, b in zip(rows_of(first, 0), rows_of(second, 2))]
+    own_odd = [a + b for a, b in zip(rows_of(first, 1), rows_of(second, 0))]
+    pairs = (
+        (0, own_even, own_odd),
+        (1, rows_of(second, 1), zero),
+        (-1, zero, rows_of(first, 2)),
+        (4, rows_of(first, 3), rows_of(second, 3)),
+    )
+
+    def joined(even, odd):
+        mixed = jnp.where(ids < 32, even[2], pltpu.roll(odd[2], 32, 1))
+        mixed = jnp.where(ids < SCALARS, mixed, scalars)
+        return jnp.concatenate(even[:2] + odd[:2] + [mixed], axis=0)
+
+    size = lax.axis_size("z")
+    columns = send.shape[0] // (size * PAIR)
+    nothing = joined(zero, zero)
+    for spot in range(columns * size):
+        send[spot * PAIR : (spot + 1) * PAIR, :] = nothing
+    for shift, even, odd in pairs:
+        value = joined(even, odd)
+        place = lax.rem(lax.axis_index("z") + shift + size, size)
+        for x in range(columns):
+            send[pl.ds((x * size + place) * PAIR, PAIR), :] = value
+
+
+def pair_sum_kernel(received, send):
+    total = received[0:PAIR, :]
+    for source in range(1, received.shape[0] // PAIR):
+        total = total + received[source * PAIR : (source + 1) * PAIR, :]
+    for spot in range(send.shape[0] // PAIR):
+        send[spot * PAIR : (spot + 1) * PAIR, :] = total
+
+
+def last_kernel(first, second, start, step, own, solution, residual, sums):
     params, width = solution.shape
     tiles = width // LANES
     per = params * tiles
     data_rows = per * BLOCKS
+    odd = lax.axis_index("core") == 1
+    ids = lane_ids()
+    for chunk in range(16):
+        base = chunk * PAIR
+        even_rows, odd_rows = second[base : base + 2, :], second[base + 2 : base + 4, :]
+        sums[2 * chunk : 2 * chunk + 2, :] = jnp.where(odd, odd_rows, even_rows)
+    for q in range(4):
+        third = jnp.zeros((1, LANES), F32)
+        for i in range(4):
+            row = second[(4 * q + i) * PAIR + 4 : (4 * q + i) * PAIR + 5, :]
+            even_row = pltpu.roll(row, 32 * i, 1) if i else row
+            odd_row = pltpu.roll(row, (32 * i - 32) % LANES, 1) if i != 1 else row
+            place = jnp.logical_and(ids >= 32 * i, ids < 32 * (i + 1))
+            third = jnp.where(place, jnp.where(odd, odd_row, even_row), third)
+        sums[32 + q : 33 + q, :] = third
+
     curve, gamma = scalar(first, data_rows), scalar(first, data_rows + BLOCKS)
-    energy, fresh, cross = (scalar(second, per + i) for i in range(3))
+    mixed = second[PAIR - 1 : PAIR, :]
+    energy, fresh, cross = (
+        jnp.sum(jnp.where(ids == SCALARS + i, mixed, 0.0), axis=1, keepdims=True) for i in range(3)
+    )
     alpha = gamma / curve
     beta = fresh / gamma
     alpha_next = fresh / (energy + 2.0 * beta * cross + beta * beta * curve)
     for t in range(tiles):
         spread = pl.ds(t * BLOCKS, params, stride=tiles * BLOCKS)
         begin, vector, change = start[spread, :], step[spread, :], first[spread, :]
-        terms = second[pl.ds(t, params, stride=tiles), :]
+        terms = sums[pl.ds(t, params, stride=tiles), :]
         damping, unweigh = (
             own[pl.ds(which * per + t, params, stride=tiles), :] for which in (DAMPING, UNWEIGH)
         )
@@ -275,7 +368,7 @@
 def spread_kernel(received, own, send):
     total = chunk_sum(received)
     per = own.shape[0] // 5
-    at = jnp.minimum(lax.axis_index("pts"), per - 1)
+    at = jnp.minimum(pts_index(), per - 1)
     rows = [own[pl.ds(which * per + at, 1), :] for which in (WEIGHTS, PULL)]
     total = jnp.concatenate([total, *rows, jnp.zeros((2, LANES), F32)], axis=0)
     for at in range(0, send.shape[0], 8):
@@ -284,7 +377,7 @@
 
 def combine_kernel(per, received, send):
     owners = received.shape[0] // 8
-    me = lax.axis_index("cam")
+    me = cam_index()
 
     def row(owner, at):
         spot = lax.rem(owner + 2 * owners, owners) * 8 + at
@@ -301,31 +394,10 @@
     total = received[0:8, :]
     for owner in range(1, owners):
         total = total + received[owner * 8 : (owner + 1) * 8, :]
-    joined = jnp.where(lax.axis_index("pts") >= per, total[0:BLOCKS], joined)
+    joined = jnp.where(pts_index() >= per, total[0:BLOCKS], joined)
     joined = jnp.concatenate([joined, joined], axis=0)
     for at in range(0, send.shape[0], 8):
         send[at : at + 8, :] = joined
-
-
-def spread_own_kernel(per, received, send):
-    total = chunk_sum(received)
-    owners = send.shape[0]
-    scalars = jnp.broadcast_to(total[0:1], send.shape)
-    chunk = lax.axis_index("pts")
-    send[...] = jnp.where(chunk >= per, scalars, 0.0)
-
-    @pl.when(chunk < per)
-    def _():
-        for block, shift in enumerate((0, 1, -1, owners // 2)):
-            spot = lax.rem(lax.axis_index("cam") + shift + owners, owners)
-            send[pl.ds(spot, 1), :] = total[block : block + 1]
-
-
-def combine_own_kernel(received, send):
-    total = received[0:8, :]
-    for at in range(8, received.shape[0], 8):
-        total = total + received[at : at + 8, :]
-    send[...] = jnp.broadcast_to(lane_sums(total), send.shape)
 
 
 def call(kernel, outs, *args, scratch=(), name=None):
@@ -341,16 +413,18 @@
     )(*args)
 
 
-def swap(value, axis, size):
+def swap(value, axes, tile=BLOCKS):
+    size = lax.axis_size(axes)
     rows = value.shape[0] // size
-    value = value.reshape(size, rows, LANES)
-    return lax.all_to_all(value, axis, 0, 0).reshape(size * rows, LANES)
+    chunks = value.reshape(size, rows // tile, tile, LANES)
+    return lax.all_to_all(chunks, axes, 0, 0).reshape(value.shape)
 
 
 def on_device(right_side, camera_damping, preconditioner, jac_cam, jac_pt, camera_index,
               point_index, point_damping, anchors):
     params, width = right_side.shape
-    owners, rows = lax.axis_size("cam"), lax.axis_size("pts")
+    pts, cam, line, plane = ("x", "y"), ("z", "core"), ("y", "core"), ("x", "z")
+    owners, rows = lax.axis_size(cam), lax.axis_size(pts)
     per = params * width // LANES
     count = camera_index.shape[1]
     jac_cam, jac_pt = jac_cam[0], jac_pt[0]
@@ -359,10 +433,10 @@
     mine = preconditioner * right_side
     shifts = (0, 1, -1, owners // 2)
     after, before, across = (
-        lax.ppermute(mine, "cam", [(i, (i - d) % owners) for i in range(owners)])
+        lax.ppermute(mine, cam, [(i, (i - d) % owners) for i in range(owners)])
         for d in shifts[1:]
     )
-    firsts = (lax.axis_index("cam") + jnp.array(shifts) + owners) % owners * width
+    firsts = (cam_index() + jnp.array(shifts) + owners) % owners * width
     ids = firsts[:, None] + jnp.arange(width, dtype=jnp.int32)[None]
     keep = 1.0 - jnp.any(anchors[:, None, None] == ids[None], axis=0).astype(F32)
     folds = [
@@ -385,43 +459,55 @@
         functools.partial(first_kernel, share), [sums, vector],
         mine, after, before, across, keep, own, *fixed, scratch=scratch, name="apply_first",
     )
-    chunks = swap(send, "pts", rows)
+    chunks = swap(send, pts)
     shape = jax.ShapeDtypeStruct((owners * 8, LANES), F32)
     chunks = call(spread_kernel, shape, chunks, own, name="spread")
-    chunks = swap(chunks, "cam", owners)
+    chunks = swap(chunks, cam)
     chunks = call(functools.partial(combine_kernel, per), sums, chunks, name="combine")
-    first = swap(chunks, "pts", rows)
-
+    first = swap(chunks, pts)
+
+    thirds = jax.ShapeDtypeStruct((16 * 3 * BLOCKS, LANES), F32)
     send, step = call(
-        functools.partial(second_kernel, share), [sums, vector],
-        first, start, own, *fixed, scratch=scratch, name="apply_second",
-    )
-    chunks = swap(send, "pts", rows)
-    shape = jax.ShapeDtypeStruct((owners, LANES), F32)
-    chunks = call(functools.partial(spread_own_kernel, per), shape, chunks, name="spread_own")
-    chunks = swap(chunks, "cam", owners)
-    shape = jax.ShapeDtypeStruct((rows, LANES), F32)
-    chunks = call(combine_own_kernel, shape, chunks, name="combine_own")
-    second = swap(chunks, "pts", rows)
+        functools.partial(second_kernel, share), [thirds, vector], first, start, own, *fixed,
+        scratch=(pltpu.VMEM(vector.shape, F32), *scratch), name="apply_second",
+    )
+    chunks = swap(send, line)
+    shape = jax.ShapeDtypeStruct((lax.axis_size(plane) * PAIR, LANES), F32)
+    chunks = call(pair_kernel, shape, chunks, name="pair")
+    chunks = swap(chunks, plane, 1)
+    shape = jax.ShapeDtypeStruct((lax.axis_size(line) * PAIR, LANES), F32)
+    chunks = call(pair_sum_kernel, shape, chunks, name="pair_sum")
+    second = swap(chunks, line, 1)
     shape = jax.ShapeDtypeStruct((params, width), F32)
-    return tuple(call(last_kernel, [shape, shape], first, second, start, step, own, name="finish"))
+    return tuple(
+        call(
+            last_kernel, [shape, shape], first, second, start, step, own,
+            scratch=[pltpu.VMEM((per, LANES), F32)], name="finish",
+        )
+    )
 
 
 def solution(mesh):
+    cores = 2
+    high = mesh.shape["cam"] // cores
+    side = int(mesh.shape["pts"] ** 0.5)
+    grid = mesh.devices.reshape(side, mesh.shape["pts"] // side, high, cores)
+    mesh = Mesh(grid, ("x", "y", "z", "core"))
+    cam, whole = ("z", "core"), ("x", "y", "z", "core")
     return jax.shard_map(
         on_device,
         mesh=mesh,
         in_specs=(
-            P(None, "cam"),
-            P(None, "cam"),
-            P(None, "cam"),
-            P(("pts", "cam"), None, None),
-            P(("pts", "cam"), None, None),
-            P(("pts", "cam"), None),
-            P(("pts", "cam"), None),
-            P(("pts", "cam"), None, None),
+            P(None, cam),
+            P(None, cam),
+            P(None, cam),
+            P(whole, None, None),
+            P(whole, None, None),
+            P(whole, None),
+            P(whole, None),
+            P(whole, None, None),
             P(),
         ),
-        out_specs=(P(None, "cam"), P(None, "cam")),
+        out_specs=(P(None, cam), P(None, cam)),
         check_vma=False,
     )

time: 127 us -> 126 us (level)
  blocking collectives: 98.8 us -> 96.9 us
    all_to_all x6, blocking collectives: 98.8 us -> 96.9 us  [swap(): return lax.all_to_all(chunks, axes, 0, 0).reshape(value.shape)]
where the time goes in v5:
time: 126 us; the launch traced here: 125 us
  blocking collectives  96.9 us (77%)
  starting transfers between devices  18 us (14%)
  Pallas kernels  5.42 us (4%)
  other arithmetic  2.34 us (2%)
  local copies, waits for them, and re-layouts  1.54 us (1%)
    all_to_all x6, blocking collectives, swap(): return lax.all_to_all(chunks, axes, 0, 0).reshape(value.shape)  96.9 us
    ppermute x3, starting transfers between devices, on_device(): lax.ppermute(mine, cam, [(i, (i - d) % owners) for i in range(owners)])  18 us
    pallas_call x8, Pallas kernels, call(): pl.pallas_call(kernel, out_shape=outs, in_specs=[VMEM] * len(args), out_s...  5.42 us
  transfers between devices with their start and end apart: 3, of which 0 were waited for; matrix products, arithmetic and copies ran while one was open for 2% of the time, Pallas kernels for 1%

profile of v5, /device:TPU:1, one launch (start us, length us, event | category | flops | bytes accessed | tf_op | source)
XLA Modules:
  0.0 125.1 jit_solution(13205500927081872837)
XLA Ops:
  0.6 0.8 mul.9.mine
  1.5 15.1 %collective-permute-start.2 = (f32[9,512]{1,0:T(8,128)S(1)}, f32[9,512]{1,0:T(8,128)S(1)}, u32[]{:S(2)}, u32[]{:S(2)}) collective-permute-start(f32[9,512]{1,0:T(8,128)S(1)} %mul.9.mine), channel_id=1, source_target_pairs={{0,8},{1,9},{2,10},{3,11},{4,12},{5,13},{6,14},{7,15},{8,0},{9,1},... | collective-permute-start | bytes 55304 | tf_op jit(solution)/shard_map/ppermute | solution.py:436
  16.6 3.0 %collective-permute-start.1 = (f32[9,512]{1,0:T(8,128)S(1)}, f32[9,512]{1,0:T(8,128)S(1)}, u32[]{:S(2)}, u32[]{:S(2)}) collective-permute-start(f32[9,512]{1,0:T(8,128)S(1)} %mul.9.mine), channel_id=1, source_target_pairs={{0,1},{1,2},{2,3},{3,4},{4,5},{5,6},{6,7},{7,8},{8,9},{9,10},{10,1... | collective-permute-start | bytes 55304 | tf_op jit(solution)/shard_map/ppermute | solution.py:436
  19.5 0.7 fusion
  20.2 0.1 iota_add_fusion
  20.3 0.8 compare_reduce_fusion
  21.1 0.7 copy.28
  21.8 0.1 copy.27
  21.9 0.2 copy.26
  22.1 0.5 copy-done
  22.6 0.0 copy-done.1
  22.6 0.0 copy-done.2
  22.7 0.7 invert.1
  23.4 1.8 %apply_first.1 = (f32[256,128]{1,0:T(8,128)S(1)}, f32[144,128]{1,0:T(8,128)S(1)}) custom-call(f32[9,512]{1,0:T(8,128)S(1)} %mul.9.mine, f32[9,512]{1,0:T(8,128)S(1)} %collective-permute-done.after, f32[9,512]{1,0:T(8,128)S(1)} %collective-permute-done.1.before, f32[9,512]{1,0:T(8,128)S(1)} %collective-permute-done.2.across, ...), custom_call_target="tpu_custom_call" | custom-call | tf_op jit(solution)/shard_map/apply_first/pallas_call | solution.py:405
  25.2 24.5 %all_to_all.30 = f32[64,1,4,128]{3,2,1,0:T(4,128)S(1)} all-to-all(f32[64,1,4,128]{3,2,1,0:T(4,128)S(1)} %bitcast.39), channel_id=1, replica_groups=mesh['x'=8,'y'=8,'z'=8,'core'=2] {'x','y'}, dimensions={0} | all-to-all | bytes 262144 | tf_op jit(solution)/shard_map/all_to_all | solution.py:420
  49.7 16.2 %all_to_all.31 = f32[16,2,4,128]{3,2,1,0:T(4,128)S(1)} all-to-all(f32[16,2,4,128]{3,2,1,0:T(4,128)S(1)} %bitcast.36), channel_id=1, replica_groups=mesh['x'=8,'y'=8,'z'=8,'core'=2] {'z','core'}, dimensions={0} | all-to-all | bytes 131072 | tf_op jit(solution)/shard_map/all_to_all | solution.py:420
  66.0 15.6 %all_to_all.32 = f32[64,1,4,128]{3,2,1,0:T(4,128)S(1)} all-to-all(f32[64,1,4,128]{3,2,1,0:T(4,128)S(1)} %bitcast.33), channel_id=1, replica_groups=mesh['x'=8,'y'=8,'z'=8,'core'=2] {'x','y'}, dimensions={0} | all-to-all | bytes 262144 | tf_op jit(solution)/shard_map/all_to_all | solution.py:420
  81.6 1.9 %apply_second.1 = (f32[192,128]{1,0:T(8,128)S(1)}, f32[144,128]{1,0:T(8,128)S(1)}) custom-call(f32[256,128]{1,0:T(8,128)S(1)} %bitcast.27, f32[144,128]{1,0:T(8,128)S(1)} %get-tuple-element.19.start, f32[180,128]{1,0:T(8,128)S(1)} %get-tuple-element.12.own, f32[18,4096]{1,0:T(8,128)S(1)} %bitcast.26, f32[48,512]{1,0:T(8,128)S(1)} %get-tuple-element.13.folded, ...), custom_call_target="tpu_custom_call" | custom-call | tf_op jit(solution)/shard_map/apply_second/pallas_call | solution.py:405
  83.5 12.8 %all_to_all.33 = f32[16,3,4,128]{3,2,1,0:T(4,128)S(1)} all-to-all(f32[16,3,4,128]{3,2,1,0:T(4,128)S(1)} %bitcast.40), channel_id=1, replica_groups=mesh['x'=8,'y'=8,'z'=8,'core'=2] {'y','core'}, dimensions={0} | all-to-all | bytes 196608 | tf_op jit(solution)/shard_map/all_to_all | solution.py:420
  96.3 0.1 pair.1
  96.4 16.0 %all_to_all.34 = f32[64,5,1,128]{3,2,1,0:T(1,128)S(1)} all-to-all(f32[64,5,1,128]{3,2,1,0:T(1,128)S(1)} %bitcast.29), channel_id=1, replica_groups=mesh['x'=8,'y'=8,'z'=8,'core'=2] {'x','z'}, dimensions={0} | all-to-all | bytes 327680 | tf_op jit(solution)/shard_map/all_to_all | solution.py:420
  112.5 0.1 pair_sum.1
  112.5 11.8 %all_to_all.35 = f32[16,5,1,128]{3,2,1,0:T(1,128)S(1)} all-to-all(f32[16,5,1,128]{3,2,1,0:T(1,128)S(1)} %bitcast.38), channel_id=1, replica_groups=mesh['x'=8,'y'=8,'z'=8,'core'=2] {'y','core'}, dimensions={0} | all-to-all | bytes 81920 | tf_op jit(solution)/shard_map/all_to_all | solution.py:420
  124.3 0.7 finish.1
  (19 shorter events, 0.1 us)
Async XLA Ops:
  0.6 21.2 %copy-start.6 = (f32[1,6,4096]{2,0,1:T(1,128)S(1)}, f32[1,6,4096]{2,0,1:T(1,128)}, u32[]{:S(2)}) copy-start(f32[1,6,4096]{2,0,1:T(1,128)} %param.14) | copy-start | bytes 294916
  0.6 21.2 %copy-start.5 = (f32[1,18,4096]{2,0,1:T(1,128)S(1)}, f32[1,18,4096]{2,0,1:T(1,128)}, u32[]{:S(2)}) copy-start(f32[1,18,4096]{2,0,1:T(1,128)} %param.13) | copy-start | bytes 884740
  1.5 21.8 %collective-permute-start.2 = (f32[9,512]{1,0:T(8,128)S(1)}, f32[9,512]{1,0:T(8,128)S(1)}, u32[]{:S(2)}, u32[]{:S(2)}) collective-permute-start(f32[9,512]{1,0:T(8,128)S(1)} %mul.9.mine), channel_id=1, source_target_pairs={{0,8},{1,9},{2,10},{3,11},{4,12},{5,13},{6,14},{7,15},{8,0},{9,1},... | collective-permute-start | bytes 55304 | tf_op jit(solution)/shard_map/ppermute | solution.py:436
  16.6 6.8 %collective-permute-start.1 = (f32[9,512]{1,0:T(8,128)S(1)}, f32[9,512]{1,0:T(8,128)S(1)}, u32[]{:S(2)}, u32[]{:S(2)}) collective-permute-start(f32[9,512]{1,0:T(8,128)S(1)} %mul.9.mine), channel_id=1, source_target_pairs={{0,1},{1,2},{2,3},{3,4},{4,5},{5,6},{6,7},{7,8},{8,9},{9,10},{10,1... | collective-permute-start | bytes 55304 | tf_op jit(solution)/shard_map/ppermute | solution.py:436
  19.5 3.8 %collective-permute-start = (f32[9,512]{1,0:T(8,128)S(1)}, f32[9,512]{1,0:T(8,128)S(1)}, u32[]{:S(2)}, u32[]{:S(2)}) collective-permute-start(f32[9,512]{1,0:T(8,128)S(1)} %mul.9.mine), channel_id=1, source_target_pairs={{0,15},{1,0},{2,1},{3,2},{4,3},{5,4},{6,5},{7,6},{8,7},{9,8},{10,9... | collective-permute-start | bytes 55304 | tf_op jit(solution)/shard_map/ppermute | solution.py:436
  21.9 0.8 copy-start
  21.9 0.8 copy-start.1
  21.9 0.8 copy-start.2
  21.9 0.8 copy-start.3
  21.9 0.8 copy-start.4

commit v6 on v5

--- a/solution.py
+++ b/solution.py
@@ -12,6 +12,8 @@
 STEPS = (1, 2, 4, 8)
 CHUNK = 512
 FOLDS = 8
+QUARTER = 32
+LINE = 10
 PAIR = 5
 SCALARS = 64
 F32, BF16 = jnp.float32, jnp.bfloat16
@@ -251,35 +253,42 @@
     energy = energy + share * lane_sums(own_part(own, DAMPING) * vector * vector)
     fresh = share * lane_sums(residual * vector)
     cross = share * lane_sums(residual * change)
-    ids = lane_ids(BLOCKS)
-    extra = jnp.zeros((BLOCKS, LANES), F32)
+    ids = lane_ids()
+    extra = jnp.zeros((1, LANES), F32)
     for index, row in enumerate((energy, fresh, cross)):
         extra = jnp.where(ids == SCALARS + index, jnp.sum(row, axis=1, keepdims=True), extra)
-    extra = jnp.where(lax.broadcasted_iota(jnp.int32, extra.shape, 0) == 0, extra, 0.0)
     for chunk in range(16):
-        base = chunk * 3 * BLOCKS
-        send[base : base + 2 * BLOCKS, :] = sums[chunk * 2 * BLOCKS : (chunk + 1) * 2 * BLOCKS, :]
-        third = (32 + chunk // 4) * BLOCKS
-        third = sums[third : third + BLOCKS, :]
-        if chunk % 4:
-            third = pltpu.roll(third, LANES - 32 * (chunk % 4), 1)
-        send[base + 2 * BLOCKS : base + 3 * BLOCKS, :] = jnp.where(ids < 32, third, extra)
+        base = chunk * LINE
+        send[base : base + 8, :] = sums[chunk * 8 : (chunk + 1) * 8, :]
+        send[base + 9 : base + 10, :] = extra
+    for q in range(4):
+        thirds = sums[(32 + q) * BLOCKS : (33 + q) * BLOCKS, :]
+        rolled = [thirds] + [pltpu.roll(thirds, QUARTER * k, 1) for k in range(1, 4)]
+        for i in range(4):
+            mixed = rolled[(0 - i) % 4][0:1]
+            for block in range(1, BLOCKS):
+                piece = rolled[(block - i) % 4][block : block + 1]
+                mixed = jnp.where(ids >= QUARTER * block, piece, mixed)
+            at = (4 * q + i) * LINE + 8
+            send[at : at + 1, :] = mixed
 
 
 def pair_kernel(received, send):
-    rows = 3 * BLOCKS
-    first = received[0:rows, :]
-    second = received[rows : 2 * rows, :]
-    for source in range(2, received.shape[0] // rows, 2):
-        first = first + received[source * rows : (source + 1) * rows, :]
-        second = second + received[(source + 1) * rows : (source + 2) * rows, :]
+    first = received[0:LINE, :]
+    second = received[LINE : 2 * LINE, :]
+    for source in range(2, received.shape[0] // LINE, 2):
+        first = first + received[source * LINE : (source + 1) * LINE, :]
+        second = second + received[(source + 1) * LINE : (source + 2) * LINE, :]
 
     def rows_of(value, block):
-        return [value[r * BLOCKS + block : r * BLOCKS + block + 1] for r in range(3)]
+        third = value[8:9]
+        if block:
+            third = pltpu.roll(third, LANES - QUARTER * block, 1)
+        return [value[block : block + 1], value[BLOCKS + block : BLOCKS + block + 1], third]
 
     zero = [jnp.zeros((1, LANES), F32)] * 3
     ids = lane_ids()
-    scalars = first[2 * BLOCKS : 2 * BLOCKS + 1] + second[2 * BLOCKS : 2 * BLOCKS + 1]
+    scalars = first[9:10] + second[9:10]
     own_even = [a + b for a, b in zip(rows_of(first, 0), rows_of(second, 2))]
     own_odd = [a + b for a, b in zip(rows_of(first, 1), rows_of(second, 0))]
     pairs = (
@@ -290,7 +299,7 @@
     )
 
     def joined(even, odd):
-        mixed = jnp.where(ids < 32, even[2], pltpu.roll(odd[2], 32, 1))
+        mixed = jnp.where(ids < QUARTER, even[2], pltpu.roll(odd[2], QUARTER, 1))
         mixed = jnp.where(ids < SCALARS, mixed, scalars)
         return jnp.concatenate(even[:2] + odd[:2] + [mixed], axis=0)
 
@@ -365,36 +374,66 @@
     return total[0:BLOCKS] + total[BLOCKS:]
 
 
+def own_rows(own):
+    per = own.shape[0] // 5
+    at = jnp.minimum(pts_index(), per - 1)
+    return [own[pl.ds(which * per + at, 1), :] for which in (WEIGHTS, PULL)]
+
+
 def spread_kernel(received, own, send):
     total = chunk_sum(received)
-    per = own.shape[0] // 5
-    at = jnp.minimum(pts_index(), per - 1)
-    rows = [own[pl.ds(which * per + at, 1), :] for which in (WEIGHTS, PULL)]
-    total = jnp.concatenate([total, *rows, jnp.zeros((2, LANES), F32)], axis=0)
+    owners = send.shape[0] // BLOCKS
+    mine, after, before, across = (total[b : b + 1] for b in range(BLOCKS))
+    zero = jnp.zeros((1, LANES), F32)
+    rows = own_rows(own)
+    half = owners // 2
+    parts = {
+        0: (mine, after, before, across),
+        1: (after, mine, *rows),
+        -1: (before, mine, *rows),
+        half: (across, mine, *rows),
+        2: (after, zero, zero, zero),
+        -2: (before, zero, zero, zero),
+        half - 1: (across, before, zero, zero),
+        half + 1: (across, after, zero, zero),
+    }
+    is_sums = pts_index() < own.shape[0] // 5
+    twice = jnp.concatenate([total, total], axis=0)
     for at in range(0, send.shape[0], 8):
-        send[at : at + 8, :] = total
-
-
-def combine_kernel(per, received, send):
-    owners = received.shape[0] // 8
+        send[at : at + 8, :] = jnp.where(is_sums, 0.0, twice)
+
+    @pl.when(is_sums)
+    def _():
+        for shift, value in parts.items():
+            spot = lax.rem(cam_index() + shift + owners, owners) * BLOCKS
+            send[pl.ds(spot, BLOCKS), :] = jnp.concatenate(value, axis=0)
+
+
+def combine_kernel(received, own, send):
+    owners = received.shape[0] // BLOCKS
+    half = owners // 2
     me = cam_index()
 
-    def row(owner, at):
-        spot = lax.rem(owner + 2 * owners, owners) * 8 + at
+    def row(shift, at):
+        spot = lax.rem(me + shift + owners, owners) * BLOCKS + at
         return received[pl.ds(spot, 1), :]
 
-    def block_change(owner):
-        terms = (row(owner, 0) + row(owner - 1, 1)) + (
-            row(owner + 1, 2) + row(owner + owners // 2, 3)
-        )
-        return row(owner, BLOCKS + 1) + row(owner, BLOCKS) * terms
-
-    joined = [block_change(me + shift) for shift in (0, 1, -1, owners // 2)]
+    sums = (
+        (row(0, 0) + row(-1, 0)) + (row(1, 0) + row(half, 0)),
+        (row(1, 1) + row(0, 1)) + (row(2, 0) + row(half + 1, 0)),
+        (row(-1, 1) + row(-2, 0)) + (row(0, 2) + row(half - 1, 0)),
+        (row(half, 1) + row(half - 1, 1)) + (row(half + 1, 1) + row(0, 3)),
+    )
+    joined = []
+    for block, shift in enumerate((0, 1, -1, half)):
+        weights, pull = (row(shift, 2), row(shift, 3)) if block else own_rows(own)
+        joined.append(pull + weights * sums[block])
     joined = jnp.concatenate(joined, axis=0)
     total = received[0:8, :]
-    for owner in range(1, owners):
-        total = total + received[owner * 8 : (owner + 1) * 8, :]
-    joined = jnp.where(pts_index() >= per, total[0:BLOCKS], joined)
+    for at in range(8, received.shape[0], 8):
+        total = total + received[at : at + 8, :]
+    total = total[0:BLOCKS] + total[BLOCKS:]
+    joined = jnp.where(pts_index() < own.shape[0] // 5, joined, total)
     joined = jnp.concatenate([joined, joined], axis=0)
     for at in range(0, send.shape[0], 8):
         send[at : at + 8, :] = joined
@@ -460,18 +499,18 @@
         mine, after, before, across, keep, own, *fixed, scratch=scratch, name="apply_first",
     )
     chunks = swap(send, pts)
-    shape = jax.ShapeDtypeStruct((owners * 8, LANES), F32)
+    shape = jax.ShapeDtypeStruct((owners * BLOCKS, LANES), F32)
     chunks = call(spread_kernel, shape, chunks, own, name="spread")
     chunks = swap(chunks, cam)
-    chunks = call(functools.partial(combine_kernel, per), sums, chunks, name="combine")
+    chunks = call(combine_kernel, sums, chunks, own, name="combine")
     first = swap(chunks, pts)
 
-    thirds = jax.ShapeDtypeStruct((16 * 3 * BLOCKS, LANES), F32)
+    chunked = jax.ShapeDtypeStruct((16 * LINE, LANES), F32)
     send, step = call(
-        functools.partial(second_kernel, share), [thirds, vector], first, start, own, *fixed,
+        functools.partial(second_kernel, share), [chunked, vector], first, start, own, *fixed,
         scratch=(pltpu.VMEM(vector.shape, F32), *scratch), name="apply_second",
     )
-    chunks = swap(send, line)
+    chunks = swap(send, line, 1)
     shape = jax.ShapeDtypeStruct((lax.axis_size(plane) * PAIR, LANES), F32)
     chunks = call(pair_kernel, shape, chunks, name="pair")
     chunks = swap(chunks, plane, 1)

time: 126 us -> 125 us (level)
  no operation moved by 1% of the time
where the time goes in v6:
time: 125 us; the launch traced here: 124 us
  blocking collectives  96.2 us (77%)
  starting transfers between devices  18 us (14%)
  Pallas kernels  5.53 us (4%)
  other arithmetic  2.34 us (2%)
  local copies, waits for them, and re-layouts  1.54 us (1%)
    all_to_all x6, blocking collectives, swap(): return lax.all_to_all(chunks, axes, 0, 0).reshape(value.shape)  96.2 us
    ppermute x3, starting transfers between devices, on_device(): lax.ppermute(mine, cam, [(i, (i - d) % owners) for i in range(owners)])  18 us
    pallas_call x8, Pallas kernels, call(): pl.pallas_call(kernel, out_shape=outs, in_specs=[VMEM] * len(args), out_s...  5.53 us
  transfers between devices with their start and end apart: 3, of which 0 were waited for; matrix products, arithmetic and copies ran while one was open for 2% of the time, Pallas kernels for 1%

profile of v6, /device:TPU:1, one launch (start us, length us, event | category | flops | bytes accessed | tf_op | source)
XLA Modules:
  0.0 124.5 jit_solution(2157682350135510072)
XLA Ops:
  0.6 0.8 mul.9.mine
  1.5 15.1 %collective-permute-start.2 = (f32[9,512]{1,0:T(8,128)S(1)}, f32[9,512]{1,0:T(8,128)S(1)}, u32[]{:S(2)}, u32[]{:S(2)}) collective-permute-start(f32[9,512]{1,0:T(8,128)S(1)} %mul.9.mine), channel_id=1, source_target_pairs={{0,8},{1,9},{2,10},{3,11},{4,12},{5,13},{6,14},{7,15},{8,0},{9,1},... | collective-permute-start | bytes 55304 | tf_op jit(solution)/shard_map/ppermute | solution.py:475
  16.6 3.0 %collective-permute-start.1 = (f32[9,512]{1,0:T(8,128)S(1)}, f32[9,512]{1,0:T(8,128)S(1)}, u32[]{:S(2)}, u32[]{:S(2)}) collective-permute-start(f32[9,512]{1,0:T(8,128)S(1)} %mul.9.mine), channel_id=1, source_target_pairs={{0,1},{1,2},{2,3},{3,4},{4,5},{5,6},{6,7},{7,8},{8,9},{9,10},{10,1... | collective-permute-start | bytes 55304 | tf_op jit(solution)/shard_map/ppermute | solution.py:475
  19.5 0.7 fusion
  20.2 0.1 iota_add_fusion
  20.3 0.8 compare_reduce_fusion
  21.1 0.7 copy.32
  21.8 0.1 copy.31
  21.9 0.2 copy.30
  22.1 0.5 copy-done
  22.6 0.0 copy-done.1
  22.7 0.7 invert.1
  23.4 1.8 %apply_first.1 = (f32[256,128]{1,0:T(8,128)S(1)}, f32[144,128]{1,0:T(8,128)S(1)}) custom-call(f32[9,512]{1,0:T(8,128)S(1)} %mul.9.mine, f32[9,512]{1,0:T(8,128)S(1)} %collective-permute-done.after, f32[9,512]{1,0:T(8,128)S(1)} %collective-permute-done.1.before, f32[9,512]{1,0:T(8,128)S(1)} %collective-permute-done.2.across, ...), custom_call_target="tpu_custom_call" | custom-call | tf_op jit(solution)/shard_map/apply_first/pallas_call | solution.py:444
  25.2 24.5 %all_to_all.30 = f32[64,1,4,128]{3,2,1,0:T(4,128)S(1)} all-to-all(f32[64,1,4,128]{3,2,1,0:T(4,128)S(1)} %bitcast.39), channel_id=1, replica_groups=mesh['x'=8,'y'=8,'z'=8,'core'=2] {'x','y'}, dimensions={0} | all-to-all | bytes 262144 | tf_op jit(solution)/shard_map/all_to_all | solution.py:459
  49.7 0.1 spread.1
  49.8 15.8 %all_to_all.31 = f32[16,1,4,128]{3,2,1,0:T(4,128)S(1)} all-to-all(f32[16,1,4,128]{3,2,1,0:T(4,128)S(1)} %bitcast.40), channel_id=1, replica_groups=mesh['x'=8,'y'=8,'z'=8,'core'=2] {'z','core'}, dimensions={0} | all-to-all | bytes 65536 | tf_op jit(solution)/shard_map/all_to_all | solution.py:459
  65.6 15.3 %all_to_all.32 = f32[64,1,4,128]{3,2,1,0:T(4,128)S(1)} all-to-all(f32[64,1,4,128]{3,2,1,0:T(4,128)S(1)} %bitcast.35), channel_id=1, replica_groups=mesh['x'=8,'y'=8,'z'=8,'core'=2] {'x','y'}, dimensions={0} | all-to-all | bytes 262144 | tf_op jit(solution)/shard_map/all_to_all | solution.py:459
  80.9 2.0 %apply_second.1 = (f32[160,128]{1,0:T(8,128)S(1)}, f32[144,128]{1,0:T(8,128)S(1)}) custom-call(f32[256,128]{1,0:T(8,128)S(1)} %bitcast.29, f32[144,128]{1,0:T(8,128)S(1)} %get-tuple-element.19.start, f32[180,128]{1,0:T(8,128)S(1)} %get-tuple-element.12.own, f32[18,4096]{1,0:T(8,128)S(1)} %bitcast.28, f32[48,512]{1,0:T(8,128)S(1)} %get-tuple-element.13.folded, ...), custom_call_target="tpu_custom_call" | custom-call | tf_op jit(solution)/shard_map/apply_second/pallas_call | solution.py:444
  82.9 12.8 %all_to_all.33 = f32[16,10,1,128]{3,2,1,0:T(1,128)S(1)} all-to-all(f32[16,10,1,128]{3,2,1,0:T(1,128)S(1)} %bitcast.42), channel_id=1, replica_groups=mesh['x'=8,'y'=8,'z'=8,'core'=2] {'y','core'}, dimensions={0} | all-to-all | bytes 163840 | tf_op jit(solution)/shard_map/all_to_all | solution.py:459
  95.7 0.2 pair.1
  95.8 16.0 %all_to_all.34 = f32[64,5,1,128]{3,2,1,0:T(1,128)S(1)} all-to-all(f32[64,5,1,128]{3,2,1,0:T(1,128)S(1)} %bitcast.31), channel_id=1, replica_groups=mesh['x'=8,'y'=8,'z'=8,'core'=2] {'x','z'}, dimensions={0} | all-to-all | bytes 327680 | tf_op jit(solution)/shard_map/all_to_all | solution.py:459
  111.8 0.1 pair_sum.1
  111.9 11.9 %all_to_all.35 = f32[16,5,1,128]{3,2,1,0:T(1,128)S(1)} all-to-all(f32[16,5,1,128]{3,2,1,0:T(1,128)S(1)} %bitcast.38), channel_id=1, replica_groups=mesh['x'=8,'y'=8,'z'=8,'core'=2] {'y','core'}, dimensions={0} | all-to-all | bytes 81920 | tf_op jit(solution)/shard_map/all_to_all | solution.py:459
  123.7 0.7 finish.1
  (19 shorter events, 0.1 us)
Async XLA Ops:
  0.6 21.2 %copy-start.6 = (f32[1,6,4096]{2,0,1:T(1,128)S(1)}, f32[1,6,4096]{2,0,1:T(1,128)}, u32[]{:S(2)}) copy-start(f32[1,6,4096]{2,0,1:T(1,128)} %param.14) | copy-start | bytes 294916
  0.6 21.2 %copy-start.5 = (f32[1,18,4096]{2,0,1:T(1,128)S(1)}, f32[1,18,4096]{2,0,1:T(1,128)}, u32[]{:S(2)}) copy-start(f32[1,18,4096]{2,0,1:T(1,128)} %param.13) | copy-start | bytes 884740
  1.5 21.8 %collective-permute-start.2 = (f32[9,512]{1,0:T(8,128)S(1)}, f32[9,512]{1,0:T(8,128)S(1)}, u32[]{:S(2)}, u32[]{:S(2)}) collective-permute-start(f32[9,512]{1,0:T(8,128)S(1)} %mul.9.mine), channel_id=1, source_target_pairs={{0,8},{1,9},{2,10},{3,11},{4,12},{5,13},{6,14},{7,15},{8,0},{9,1},... | collective-permute-start | bytes 55304 | tf_op jit(solution)/shard_map/ppermute | solution.py:475
  16.6 6.8 %collective-permute-start.1 = (f32[9,512]{1,0:T(8,128)S(1)}, f32[9,512]{1,0:T(8,128)S(1)}, u32[]{:S(2)}, u32[]{:S(2)}) collective-permute-start(f32[9,512]{1,0:T(8,128)S(1)} %mul.9.mine), channel_id=1, source_target_pairs={{0,1},{1,2},{2,3},{3,4},{4,5},{5,6},{6,7},{7,8},{8,9},{9,10},{10,1... | collective-permute-start | bytes 55304 | tf_op jit(solution)/shard_map/ppermute | solution.py:475
  19.5 3.8 %collective-permute-start = (f32[9,512]{1,0:T(8,128)S(1)}, f32[9,512]{1,0:T(8,128)S(1)}, u32[]{:S(2)}, u32[]{:S(2)}) collective-permute-start(f32[9,512]{1,0:T(8,128)S(1)} %mul.9.mine), channel_id=1, source_target_pairs={{0,15},{1,0},{2,1},{3,2},{4,3},{5,4},{6,5},{7,6},{8,7},{9,8},{10,9... | collective-permute-start | bytes 55304 | tf_op jit(solution)/shard_map/ppermute | solution.py:475
  21.9 0.8 copy-start
  21.9 0.8 copy-start.1
  21.9 0.8 copy-start.2
  21.9 0.8 copy-start.3
  21.9 0.8 copy-start.4

commit v7 on v6

--- a/solution.py
+++ b/solution.py
@@ -222,13 +222,12 @@
 
 def first_kernel(share, mine, after, before, across, keep, own, jac_cam, folded, lane, slot,
                  masks, inverse, send, start, hot, error):
-    params, width = mine.shape
-    tiles = width // LANES
+    params, tiles, _ = mine.shape
     for block, ref in enumerate((mine, after, before, across)):
-        value = ref[...] * keep[block : block + 1, :]
         for t in range(tiles):
             place = pl.ds(t * BLOCKS + block, params, stride=tiles * BLOCKS)
-            start[place, :] = value[:, t * LANES : (t + 1) * LANES]
+            kept = keep[block : block + 1, t * LANES : (t + 1) * LANES]
+            start[place, :] = ref[:, t, :] * kept
     energy = schur(start[...], send, jac_cam, folded, lane, slot, masks, inverse, hot, error)
     vector = start[pl.ds(0, params * tiles, stride=BLOCKS), :]
     energy = energy + share * lane_sums(own_part(own, DAMPING) * vector * vector)
@@ -469,7 +468,8 @@
     jac_cam, jac_pt = jac_cam[0], jac_pt[0]
     share = 1.0 / rows
 
-    mine = preconditioner * right_side
+    tiles = width // LANES
+    mine = preconditioner.reshape(params, tiles, LANES) * right_side.reshape(params, tiles, LANES)
     shifts = (0, 1, -1, owners // 2)
     after, before, across = (
         lax.ppermute(mine, cam, [(i, (i - d) % owners) for i in range(owners)])

time: 125 us -> 125 us (level)
  no operation moved by 1% of the time
where the time goes in v7:
time: 125 us
  blocking collectives  96.2 us (77%)
  starting transfers between devices  18.1 us (14%)
  Pallas kernels  5.58 us (4%)
  other arithmetic  2.34 us (2%)
  local copies, waits for them, and re-layouts  1.55 us (1%)
    all_to_all x6, blocking collectives, swap(): return lax.all_to_all(chunks, axes, 0, 0).reshape(value.shape)  96.2 us
    ppermute x3, starting transfers between devices, on_device(): lax.ppermute(mine, cam, [(i, (i - d) % owners) for i in range(owners)])  18.1 us
    pallas_call x8, Pallas kernels, call(): pl.pallas_call(kernel, out_shape=outs, in_specs=[VMEM] * len(args), out_s...  5.58 us
  transfers between devices with their start and end apart: 3, of which 0 were waited for; matrix products, arithmetic and copies ran while one was open for 2% of the time, Pallas kernels for 1%

profile of v7, /device:TPU:1, one launch (start us, length us, event | category | flops | bytes accessed | tf_op | source)
XLA Modules:
  0.0 124.6 jit_solution(15099704039015539460)
XLA Ops:
  0.6 0.8 mul.11
  1.5 15.1 %collective-permute-start.2 = (f32[9,4,128]{2,1,0:T(4,128)S(1)}, f32[9,4,128]{2,1,0:T(4,128)S(1)}, u32[]{:S(2)}, u32[]{:S(2)}) collective-permute-start(f32[9,4,128]{2,1,0:T(4,128)S(1)} %mul.12.mine), channel_id=1, source_target_pairs={{0,8},{1,9},{2,10},{3,11},{4,12},{5,13},{6,14},{7,15},{8,0},{9,1},... | collective-permute-start | bytes 55304 | tf_op jit(solution)/shard_map/ppermute | solution.py:475
  16.6 3.0 %collective-permute-start.1 = (f32[9,4,128]{2,1,0:T(4,128)S(1)}, f32[9,4,128]{2,1,0:T(4,128)S(1)}, u32[]{:S(2)}, u32[]{:S(2)}) collective-permute-start(f32[9,4,128]{2,1,0:T(4,128)S(1)} %mul.12.mine), channel_id=1, source_target_pairs={{0,1},{1,2},{2,3},{3,4},{4,5},{5,6},{6,7},{7,8},{8,9},{9,10},{10,1... | collective-permute-start | bytes 55304 | tf_op jit(solution)/shard_map/ppermute | solution.py:475
  19.6 0.7 fusion
  20.2 0.1 iota_add_fusion
  20.3 0.8 compare_reduce_fusion
  21.1 0.7 copy.32
  21.8 0.1 copy.31
  21.9 0.2 copy.30
  22.1 0.5 copy-done
  22.6 0.0 copy-done.1
  22.7 0.7 invert.1
  23.4 1.9 %apply_first.1 = (f32[256,128]{1,0:T(8,128)S(1)}, f32[144,128]{1,0:T(8,128)S(1)}) custom-call(f32[9,4,128]{2,1,0:T(4,128)S(1)} %mul.12.mine, f32[9,4,128]{2,1,0:T(4,128)S(1)} %collective-permute-done.after, f32[9,4,128]{2,1,0:T(4,128)S(1)} %collective-permute-done.1.before, f32[9,4,128]{2,1,0:T(4,128)S(1)} %collective-permute-done.2.across, ...), custom_call_target="tpu_custom_call" | custom-call | tf_op jit(solution)/shard_map/apply_first/pallas_call | solution.py:443
  25.3 24.5 %all_to_all.30 = f32[64,1,4,128]{3,2,1,0:T(4,128)S(1)} all-to-all(f32[64,1,4,128]{3,2,1,0:T(4,128)S(1)} %bitcast.39), channel_id=1, replica_groups=mesh['x'=8,'y'=8,'z'=8,'core'=2] {'x','y'}, dimensions={0} | all-to-all | bytes 262144 | tf_op jit(solution)/shard_map/all_to_all | solution.py:458
  49.8 0.1 spread.1
  49.8 15.8 %all_to_all.31 = f32[16,1,4,128]{3,2,1,0:T(4,128)S(1)} all-to-all(f32[16,1,4,128]{3,2,1,0:T(4,128)S(1)} %bitcast.40), channel_id=1, replica_groups=mesh['x'=8,'y'=8,'z'=8,'core'=2] {'z','core'}, dimensions={0} | all-to-all | bytes 65536 | tf_op jit(solution)/shard_map/all_to_all | solution.py:458
  65.7 15.3 %all_to_all.32 = f32[64,1,4,128]{3,2,1,0:T(4,128)S(1)} all-to-all(f32[64,1,4,128]{3,2,1,0:T(4,128)S(1)} %bitcast.35), channel_id=1, replica_groups=mesh['x'=8,'y'=8,'z'=8,'core'=2] {'x','y'}, dimensions={0} | all-to-all | bytes 262144 | tf_op jit(solution)/shard_map/all_to_all | solution.py:458
  81.0 2.0 %apply_second.1 = (f32[160,128]{1,0:T(8,128)S(1)}, f32[144,128]{1,0:T(8,128)S(1)}) custom-call(f32[256,128]{1,0:T(8,128)S(1)} %bitcast.29, f32[144,128]{1,0:T(8,128)S(1)} %get-tuple-element.19.start, f32[180,128]{1,0:T(8,128)S(1)} %get-tuple-element.12.own, f32[18,4096]{1,0:T(8,128)S(1)} %bitcast.28, f32[48,512]{1,0:T(8,128)S(1)} %get-tuple-element.13.folded, ...), custom_call_target="tpu_custom_call" | custom-call | tf_op jit(solution)/shard_map/apply_second/pallas_call | solution.py:443
  83.0 12.8 %all_to_all.33 = f32[16,10,1,128]{3,2,1,0:T(1,128)S(1)} all-to-all(f32[16,10,1,128]{3,2,1,0:T(1,128)S(1)} %bitcast.42), channel_id=1, replica_groups=mesh['x'=8,'y'=8,'z'=8,'core'=2] {'y','core'}, dimensions={0} | all-to-all | bytes 163840 | tf_op jit(solution)/shard_map/all_to_all | solution.py:458
  95.7 0.2 pair.1
  95.9 16.0 %all_to_all.34 = f32[64,5,1,128]{3,2,1,0:T(1,128)S(1)} all-to-all(f32[64,5,1,128]{3,2,1,0:T(1,128)S(1)} %bitcast.31), channel_id=1, replica_groups=mesh['x'=8,'y'=8,'z'=8,'core'=2] {'x','z'}, dimensions={0} | all-to-all | bytes 327680 | tf_op jit(solution)/shard_map/all_to_all | solution.py:458
  111.9 0.1 pair_sum.1
  112.0 11.9 %all_to_all.35 = f32[16,5,1,128]{3,2,1,0:T(1,128)S(1)} all-to-all(f32[16,5,1,128]{3,2,1,0:T(1,128)S(1)} %bitcast.38), channel_id=1, replica_groups=mesh['x'=8,'y'=8,'z'=8,'core'=2] {'y','core'}, dimensions={0} | all-to-all | bytes 81920 | tf_op jit(solution)/shard_map/all_to_all | solution.py:458
  123.8 0.7 finish.1
  (20 shorter events, 0.1 us)
Async XLA Ops:
  0.6 21.2 %copy-start.6 = (f32[1,6,4096]{2,0,1:T(1,128)S(1)}, f32[1,6,4096]{2,0,1:T(1,128)}, u32[]{:S(2)}) copy-start(f32[1,6,4096]{2,0,1:T(1,128)} %param.14) | copy-start | bytes 294916
  0.6 21.2 %copy-start.5 = (f32[1,18,4096]{2,0,1:T(1,128)S(1)}, f32[1,18,4096]{2,0,1:T(1,128)}, u32[]{:S(2)}) copy-start(f32[1,18,4096]{2,0,1:T(1,128)} %param.13) | copy-start | bytes 884740
  1.5 21.9 %collective-permute-start.2 = (f32[9,4,128]{2,1,0:T(4,128)S(1)}, f32[9,4,128]{2,1,0:T(4,128)S(1)}, u32[]{:S(2)}, u32[]{:S(2)}) collective-permute-start(f32[9,4,128]{2,1,0:T(4,128)S(1)} %mul.12.mine), channel_id=1, source_target_pairs={{0,8},{1,9},{2,10},{3,11},{4,12},{5,13},{6,14},{7,15},{8,0},{9,1},... | collective-permute-start | bytes 55304 | tf_op jit(solution)/shard_map/ppermute | solution.py:475
  16.6 6.8 %collective-permute-start.1 = (f32[9,4,128]{2,1,0:T(4,128)S(1)}, f32[9,4,128]{2,1,0:T(4,128)S(1)}, u32[]{:S(2)}, u32[]{:S(2)}) collective-permute-start(f32[9,4,128]{2,1,0:T(4,128)S(1)} %mul.12.mine), channel_id=1, source_target_pairs={{0,1},{1,2},{2,3},{3,4},{4,5},{5,6},{6,7},{7,8},{8,9},{9,10},{10,1... | collective-permute-start | bytes 55304 | tf_op jit(solution)/shard_map/ppermute | solution.py:475
  19.6 3.8 %collective-permute-start = (f32[9,4,128]{2,1,0:T(4,128)S(1)}, f32[9,4,128]{2,1,0:T(4,128)S(1)}, u32[]{:S(2)}, u32[]{:S(2)}) collective-permute-start(f32[9,4,128]{2,1,0:T(4,128)S(1)} %mul.12.mine), channel_id=1, source_target_pairs={{0,15},{1,0},{2,1},{3,2},{4,3},{5,4},{6,5},{7,6},{8,7},{9,8},{10,9... | collective-permute-start | bytes 55304 | tf_op jit(solution)/shard_map/ppermute | solution.py:475
  21.9 0.8 copy-start
  21.9 0.8 copy-start.1
  21.9 0.8 copy-start.2
  21.9 0.8 copy-start.3
  21.9 0.8 copy-start.4

commit v8 on v7

--- a/solution.py
+++ b/solution.py
@@ -13,8 +13,8 @@
 CHUNK = 512
 FOLDS = 8
 QUARTER = 32
-LINE = 10
 PAIR = 5
+OWN = 3
 SCALARS = 64
 F32, BF16 = jnp.float32, jnp.bfloat16
 VMEM = pl.BlockSpec(memory_space=pltpu.VMEM)
@@ -31,7 +31,8 @@
 
 
 def pts_index():
-    return lax.axis_index("x") * lax.axis_size("y") + lax.axis_index("y")
+    x = lax.axis_index("xa") * 2 + lax.axis_index("xb")
+    return x * lax.axis_size("y") + lax.axis_index("y")
 
 
 def short_one_hot(row, count):
@@ -256,70 +257,73 @@
     extra = jnp.zeros((1, LANES), F32)
     for index, row in enumerate((energy, fresh, cross)):
         extra = jnp.where(ids == SCALARS + index, jnp.sum(row, axis=1, keepdims=True), extra)
+    odd = lax.axis_index("core") == 1
     for chunk in range(16):
-        base = chunk * LINE
-        send[base : base + 8, :] = sums[chunk * 8 : (chunk + 1) * 8, :]
-        send[base + 9 : base + 10, :] = extra
-    for q in range(4):
+        q, i = chunk // 4, chunk % 4
         thirds = sums[(32 + q) * BLOCKS : (33 + q) * BLOCKS, :]
-        rolled = [thirds] + [pltpu.roll(thirds, QUARTER * k, 1) for k in range(1, 4)]
-        for i in range(4):
-            mixed = rolled[(0 - i) % 4][0:1]
-            for block in range(1, BLOCKS):
-                piece = rolled[(block - i) % 4][block : block + 1]
-                mixed = jnp.where(ids >= QUARTER * block, piece, mixed)
-            at = (4 * q + i) * LINE + 8
-            send[at : at + 1, :] = mixed
-
-
-def pair_kernel(received, send):
-    first = received[0:LINE, :]
-    second = received[LINE : 2 * LINE, :]
-    for source in range(2, received.shape[0] // LINE, 2):
-        first = first + received[source * LINE : (source + 1) * LINE, :]
-        second = second + received[(source + 1) * LINE : (source + 2) * LINE, :]
-
-    def rows_of(value, block):
-        third = value[8:9]
-        if block:
-            third = pltpu.roll(third, LANES - QUARTER * block, 1)
-        return [value[block : block + 1], value[BLOCKS + block : BLOCKS + block + 1], third]
-
-    zero = [jnp.zeros((1, LANES), F32)] * 3
+        low = pltpu.roll(thirds, (-QUARTER * i) % LANES, 1) if i else thirds
+        high = pltpu.roll(thirds, (QUARTER - QUARTER * i) % LANES, 1) if i != 1 else thirds
+        rows = sums[chunk * 2 * BLOCKS : (chunk + 1) * 2 * BLOCKS, :]
+
+        def two(a, b):
+            mixed = jnp.where(ids < SCALARS, high[b : b + 1], extra)
+            mixed = jnp.where(ids < QUARTER, low[a : a + 1], mixed)
+            pieces = [rows[at : at + 1] for at in (a, BLOCKS + a, b, BLOCKS + b)]
+            return jnp.concatenate(pieces + [mixed], axis=0)
+
+        same, other = two(0, 3), two(1, 2)
+        base = 2 * chunk * PAIR
+        send[base : base + PAIR, :] = jnp.where(odd, other, same)
+        send[base + PAIR : base + 2 * PAIR, :] = jnp.where(odd, same, other)
+
+
+def own_block_kernel(received, send):
+    evens = received[0:PAIR, :]
+    odds = received[PAIR : 2 * PAIR, :]
+    for source in range(2, received.shape[0] // PAIR, 2):
+        evens = evens + received[source * PAIR : (source + 1) * PAIR, :]
+        odds = odds + received[(source + 1) * PAIR : (source + 2) * PAIR, :]
+    odd = lax.axis_index("core") == 1
     ids = lane_ids()
-    scalars = first[9:10] + second[9:10]
-    own_even = [a + b for a, b in zip(rows_of(first, 0), rows_of(second, 2))]
-    own_odd = [a + b for a, b in zip(rows_of(first, 1), rows_of(second, 0))]
-    pairs = (
-        (0, own_even, own_odd),
-        (1, rows_of(second, 1), zero),
-        (-1, zero, rows_of(first, 2)),
-        (4, rows_of(first, 3), rows_of(second, 3)),
-    )
-
-    def joined(even, odd):
-        mixed = jnp.where(ids < QUARTER, even[2], pltpu.roll(odd[2], QUARTER, 1))
-        mixed = jnp.where(ids < SCALARS, mixed, scalars)
-        return jnp.concatenate(even[:2] + odd[:2] + [mixed], axis=0)
+    scalars = evens[PAIR - 1 : PAIR] + odds[PAIR - 1 : PAIR]
+    same = jnp.where(odd, odds, evens)
+    other = jnp.where(odd, evens, odds)
+
+    def block(value, which):
+        third = value[PAIR - 1 : PAIR]
+        if which:
+            third = pltpu.roll(third, LANES - QUARTER, 1)
+        return jnp.concatenate([value[2 * which : 2 * which + 2], third], axis=0)
+
+    other_first, other_second = block(other, 0), block(other, 1)
+    own = block(same, 0) + jnp.where(odd, other_first, other_second)
+    beside = jnp.where(odd, other_second, other_first)
+    across = block(same, 1)
+    is_third = lax.broadcasted_iota(jnp.int32, (OWN, LANES), 0) == OWN - 1
+    is_rest = jnp.logical_and(is_third, lane_ids(OWN) >= SCALARS)
+
+    def with_scalars(value):
+        return jnp.where(is_rest, scalars, value)
 
     size = lax.axis_size("z")
-    columns = send.shape[0] // (size * PAIR)
-    nothing = joined(zero, zero)
+    columns = send.shape[0] // (size * OWN)
+    nothing = with_scalars(jnp.zeros((OWN, LANES), F32))
     for spot in range(columns * size):
-        send[spot * PAIR : (spot + 1) * PAIR, :] = nothing
-    for shift, even, odd in pairs:
-        value = joined(even, odd)
+        send[spot * OWN : (spot + 1) * OWN, :] = nothing
+    step = 1 - 2 * lax.axis_index("core")
+    for shift, value in ((0, own), (step, beside), (size // 2, across)):
         place = lax.rem(lax.axis_index("z") + shift + size, size)
+        value = with_scalars(value)
         for x in range(columns):
-            send[pl.ds((x * size + place) * PAIR, PAIR), :] = value
-
-
-def pair_sum_kernel(received, send):
-    total = received[0:PAIR, :]
-    for source in range(1, received.shape[0] // PAIR):
-        total = total + received[source * PAIR : (source + 1) * PAIR, :]
-    for spot in range(send.shape[0] // PAIR):
-        send[spot * PAIR : (spot + 1) * PAIR, :] = total
+            send[pl.ds((x * size + place) * OWN, OWN), :] = value
+
+
+def own_sum_kernel(received, send):
+    total = received[0:OWN, :]
+    for source in range(1, received.shape[0] // OWN):
+        total = total + received[source * OWN : (source + 1) * OWN, :]
+    for spot in range(send.shape[0] // OWN):
+        send[spot * OWN : (spot + 1) * OWN, :] = total
 
 
 def last_kernel(first, second, start, step, own, solution, residual, sums):
@@ -327,24 +331,20 @@
     tiles = width // LANES
     per = params * tiles
     data_rows = per * BLOCKS
-    odd = lax.axis_index("core") == 1
     ids = lane_ids()
     for chunk in range(16):
-        base = chunk * PAIR
-        even_rows, odd_rows = second[base : base + 2, :], second[base + 2 : base + 4, :]
-        sums[2 * chunk : 2 * chunk + 2, :] = jnp.where(odd, odd_rows, even_rows)
+        sums[2 * chunk : 2 * chunk + 2, :] = second[chunk * OWN : chunk * OWN + 2, :]
     for q in range(4):
         third = jnp.zeros((1, LANES), F32)
         for i in range(4):
-            row = second[(4 * q + i) * PAIR + 4 : (4 * q + i) * PAIR + 5, :]
-            even_row = pltpu.roll(row, 32 * i, 1) if i else row
-            odd_row = pltpu.roll(row, (32 * i - 32) % LANES, 1) if i != 1 else row
-            place = jnp.logical_and(ids >= 32 * i, ids < 32 * (i + 1))
-            third = jnp.where(place, jnp.where(odd, odd_row, even_row), third)
+            at = (4 * q + i) * OWN + 2
+            row = second[at : at + 1, :]
+            row = pltpu.roll(row, QUARTER * i, 1) if i else row
+            third = jnp.where(ids >= QUARTER * i, row, third)
         sums[32 + q : 33 + q, :] = third
 
     curve, gamma = scalar(first, data_rows), scalar(first, data_rows + BLOCKS)
-    mixed = second[PAIR - 1 : PAIR, :]
+    mixed = second[OWN - 1 : OWN, :]
     energy, fresh, cross = (
         jnp.sum(jnp.where(ids == SCALARS + i, mixed, 0.0), axis=1, keepdims=True) for i in range(3)
     )
@@ -461,7 +461,8 @@
 def on_device(right_side, camera_damping, preconditioner, jac_cam, jac_pt, camera_index,
               point_index, point_damping, anchors):
     params, width = right_side.shape
-    pts, cam, line, plane = ("x", "y"), ("z", "core"), ("y", "core"), ("x", "z")
+    pts, cam = ("xa", "xb", "y"), ("z", "core")
+    near, wide, last = ("xb", "y", "core"), ("xa", "z"), ("xb", "y")
     owners, rows = lax.axis_size(cam), lax.axis_size(pts)
     per = params * width // LANES
     count = camera_index.shape[1]
@@ -505,18 +506,18 @@
     chunks = call(combine_kernel, sums, chunks, own, name="combine")
     first = swap(chunks, pts)
 
-    chunked = jax.ShapeDtypeStruct((16 * LINE, LANES), F32)
+    chunked = jax.ShapeDtypeStruct((lax.axis_size(near) * PAIR, LANES), F32)
     send, step = call(
         functools.partial(second_kernel, share), [chunked, vector], first, start, own, *fixed,
         scratch=(pltpu.VMEM(vector.shape, F32), *scratch), name="apply_second",
     )
-    chunks = swap(send, line, 1)
-    shape = jax.ShapeDtypeStruct((lax.axis_size(plane) * PAIR, LANES), F32)
-    chunks = call(pair_kernel, shape, chunks, name="pair")
-    chunks = swap(chunks, plane, 1)
-    shape = jax.ShapeDtypeStruct((lax.axis_size(line) * PAIR, LANES), F32)
-    chunks = call(pair_sum_kernel, shape, chunks, name="pair_sum")
-    second = swap(chunks, line, 1)
+    chunks = swap(send, near, 1)
+    shape = jax.ShapeDtypeStruct((lax.axis_size(wide) * OWN, LANES), F32)
+    chunks = call(own_block_kernel, shape, chunks, name="own_block")
+    chunks = swap(chunks, wide, 1)
+    shape = jax.ShapeDtypeStruct((lax.axis_size(last) * OWN, LANES), F32)
+    chunks = call(own_sum_kernel, shape, chunks, name="own_sum")
+    second = swap(chunks, last, 1)
     shape = jax.ShapeDtypeStruct((params, width), F32)
     return tuple(
         call(
@@ -530,9 +531,9 @@
     cores = 2
     high = mesh.shape["cam"] // cores
     side = int(mesh.shape["pts"] ** 0.5)
-    grid = mesh.devices.reshape(side, mesh.shape["pts"] // side, high, cores)
-    mesh = Mesh(grid, ("x", "y", "z", "core"))
-    cam, whole = ("z", "core"), ("x", "y", "z", "core")
+    grid = mesh.devices.reshape(side // 2, 2, mesh.shape["pts"] // side, high, cores)
+    cam, whole = ("z", "core"), ("xa", "xb", "y", "z", "core")
+    mesh = Mesh(grid, whole)
     return jax.shard_map(
         on_device,
         mesh=mesh,

time: 125 us -> 122 us (0.976)
  blocking collectives: 96.2 us -> 92.6 us
    all_to_all x6, blocking collectives: 96.2 us -> 92.6 us  [swap(): return lax.all_to_all(chunks, axes, 0, 0).reshape(value.shape)]
where the time goes in v8:
time: 122 us; the launch traced here: 121 us
  blocking collectives  92.6 us (76%)
  starting transfers between devices  18.1 us (15%)
  Pallas kernels  5.44 us (4%)
  other arithmetic  2.34 us (2%)
  local copies, waits for them, and re-layouts  1.55 us (1%)
    all_to_all x6, blocking collectives, swap(): return lax.all_to_all(chunks, axes, 0, 0).reshape(value.shape)  92.6 us
    ppermute x3, starting transfers between devices, on_device(): lax.ppermute(mine, cam, [(i, (i - d) % owners) for i in range(owners)])  18.1 us
    pallas_call x8, Pallas kernels, call(): pl.pallas_call(kernel, out_shape=outs, in_specs=[VMEM] * len(args), out_s...  5.44 us
  transfers between devices with their start and end apart: 3, of which 0 were waited for; matrix products, arithmetic and copies ran while one was open for 2% of the time, Pallas kernels for 1%

profile of v8, /device:TPU:1, one launch (start us, length us, event | category | flops | bytes accessed | tf_op | source)
XLA Modules:
  0.0 120.8 jit_solution(13017936558967635058)
XLA Ops:
  0.6 0.8 mul.11
  1.5 15.1 %collective-permute-start.2 = (f32[9,4,128]{2,1,0:T(4,128)S(1)}, f32[9,4,128]{2,1,0:T(4,128)S(1)}, u32[]{:S(2)}, u32[]{:S(2)}) collective-permute-start(f32[9,4,128]{2,1,0:T(4,128)S(1)} %mul.12.mine), channel_id=1, source_target_pairs={{0,8},{1,9},{2,10},{3,11},{4,12},{5,13},{6,14},{7,15},{8,0},{9,1},... | collective-permute-start | bytes 55304 | tf_op jit(solution)/shard_map/ppermute | solution.py:476
  16.6 3.0 %collective-permute-start.1 = (f32[9,4,128]{2,1,0:T(4,128)S(1)}, f32[9,4,128]{2,1,0:T(4,128)S(1)}, u32[]{:S(2)}, u32[]{:S(2)}) collective-permute-start(f32[9,4,128]{2,1,0:T(4,128)S(1)} %mul.12.mine), channel_id=1, source_target_pairs={{0,1},{1,2},{2,3},{3,4},{4,5},{5,6},{6,7},{7,8},{8,9},{9,10},{10,1... | collective-permute-start | bytes 55304 | tf_op jit(solution)/shard_map/ppermute | solution.py:476
  19.6 0.7 fusion
  20.2 0.1 iota_add_fusion
  20.3 0.8 compare_reduce_fusion
  21.1 0.7 copy.32
  21.8 0.1 copy.31
  21.9 0.2 copy.30
  22.1 0.5 copy-done
  22.6 0.0 copy-done.1
  22.7 0.0 copy-done.2
  22.7 0.7 invert.1
  23.4 1.9 %apply_first.1 = (f32[256,128]{1,0:T(8,128)S(1)}, f32[144,128]{1,0:T(8,128)S(1)}) custom-call(f32[9,4,128]{2,1,0:T(4,128)S(1)} %mul.12.mine, f32[9,4,128]{2,1,0:T(4,128)S(1)} %collective-permute-done.after, f32[9,4,128]{2,1,0:T(4,128)S(1)} %collective-permute-done.1.before, f32[9,4,128]{2,1,0:T(4,128)S(1)} %collective-permute-done.2.across, ...), custom_call_target="tpu_custom_call" | custom-call | tf_op jit(solution)/shard_map/apply_first/pallas_call | solution.py:443
  25.3 24.5 %all_to_all.30 = f32[64,1,4,128]{3,2,1,0:T(4,128)S(1)} all-to-all(f32[64,1,4,128]{3,2,1,0:T(4,128)S(1)} %bitcast.37), channel_id=1, replica_groups=mesh['xa'=4,'xb'=2,'y'=8,'z'=8,'core'=2] {'xa','xb','y'}, dimensions={0} | all-to-all | bytes 262144 | tf_op jit(solution)/shard_map/all_to_all | solution.py:458
  49.8 0.1 spread.1
  49.8 15.8 %all_to_all.31 = f32[16,1,4,128]{3,2,1,0:T(4,128)S(1)} all-to-all(f32[16,1,4,128]{3,2,1,0:T(4,128)S(1)} %bitcast.38), channel_id=1, replica_groups=mesh['xa'=4,'xb'=2,'y'=8,'z'=8,'core'=2] {'z','core'}, dimensions={0} | all-to-all | bytes 65536 | tf_op jit(solution)/shard_map/all_to_all | solution.py:458
  65.7 15.3 %all_to_all.32 = f32[64,1,4,128]{3,2,1,0:T(4,128)S(1)} all-to-all(f32[64,1,4,128]{3,2,1,0:T(4,128)S(1)} %bitcast.33), channel_id=1, replica_groups=mesh['xa'=4,'xb'=2,'y'=8,'z'=8,'core'=2] {'xa','xb','y'}, dimensions={0} | all-to-all | bytes 262144 | tf_op jit(solution)/shard_map/all_to_all | solution.py:458
  81.0 2.0 %apply_second.1 = (f32[160,128]{1,0:T(8,128)S(1)}, f32[144,128]{1,0:T(8,128)S(1)}) custom-call(f32[256,128]{1,0:T(8,128)S(1)} %bitcast.29, f32[144,128]{1,0:T(8,128)S(1)} %get-tuple-element.19.start, f32[180,128]{1,0:T(8,128)S(1)} %get-tuple-element.12.own, f32[18,4096]{1,0:T(8,128)S(1)} %bitcast.28, f32[48,512]{1,0:T(8,128)S(1)} %get-tuple-element.13.folded, ...), custom_call_target="tpu_custom_call" | custom-call | tf_op jit(solution)/shard_map/apply_second/pallas_call | solution.py:443
  82.9 12.9 %all_to_all.33 = f32[32,5,1,128]{3,2,1,0:T(1,128)S(1)} all-to-all(f32[32,5,1,128]{3,2,1,0:T(1,128)S(1)} %bitcast.42), channel_id=1, replica_groups=mesh['xa'=4,'xb'=2,'y'=8,'z'=8,'core'=2] {'xb','y','core'}, dimensions={0} | all-to-all | bytes 163840 | tf_op jit(solution)/shard_map/all_to_all | solution.py:458
  95.8 0.1 own_block.1
  95.9 14.2 %all_to_all.34 = f32[32,3,1,128]{3,2,1,0:T(1,128)S(1)} all-to-all(f32[32,3,1,128]{3,2,1,0:T(1,128)S(1)} %bitcast.36), channel_id=1, replica_groups=mesh['xa'=4,'xb'=2,'y'=8,'z'=8,'core'=2] {'xa','z'}, dimensions={0} | all-to-all | bytes 98304 | tf_op jit(solution)/shard_map/all_to_all | solution.py:458
  110.1 9.9 %all_to_all.35 = f32[16,3,1,128]{3,2,1,0:T(1,128)S(1)} all-to-all(f32[16,3,1,128]{3,2,1,0:T(1,128)S(1)} %bitcast.41), channel_id=1, replica_groups=mesh['xa'=4,'xb'=2,'y'=8,'z'=8,'core'=2] {'xb','y'}, dimensions={0} | all-to-all | bytes 49152 | tf_op jit(solution)/shard_map/all_to_all | solution.py:458
  120.1 0.7 finish.1
  (20 shorter events, 0.1 us)
Async XLA Ops:
  0.6 21.2 %copy-start.6 = (f32[1,6,4096]{2,0,1:T(1,128)S(1)}, f32[1,6,4096]{2,0,1:T(1,128)}, u32[]{:S(2)}) copy-start(f32[1,6,4096]{2,0,1:T(1,128)} %param.14) | copy-start | bytes 294916
  0.6 21.2 %copy-start.5 = (f32[1,18,4096]{2,0,1:T(1,128)S(1)}, f32[1,18,4096]{2,0,1:T(1,128)}, u32[]{:S(2)}) copy-start(f32[1,18,4096]{2,0,1:T(1,128)} %param.13) | copy-start | bytes 884740
  1.5 21.9 %collective-permute-start.2 = (f32[9,4,128]{2,1,0:T(4,128)S(1)}, f32[9,4,128]{2,1,0:T(4,128)S(1)}, u32[]{:S(2)}, u32[]{:S(2)}) collective-permute-start(f32[9,4,128]{2,1,0:T(4,128)S(1)} %mul.12.mine), channel_id=1, source_target_pairs={{0,8},{1,9},{2,10},{3,11},{4,12},{5,13},{6,14},{7,15},{8,0},{9,1},... | collective-permute-start | bytes 55304 | tf_op jit(solution)/shard_map/ppermute | solution.py:476
  16.6 6.8 %collective-permute-start.1 = (f32[9,4,128]{2,1,0:T(4,128)S(1)}, f32[9,4,128]{2,1,0:T(4,128)S(1)}, u32[]{:S(2)}, u32[]{:S(2)}) collective-permute-start(f32[9,4,128]{2,1,0:T(4,128)S(1)} %mul.12.mine), channel_id=1, source_target_pairs={{0,1},{1,2},{2,3},{3,4},{4,5},{5,6},{6,7},{7,8},{8,9},{9,10},{10,1... | collective-permute-start | bytes 55304 | tf_op jit(solution)/shard_map/ppermute | solution.py:476
  19.6 3.8 %collective-permute-start = (f32[9,4,128]{2,1,0:T(4,128)S(1)}, f32[9,4,128]{2,1,0:T(4,128)S(1)}, u32[]{:S(2)}, u32[]{:S(2)}) collective-permute-start(f32[9,4,128]{2,1,0:T(4,128)S(1)} %mul.12.mine), channel_id=1, source_target_pairs={{0,15},{1,0},{2,1},{3,2},{4,3},{5,4},{6,5},{7,6},{8,7},{9,8},{10,9... | collective-permute-start | bytes 55304 | tf_op jit(solution)/shard_map/ppermute | solution.py:476
  21.9 0.8 copy-start
  21.9 0.8 copy-start.1
  21.9 0.8 copy-start.2
  21.9 0.8 copy-start.3
  21.9 0.8 copy-start.4

commit v9 on v8

--- a/solution.py
+++ b/solution.py
@@ -15,6 +15,9 @@
 QUARTER = 32
 PAIR = 5
 OWN = 3
+TRIPLE = 7
+WIDE = 10
+FIRST_SCALARS = 96
 SCALARS = 64
 F32, BF16 = jnp.float32, jnp.bfloat16
 VMEM = pl.BlockSpec(memory_space=pltpu.VMEM)
@@ -209,53 +212,14 @@
             own[place, :] = value[:, lanes]
 
 
-def send_scalars(send, data_rows, rows):
-    rest = send.shape[0] - data_rows
-    send[data_rows:, :] = jnp.zeros((rest, LANES), F32)
-    for index, row in enumerate(rows):
-        at = data_rows + index * BLOCKS
-        send[at : at + 1, :] = row
-
-
-def scalar(ref, row):
-    return jnp.sum(ref[row : row + 1, :], axis=1, keepdims=True)
-
-
-def first_kernel(share, mine, after, before, across, keep, own, jac_cam, folded, lane, slot,
-                 masks, inverse, send, start, hot, error):
-    params, tiles, _ = mine.shape
-    for block, ref in enumerate((mine, after, before, across)):
-        for t in range(tiles):
-            place = pl.ds(t * BLOCKS + block, params, stride=tiles * BLOCKS)
-            kept = keep[block : block + 1, t * LANES : (t + 1) * LANES]
-            start[place, :] = ref[:, t, :] * kept
-    energy = schur(start[...], send, jac_cam, folded, lane, slot, masks, inverse, hot, error)
-    vector = start[pl.ds(0, params * tiles, stride=BLOCKS), :]
-    energy = energy + share * lane_sums(own_part(own, DAMPING) * vector * vector)
-    gamma = share * lane_sums(own_part(own, RIGHT) * vector)
-    send_scalars(send, start.shape[0], (energy, gamma))
-
-
 def lane_ids(rows=1):
     return lax.broadcasted_iota(jnp.int32, (rows, LANES), 1)
 
 
-def second_kernel(share, received, start, own, jac_cam, folded, lane, slot, masks, inverse,
-                  send, step, sums, hot, error):
-    data_rows = start.shape[0]
-    per = data_rows // BLOCKS
-    alpha = scalar(received, data_rows + BLOCKS) / scalar(received, data_rows)
-    step[...] = start[...] - alpha * received[0:data_rows, :]
-    energy = schur(step[...], sums, jac_cam, folded, lane, slot, masks, inverse, hot, error)
-    vector = step[pl.ds(0, per, stride=BLOCKS), :]
-    change = received[pl.ds(0, per, stride=BLOCKS), :]
-    residual = own_part(own, UNWEIGH) * vector
-    energy = energy + share * lane_sums(own_part(own, DAMPING) * vector * vector)
-    fresh = share * lane_sums(residual * vector)
-    cross = share * lane_sums(residual * change)
+def send_pairs(sums, scalars, send):
     ids = lane_ids()
     extra = jnp.zeros((1, LANES), F32)
-    for index, row in enumerate((energy, fresh, cross)):
+    for index, row in enumerate(scalars):
         extra = jnp.where(ids == SCALARS + index, jnp.sum(row, axis=1, keepdims=True), extra)
     odd = lax.axis_index("core") == 1
     for chunk in range(16):
@@ -277,28 +241,79 @@
         send[base + PAIR : base + 2 * PAIR, :] = jnp.where(odd, same, other)
 
 
-def own_block_kernel(received, send):
-    evens = received[0:PAIR, :]
-    odds = received[PAIR : 2 * PAIR, :]
-    for source in range(2, received.shape[0] // PAIR, 2):
-        evens = evens + received[source * PAIR : (source + 1) * PAIR, :]
-        odds = odds + received[(source + 1) * PAIR : (source + 2) * PAIR, :]
+def scalar(row, lane):
+    return jnp.sum(jnp.where(lane_ids() == lane, row, 0.0), axis=1, keepdims=True)
+
+
+def first_kernel(share, mine, after, before, across, keep, own, jac_cam, folded, lane, slot,
+                 masks, inverse, send, start, sums, hot, error):
+    params, tiles, _ = mine.shape
+    for block, ref in enumerate((mine, after, before, across)):
+        for t in range(tiles):
+            place = pl.ds(t * BLOCKS + block, params, stride=tiles * BLOCKS)
+            kept = keep[block : block + 1, t * LANES : (t + 1) * LANES]
+            start[place, :] = ref[:, t, :] * kept
+    energy = schur(start[...], sums, jac_cam, folded, lane, slot, masks, inverse, hot, error)
+    vector = start[pl.ds(0, params * tiles, stride=BLOCKS), :]
+    energy = energy + share * lane_sums(own_part(own, DAMPING) * vector * vector)
+    gamma = share * lane_sums(own_part(own, RIGHT) * vector)
+    send_pairs(sums, (energy, gamma), send)
+
+
+def unpack(received, change):
     odd = lax.axis_index("core") == 1
     ids = lane_ids()
-    scalars = evens[PAIR - 1 : PAIR] + odds[PAIR - 1 : PAIR]
-    same = jnp.where(odd, odds, evens)
-    other = jnp.where(odd, evens, odds)
-
-    def block(value, which):
-        third = value[PAIR - 1 : PAIR]
-        if which:
-            third = pltpu.roll(third, LANES - QUARTER, 1)
-        return jnp.concatenate([value[2 * which : 2 * which + 2], third], axis=0)
-
-    other_first, other_second = block(other, 0), block(other, 1)
-    own = block(same, 0) + jnp.where(odd, other_first, other_second)
-    beside = jnp.where(odd, other_second, other_first)
-    across = block(same, 1)
+    for q in range(4):
+        thirds = [jnp.zeros((1, LANES), F32)] * BLOCKS
+        for i in range(4):
+            chunk = 4 * q + i
+            even = received[2 * chunk * TRIPLE : (2 * chunk + 1) * TRIPLE, :]
+            odds = received[(2 * chunk + 1) * TRIPLE : (2 * chunk + 2) * TRIPLE, :]
+            same, other = jnp.where(odd, odds, even), jnp.where(odd, even, odds)
+            near = jnp.where(odd, other[2:4], other[0:2])
+            far = jnp.where(odd, other[0:2], other[2:4])
+            rows = []
+            for r in range(2):
+                rows += [same[r : r + 1], near[r : r + 1], far[r : r + 1], same[4 + r : 5 + r]]
+            change[chunk * 8 : (chunk + 1) * 8, :] = jnp.concatenate(rows, axis=0)
+
+            def moved(row, quarter):
+                by = (QUARTER * (i - quarter)) % LANES
+                return pltpu.roll(row, by, 1) if by else row
+
+            first, second = moved(other[6:7], 0), moved(other[6:7], 1)
+            pieces = (
+                moved(same[6:7], 0),
+                jnp.where(odd, second, first),
+                jnp.where(odd, first, second),
+                moved(same[6:7], 2),
+            )
+            thirds = [jnp.where(ids >= QUARTER * i, p, t) for p, t in zip(pieces, thirds)]
+        at = (32 + q) * BLOCKS
+        change[at : at + BLOCKS, :] = jnp.concatenate(thirds, axis=0)
+
+
+def second_kernel(share, received, start, own, jac_cam, folded, lane, slot, masks, inverse,
+                  send, step, change_ref, sums, hot, error):
+    per = start.shape[0] // BLOCKS
+    unpack(received, change_ref)
+    scalars = received[TRIPLE - 1 : TRIPLE, :]
+    alpha = scalar(scalars, FIRST_SCALARS + 1) / scalar(scalars, FIRST_SCALARS)
+    step[...] = start[...] - alpha * change_ref[...]
+    energy = schur(step[...], sums, jac_cam, folded, lane, slot, masks, inverse, hot, error)
+    vector = step[pl.ds(0, per, stride=BLOCKS), :]
+    change = change_ref[pl.ds(0, per, stride=BLOCKS), :]
+    residual = own_part(own, UNWEIGH) * vector
+    energy = energy + share * lane_sums(own_part(own, DAMPING) * vector * vector)
+    fresh = share * lane_sums(residual * vector)
+    cross = share * lane_sums(residual * change)
+    send_pairs(sums, (energy, fresh, cross), send)
+
+
+def own_block_kernel(received, send):
+    same, other = core_sums(received)
+    own, beside, across = three_blocks(same, other)
+    scalars = same[PAIR - 1 : PAIR] + other[PAIR - 1 : PAIR]
     is_third = lax.broadcasted_iota(jnp.int32, (OWN, LANES), 0) == OWN - 1
     is_rest = jnp.logical_and(is_third, lane_ids(OWN) >= SCALARS)
 
@@ -326,11 +341,10 @@
         send[spot * OWN : (spot + 1) * OWN, :] = total
 
 
-def last_kernel(first, second, start, step, own, solution, residual, sums):
+def last_kernel(first, second, start, step, change_ref, own, solution, residual, sums):
     params, width = solution.shape
     tiles = width // LANES
     per = params * tiles
-    data_rows = per * BLOCKS
     ids = lane_ids()
     for chunk in range(16):
         sums[2 * chunk : 2 * chunk + 2, :] = second[chunk * OWN : chunk * OWN + 2, :]
@@ -343,17 +357,16 @@
             third = jnp.where(ids >= QUARTER * i, row, third)
         sums[32 + q : 33 + q, :] = third
 
-    curve, gamma = scalar(first, data_rows), scalar(first, data_rows + BLOCKS)
-    mixed = second[OWN - 1 : OWN, :]
-    energy, fresh, cross = (
-        jnp.sum(jnp.where(ids == SCALARS + i, mixed, 0.0), axis=1, keepdims=True) for i in range(3)
-    )
+    row = first[TRIPLE - 1 : TRIPLE, :]
+    curve, gamma = scalar(row, FIRST_SCALARS), scalar(row, FIRST_SCALARS + 1)
+    row = second[OWN - 1 : OWN, :]
+    energy, fresh, cross = (scalar(row, SCALARS + i) for i in range(3))
     alpha = gamma / curve
     beta = fresh / gamma
     alpha_next = fresh / (energy + 2.0 * beta * cross + beta * beta * curve)
     for t in range(tiles):
         spread = pl.ds(t * BLOCKS, params, stride=tiles * BLOCKS)
-        begin, vector, change = start[spread, :], step[spread, :], first[spread, :]
+        begin, vector, change = start[spread, :], step[spread, :], change_ref[spread, :]
         terms = sums[pl.ds(t, params, stride=tiles), :]
         damping, unweigh = (
             own[pl.ds(which * per + t, params, stride=tiles), :] for which in (DAMPING, UNWEIGH)
@@ -366,76 +379,128 @@
         residual[:, lanes] = unweigh * vector - alpha_next * image
 
 
-def chunk_sum(received):
-    total = received[0:8, :]
-    for at in range(8, received.shape[0], 8):
-        total = total + received[at : at + 8, :]
-    return total[0:BLOCKS] + total[BLOCKS:]
+def core_sums(received):
+    evens = received[0:PAIR, :]
+    odds = received[PAIR : 2 * PAIR, :]
+    for source in range(2, received.shape[0] // PAIR, 2):
+        evens = evens + received[source * PAIR : (source + 1) * PAIR, :]
+        odds = odds + received[(source + 1) * PAIR : (source + 2) * PAIR, :]
+    odd = lax.axis_index("core") == 1
+    return jnp.where(odd, odds, evens), jnp.where(odd, evens, odds)
+
+
+def three_blocks(same, other):
+    odd = lax.axis_index("core") == 1
+
+    def block(value, which):
+        third = value[PAIR - 1 : PAIR]
+        if which:
+            third = pltpu.roll(third, LANES - QUARTER, 1)
+        return jnp.concatenate([value[2 * which : 2 * which + 2], third], axis=0)
+
+    first, second = block(other, 0), block(other, 1)
+    own = block(same, 0) + jnp.where(odd, first, second)
+    return own, jnp.where(odd, second, first), block(same, 1)
 
 
 def own_rows(own):
     per = own.shape[0] // 5
-    at = jnp.minimum(pts_index(), per - 1)
-    return [own[pl.ds(which * per + at, 1), :] for which in (WEIGHTS, PULL)]
+    chunk = lax.axis_index("xb") * lax.axis_size("y") + lax.axis_index("y")
+    found = []
+    for which in (WEIGHTS, PULL):
+        two = own[pl.ds(which * per + 2 * chunk, 2), :]
+        third = own[pl.ds(which * per + 32 + lax.div(chunk, 4), 1), :]
+        turned = third
+        for i in range(1, 4):
+            moved = pltpu.roll(third, LANES - QUARTER * i, 1)
+            turned = jnp.where(lax.rem(chunk, 4) == i, moved, turned)
+        found.append(jnp.concatenate([two, turned], axis=0))
+    return found
 
 
 def spread_kernel(received, own, send):
-    total = chunk_sum(received)
-    owners = send.shape[0] // BLOCKS
-    mine, after, before, across = (total[b : b + 1] for b in range(BLOCKS))
-    zero = jnp.zeros((1, LANES), F32)
-    rows = own_rows(own)
-    half = owners // 2
-    parts = {
-        0: (mine, after, before, across),
-        1: (after, mine, *rows),
-        -1: (before, mine, *rows),
-        half: (across, mine, *rows),
-        2: (after, zero, zero, zero),
-        -2: (before, zero, zero, zero),
-        half - 1: (across, before, zero, zero),
-        half + 1: (across, after, zero, zero),
-    }
-    is_sums = pts_index() < own.shape[0] // 5
-    twice = jnp.concatenate([total, total], axis=0)
-    for at in range(0, send.shape[0], 8):
-        send[at : at + 8, :] = jnp.where(is_sums, 0.0, twice)
-
-    @pl.when(is_sums)
-    def _():
-        for shift, value in parts.items():
-            spot = lax.rem(cam_index() + shift + owners, owners) * BLOCKS
-            send[pl.ds(spot, BLOCKS), :] = jnp.concatenate(value, axis=0)
+    same, other = core_sums(received)
+    mine, beside, across = three_blocks(same, other)
+    weights, pull = own_rows(own)
+    scalars = same[PAIR - 1 : PAIR] + other[PAIR - 1 : PAIR]
+    scalars = jnp.where(lane_ids() >= SCALARS, scalars, 0.0)
+    zero = jnp.zeros((OWN, LANES), F32)
+    ids = lane_ids()
+
+    def joined(*units):
+        units = units + (zero,) * (BLOCKS - len(units))
+        mixed = units[0][2:3]
+        for u in range(1, BLOCKS):
+            mixed = jnp.where(ids >= QUARTER * u, pltpu.roll(units[u][2:3], QUARTER * u, 1), mixed)
+        return jnp.concatenate([unit[0:2] for unit in units] + [mixed, scalars], axis=0)
+
+    size = lax.axis_size("z")
+    columns = send.shape[0] // (size * WIDE)
+    nothing = joined()
+    for spot in range(columns * size):
+        send[spot * WIDE : (spot + 1) * WIDE, :] = nothing
+    step = 1 - 2 * lax.axis_index("core")
+    half = size // 2
+    parts = (
+        (0, joined(mine, beside, across)),
+        (step, joined(beside)),
+        (half, joined(across, mine, weights, pull)),
+        (-step, joined(mine, zero, weights, pull)),
+        (half - step, joined(across)),
+        (half + step, joined(beside)),
+    )
+    for shift, value in parts:
+        place = lax.rem(lax.axis_index("z") + shift + size, size)
+        for x in range(columns):
+            send[pl.ds((x * size + place) * WIDE, WIDE), :] = value
 
 
 def combine_kernel(received, own, send):
-    owners = received.shape[0] // BLOCKS
-    half = owners // 2
-    me = cam_index()
-
-    def row(shift, at):
-        spot = lax.rem(me + shift + owners, owners) * BLOCKS + at
-        return received[pl.ds(spot, 1), :]
-
-    sums = (
-        (row(0, 0) + row(-1, 0)) + (row(1, 0) + row(half, 0)),
-        (row(1, 1) + row(0, 1)) + (row(2, 0) + row(half + 1, 0)),
-        (row(-1, 1) + row(-2, 0)) + (row(0, 2) + row(half - 1, 0)),
-        (row(half, 1) + row(half - 1, 1)) + (row(half + 1, 1) + row(0, 3)),
-    )
-    joined = []
-    for block, shift in enumerate((0, 1, -1, half)):
-        weights, pull = (row(shift, 2), row(shift, 3)) if block else own_rows(own)
-        joined.append(pull + weights * sums[block])
-    joined = jnp.concatenate(joined, axis=0)
-    total = received[0:8, :]
-    for at in range(8, received.shape[0], 8):
-        total = total + received[at : at + 8, :]
-    total = total[0:BLOCKS] + total[BLOCKS:]
-    joined = jnp.where(pts_index() < own.shape[0] // 5, joined, total)
-    joined = jnp.concatenate([joined, joined], axis=0)
-    for at in range(0, send.shape[0], 8):
-        send[at : at + 8, :] = joined
+    size = lax.axis_size("z")
+    columns = received.shape[0] // (size * WIDE)
+    step = 1 - 2 * lax.axis_index("core")
+    half = size // 2
+    ids = lane_ids()
+
+    def message(shift, x):
+        place = lax.rem(lax.axis_index("z") - shift + 2 * size, size)
+        return received[pl.ds((x * size + place) * WIDE, WIDE), :]
+
+    def summed(shift):
+        total = message(shift, 0)
+        for x in range(1, columns):
+            total = total + message(shift, x)
+        return total
+
+    def unit(value, which):
+        third = value[8:9]
+        if which:
+            third = pltpu.roll(third, LANES - QUARTER * which, 1)
+        return jnp.concatenate([value[2 * which : 2 * which + 2], third], axis=0)
+
+    here, over, back = summed(0), summed(half), summed(-step)
+    terms = (
+        unit(here, 0) + (unit(summed(step), 0) + unit(over, 0)),
+        unit(back, 0) + (unit(here, 1) + unit(summed(half - step), 0)),
+        unit(over, 1) + (unit(summed(half + step), 0) + unit(here, 2)),
+    )
+    rows = (
+        own_rows(own),
+        [unit(message(-step, 0), u) for u in (2, 3)],
+        [unit(message(half, 0), u) for u in (2, 3)],
+    )
+    changes = [pull + weights * term for (weights, pull), term in zip(rows, terms)]
+    scalars = received[WIDE - 1 : WIDE, :]
+    for source in range(1, received.shape[0] // WIDE):
+        scalars = scalars + received[(source + 1) * WIDE - 1 : (source + 1) * WIDE, :]
+    mixed = pltpu.roll(scalars, FIRST_SCALARS - SCALARS, 1)
+    for u in (2, 1, 0):
+        third = changes[u][2:3]
+        third = pltpu.roll(third, QUARTER * u, 1) if u else third
+        mixed = jnp.where(ids < QUARTER * (u + 1), third, mixed)
+    joined = jnp.concatenate([change[0:2] for change in changes] + [mixed], axis=0)
+    for spot in range(send.shape[0] // TRIPLE):
+        send[spot * TRIPLE : (spot + 1) * TRIPLE, :] = joined
 
 
 def call(kernel, outs, *args, scratch=(), name=None):
@@ -492,24 +557,25 @@
     fixed = (jac_cam, folded, lane, slot, masks, inverse)
     half = width // (2 * LANES)
     scratch = (pltpu.VMEM((half * LANES, count), BF16), pltpu.VMEM((2 * FOLDS, CHUNK), F32))
-    sums = jax.ShapeDtypeStruct((rows * BLOCKS, LANES), F32)
     vector = jax.ShapeDtypeStruct((per * BLOCKS, LANES), F32)
+    chunked = jax.ShapeDtypeStruct((lax.axis_size(near) * PAIR, LANES), F32)
+    scratch = (pltpu.VMEM(vector.shape, F32), *scratch)
 
     send, start = call(
-        functools.partial(first_kernel, share), [sums, vector],
+        functools.partial(first_kernel, share), [chunked, vector],
         mine, after, before, across, keep, own, *fixed, scratch=scratch, name="apply_first",
     )
-    chunks = swap(send, pts)
-    shape = jax.ShapeDtypeStruct((owners * BLOCKS, LANES), F32)
+    chunks = swap(send, near, 1)
+    shape = jax.ShapeDtypeStruct((lax.axis_size(wide) * WIDE, LANES), F32)
     chunks = call(spread_kernel, shape, chunks, own, name="spread")
-    chunks = swap(chunks, cam)
-    chunks = call(combine_kernel, sums, chunks, own, name="combine")
-    first = swap(chunks, pts)
-
-    chunked = jax.ShapeDtypeStruct((lax.axis_size(near) * PAIR, LANES), F32)
-    send, step = call(
-        functools.partial(second_kernel, share), [chunked, vector], first, start, own, *fixed,
-        scratch=(pltpu.VMEM(vector.shape, F32), *scratch), name="apply_second",
+    chunks = swap(chunks, wide, 1)
+    shape = jax.ShapeDtypeStruct((lax.axis_size(near) * TRIPLE, LANES), F32)
+    chunks = call(combine_kernel, shape, chunks, own, name="combine")
+    first = swap(chunks, near, 1)
+
+    send, step, change = call(
+        functools.partial(second_kernel, share), [chunked, vector, vector], first, start, own,
+        *fixed, scratch=scratch, name="apply_second",
     )
     chunks = swap(send, near, 1)
     shape = jax.ShapeDtypeStruct((lax.axis_size(wide) * OWN, LANES), F32)
@@ -521,7 +587,7 @@
     shape = jax.ShapeDtypeStruct((params, width), F32)
     return tuple(
         call(
-            last_kernel, [shape, shape], first, second, start, step, own,
+            last_kernel, [shape, shape], first, second, start, step, change, own,
             scratch=[pltpu.VMEM((per, LANES), F32)], name="finish",
         )
     )

time: 122 us -> 119 us (0.975)
  blocking collectives: 92.6 us -> 89.1 us
    all_to_all x6, blocking collectives: 92.6 us -> 89.1 us  [swap(): return lax.all_to_all(chunks, axes, 0, 0).reshape(value.shape)]
where the time goes in v9:
time: 119 us; the launch traced here: 118 us
  blocking collectives  89.1 us (75%)
  starting transfers between devices  18.1 us (15%)
  Pallas kernels  5.82 us (5%)
  other arithmetic  2.34 us (2%)
  local copies, waits for them, and re-layouts  1.55 us (1%)
    all_to_all x6, blocking collectives, swap(): return lax.all_to_all(chunks, axes, 0, 0).reshape(value.shape)  89.1 us
    ppermute x3, starting transfers between devices, on_device(): lax.ppermute(mine, cam, [(i, (i - d) % owners) for i in range(owners)])  18.1 us
    pallas_call x8, Pallas kernels, call(): pl.pallas_call(kernel, out_shape=outs, in_specs=[VMEM] * len(args), out_s...  5.82 us
  transfers between devices with their start and end apart: 3, of which 0 were waited for; matrix products, arithmetic and copies ran while one was open for 2% of the time, Pallas kernels for 1%

profile of v9, /device:TPU:1, one launch (start us, length us, event | category | flops | bytes accessed | tf_op | source)
XLA Modules:
  0.0 117.7 jit_solution(17627486417317062893)
XLA Ops:
  0.6 0.8 mul.11
  1.5 15.1 %collective-permute-start.2 = (f32[9,4,128]{2,1,0:T(4,128)S(1)}, f32[9,4,128]{2,1,0:T(4,128)S(1)}, u32[]{:S(2)}, u32[]{:S(2)}) collective-permute-start(f32[9,4,128]{2,1,0:T(4,128)S(1)} %mul.12.mine), channel_id=1, source_target_pairs={{0,8},{1,9},{2,10},{3,11},{4,12},{5,13},{6,14},{7,15},{8,0},{9,1},... | collective-permute-start | bytes 55304 | tf_op jit(solution)/shard_map/ppermute | solution.py:541
  16.6 3.0 %collective-permute-start.1 = (f32[9,4,128]{2,1,0:T(4,128)S(1)}, f32[9,4,128]{2,1,0:T(4,128)S(1)}, u32[]{:S(2)}, u32[]{:S(2)}) collective-permute-start(f32[9,4,128]{2,1,0:T(4,128)S(1)} %mul.12.mine), channel_id=1, source_target_pairs={{0,1},{1,2},{2,3},{3,4},{4,5},{5,6},{6,7},{7,8},{8,9},{9,10},{10,1... | collective-permute-start | bytes 55304 | tf_op jit(solution)/shard_map/ppermute | solution.py:541
  19.6 0.7 fusion
  20.2 0.1 iota_add_fusion
  20.3 0.8 compare_reduce_fusion
  21.1 0.7 copy.32
  21.8 0.1 copy.31
  21.9 0.2 copy.30
  22.1 0.5 copy-done
  22.6 0.0 copy-done.1
  22.7 0.7 invert.1
  23.4 2.0 %apply_first.1 = (f32[160,128]{1,0:T(8,128)S(1)}, f32[144,128]{1,0:T(8,128)S(1)}) custom-call(f32[9,4,128]{2,1,0:T(4,128)S(1)} %mul.12.mine, f32[9,4,128]{2,1,0:T(4,128)S(1)} %collective-permute-done.after, f32[9,4,128]{2,1,0:T(4,128)S(1)} %collective-permute-done.1.before, f32[9,4,128]{2,1,0:T(4,128)S(1)} %collective-permute-done.2.across, ...), custom_call_target="tpu_custom_call" | custom-call | tf_op jit(solution)/shard_map/apply_first/pallas_call | solution.py:508
  25.3 17.4 %all_to_all.30 = f32[32,5,1,128]{3,2,1,0:T(1,128)S(1)} all-to-all(f32[32,5,1,128]{3,2,1,0:T(1,128)S(1)} %bitcast.36), channel_id=1, replica_groups=mesh['xa'=4,'xb'=2,'y'=8,'z'=8,'core'=2] {'xb','y','core'}, dimensions={0} | all-to-all | bytes 163840 | tf_op jit(solution)/shard_map/all_to_all | solution.py:523
  42.7 0.2 spread.1
  42.9 21.8 %all_to_all.31 = f32[32,10,1,128]{3,2,1,0:T(1,128)S(1)} all-to-all(f32[32,10,1,128]{3,2,1,0:T(1,128)S(1)} %bitcast.25), channel_id=1, replica_groups=mesh['xa'=4,'xb'=2,'y'=8,'z'=8,'core'=2] {'xa','z'}, dimensions={0} | all-to-all | bytes 327680 | tf_op jit(solution)/shard_map/all_to_all | solution.py:523
  64.7 0.2 combine.1
  64.9 13.4 %all_to_all.32 = f32[32,7,1,128]{3,2,1,0:T(1,128)S(1)} all-to-all(f32[32,7,1,128]{3,2,1,0:T(1,128)S(1)} %bitcast.28), channel_id=1, replica_groups=mesh['xa'=4,'xb'=2,'y'=8,'z'=8,'core'=2] {'xb','y','core'}, dimensions={0} | all-to-all | bytes 229376 | tf_op jit(solution)/shard_map/all_to_all | solution.py:523
  78.3 2.0 %apply_second.1 = (f32[160,128]{1,0:T(8,128)S(1)}, f32[144,128]{1,0:T(8,128)S(1)}, f32[144,128]{1,0:T(8,128)S(1)}) custom-call(f32[224,128]{1,0:T(8,128)S(1)} %bitcast.23, f32[144,128]{1,0:T(8,128)S(1)} %get-tuple-element.20.start, f32[180,128]{1,0:T(8,128)S(1)} %get-tuple-element.13.own, f32[18,4096]{1,0:T(8,128)S(1)} %bitcast.22, ...), custom_call_target="tpu_custom_call" | custom-call | tf_op jit(solution)/shard_map/apply_second/pallas_call | solution.py:508
  80.3 12.1 %all_to_all.33 = f32[32,5,1,128]{3,2,1,0:T(1,128)S(1)} all-to-all(f32[32,5,1,128]{3,2,1,0:T(1,128)S(1)} %bitcast.35), channel_id=1, replica_groups=mesh['xa'=4,'xb'=2,'y'=8,'z'=8,'core'=2] {'xb','y','core'}, dimensions={0} | all-to-all | bytes 163840 | tf_op jit(solution)/shard_map/all_to_all | solution.py:523
  92.4 0.1 own_block.1
  92.4 14.5 %all_to_all.34 = f32[32,3,1,128]{3,2,1,0:T(1,128)S(1)} all-to-all(f32[32,3,1,128]{3,2,1,0:T(1,128)S(1)} %bitcast.32), channel_id=1, replica_groups=mesh['xa'=4,'xb'=2,'y'=8,'z'=8,'core'=2] {'xa','z'}, dimensions={0} | all-to-all | bytes 98304 | tf_op jit(solution)/shard_map/all_to_all | solution.py:523
  107.0 10.0 %all_to_all.35 = f32[16,3,1,128]{3,2,1,0:T(1,128)S(1)} all-to-all(f32[16,3,1,128]{3,2,1,0:T(1,128)S(1)} %bitcast.34), channel_id=1, replica_groups=mesh['xa'=4,'xb'=2,'y'=8,'z'=8,'core'=2] {'xb','y'}, dimensions={0} | all-to-all | bytes 49152 | tf_op jit(solution)/shard_map/all_to_all | solution.py:523
  116.9 0.7 finish.1
  (20 shorter events, 0.1 us)
Async XLA Ops:
  0.6 21.2 %copy-start.6 = (f32[1,6,4096]{2,0,1:T(1,128)S(1)}, f32[1,6,4096]{2,0,1:T(1,128)}, u32[]{:S(2)}) copy-start(f32[1,6,4096]{2,0,1:T(1,128)} %param.14) | copy-start | bytes 294916
  0.6 21.2 %copy-start.5 = (f32[1,18,4096]{2,0,1:T(1,128)S(1)}, f32[1,18,4096]{2,0,1:T(1,128)}, u32[]{:S(2)}) copy-start(f32[1,18,4096]{2,0,1:T(1,128)} %param.13) | copy-start | bytes 884740
  1.5 21.9 %collective-permute-start.2 = (f32[9,4,128]{2,1,0:T(4,128)S(1)}, f32[9,4,128]{2,1,0:T(4,128)S(1)}, u32[]{:S(2)}, u32[]{:S(2)}) collective-permute-start(f32[9,4,128]{2,1,0:T(4,128)S(1)} %mul.12.mine), channel_id=1, source_target_pairs={{0,8},{1,9},{2,10},{3,11},{4,12},{5,13},{6,14},{7,15},{8,0},{9,1},... | collective-permute-start | bytes 55304 | tf_op jit(solution)/shard_map/ppermute | solution.py:541
  16.6 6.8 %collective-permute-start.1 = (f32[9,4,128]{2,1,0:T(4,128)S(1)}, f32[9,4,128]{2,1,0:T(4,128)S(1)}, u32[]{:S(2)}, u32[]{:S(2)}) collective-permute-start(f32[9,4,128]{2,1,0:T(4,128)S(1)} %mul.12.mine), channel_id=1, source_target_pairs={{0,1},{1,2},{2,3},{3,4},{4,5},{5,6},{6,7},{7,8},{8,9},{9,10},{10,1... | collective-permute-start | bytes 55304 | tf_op jit(solution)/shard_map/ppermute | solution.py:541
  19.6 3.8 %collective-permute-start = (f32[9,4,128]{2,1,0:T(4,128)S(1)}, f32[9,4,128]{2,1,0:T(4,128)S(1)}, u32[]{:S(2)}, u32[]{:S(2)}) collective-permute-start(f32[9,4,128]{2,1,0:T(4,128)S(1)} %mul.12.mine), channel_id=1, source_target_pairs={{0,15},{1,0},{2,1},{3,2},{4,3},{5,4},{6,5},{7,6},{8,7},{9,8},{10,9... | collective-permute-start | bytes 55304 | tf_op jit(solution)/shard_map/ppermute | solution.py:541
  21.9 0.8 copy-start
  21.9 0.8 copy-start.1
  21.9 0.8 copy-start.2
  21.9 0.8 copy-start.3
  21.9 0.8 copy-start.4

commit v10 on v9

--- a/solution.py
+++ b/solution.py
@@ -16,7 +16,6 @@
 PAIR = 5
 OWN = 3
 TRIPLE = 7
-WIDE = 10
 FIRST_SCALARS = 96
 SCALARS = 64
 F32, BF16 = jnp.float32, jnp.bfloat16
@@ -423,48 +422,50 @@
     mine, beside, across = three_blocks(same, other)
     weights, pull = own_rows(own)
     scalars = same[PAIR - 1 : PAIR] + other[PAIR - 1 : PAIR]
-    scalars = jnp.where(lane_ids() >= SCALARS, scalars, 0.0)
+    scalars = pltpu.roll(scalars, FIRST_SCALARS - SCALARS, 1)
     zero = jnp.zeros((OWN, LANES), F32)
     ids = lane_ids()
+    size = lax.axis_size("z")
+    columns = send.shape[0] // (size * TRIPLE)
+    joint = pull * (1.0 / columns) + weights * mine
 
     def joined(*units):
-        units = units + (zero,) * (BLOCKS - len(units))
+        units = units + (zero,) * (3 - len(units))
         mixed = units[0][2:3]
-        for u in range(1, BLOCKS):
+        for u in (1, 2):
             mixed = jnp.where(ids >= QUARTER * u, pltpu.roll(units[u][2:3], QUARTER * u, 1), mixed)
-        return jnp.concatenate([unit[0:2] for unit in units] + [mixed, scalars], axis=0)
-
-    size = lax.axis_size("z")
-    columns = send.shape[0] // (size * WIDE)
+        mixed = jnp.where(ids >= FIRST_SCALARS, scalars, mixed)
+        return jnp.concatenate([unit[0:2] for unit in units] + [mixed], axis=0)
+
     nothing = joined()
     for spot in range(columns * size):
-        send[spot * WIDE : (spot + 1) * WIDE, :] = nothing
+        send[spot * TRIPLE : (spot + 1) * TRIPLE, :] = nothing
     step = 1 - 2 * lax.axis_index("core")
     half = size // 2
     parts = (
         (0, joined(mine, beside, across)),
         (step, joined(beside)),
-        (half, joined(across, mine, weights, pull)),
-        (-step, joined(mine, zero, weights, pull)),
+        (half, joined(across, joint, weights)),
+        (-step, joined(zero, joint, weights)),
         (half - step, joined(across)),
         (half + step, joined(beside)),
     )
     for shift, value in parts:
         place = lax.rem(lax.axis_index("z") + shift + size, size)
         for x in range(columns):
-            send[pl.ds((x * size + place) * WIDE, WIDE), :] = value
+            send[pl.ds((x * size + place) * TRIPLE, TRIPLE), :] = value
 
 
 def combine_kernel(received, own, send):
     size = lax.axis_size("z")
-    columns = received.shape[0] // (size * WIDE)
+    columns = received.shape[0] // (size * TRIPLE)
     step = 1 - 2 * lax.axis_index("core")
     half = size // 2
     ids = lane_ids()
 
     def message(shift, x):
         place = lax.rem(lax.axis_index("z") - shift + 2 * size, size)
-        return received[pl.ds((x * size + place) * WIDE, WIDE), :]
+        return received[pl.ds((x * size + place) * TRIPLE, TRIPLE), :]
 
     def summed(shift):
         total = message(shift, 0)
@@ -473,27 +474,23 @@
         return total
 
     def unit(value, which):
-        third = value[8:9]
+        third = value[6:7]
         if which:
             third = pltpu.roll(third, LANES - QUARTER * which, 1)
         return jnp.concatenate([value[2 * which : 2 * which + 2], third], axis=0)
 
     here, over, back = summed(0), summed(half), summed(-step)
-    terms = (
-        unit(here, 0) + (unit(summed(step), 0) + unit(over, 0)),
-        unit(back, 0) + (unit(here, 1) + unit(summed(half - step), 0)),
-        unit(over, 1) + (unit(summed(half + step), 0) + unit(here, 2)),
-    )
-    rows = (
-        own_rows(own),
-        [unit(message(-step, 0), u) for u in (2, 3)],
-        [unit(message(half, 0), u) for u in (2, 3)],
-    )
-    changes = [pull + weights * term for (weights, pull), term in zip(rows, terms)]
-    scalars = received[WIDE - 1 : WIDE, :]
-    for source in range(1, received.shape[0] // WIDE):
-        scalars = scalars + received[(source + 1) * WIDE - 1 : (source + 1) * WIDE, :]
-    mixed = pltpu.roll(scalars, FIRST_SCALARS - SCALARS, 1)
+    weights, pull = own_rows(own)
+    near_weights = unit(message(-step, 0), 2)
+    far_weights = unit(message(half, 0), 2)
+    changes = (
+        pull + weights * (unit(here, 0) + (unit(summed(step), 0) + unit(over, 0))),
+        unit(back, 1) + near_weights * (unit(here, 1) + unit(summed(half - step), 0)),
+        unit(over, 1) + far_weights * (unit(summed(half + step), 0) + unit(here, 2)),
+    )
+    mixed = received[TRIPLE - 1 : TRIPLE, :]
+    for source in range(1, received.shape[0] // TRIPLE):
+        mixed = mixed + received[(source + 1) * TRIPLE - 1 : (source + 1) * TRIPLE, :]
     for u in (2, 1, 0):
         third = changes[u][2:3]
         third = pltpu.roll(third, QUARTER * u, 1) if u else third
@@ -566,7 +563,7 @@
         mine, after, before, across, keep, own, *fixed, scratch=scratch, name="apply_first",
     )
     chunks = swap(send, near, 1)
-    shape = jax.ShapeDtypeStruct((lax.axis_size(wide) * WIDE, LANES), F32)
+    shape = jax.ShapeDtypeStruct((lax.axis_size(wide) * TRIPLE, LANES), F32)
     chunks = call(spread_kernel, shape, chunks, own, name="spread")
     chunks = swap(chunks, wide, 1)
     shape = jax.ShapeDtypeStruct((lax.axis_size(near) * TRIPLE, LANES), F32)

time: 119 us -> 118 us (level)
  no operation moved by 1% of the time
where the time goes in v10:
time: 118 us; the launch traced here: 117 us
  blocking collectives  88.3 us (75%)
  starting transfers between devices  18.1 us (15%)
  Pallas kernels  5.81 us (5%)
  other arithmetic  2.34 us (2%)
  local copies, waits for them, and re-layouts  1.55 us (1%)
    all_to_all x6, blocking collectives, swap(): return lax.all_to_all(chunks, axes, 0, 0).reshape(value.shape)  88.3 us
    ppermute x3, starting transfers between devices, on_device(): lax.ppermute(mine, cam, [(i, (i - d) % owners) for i in range(owners)])  18.1 us
    pallas_call x8, Pallas kernels, call(): pl.pallas_call(kernel, out_shape=outs, in_specs=[VMEM] * len(args), out_s...  5.81 us
  transfers between devices with their start and end apart: 3, of which 0 were waited for; matrix products, arithmetic and copies ran while one was open for 2% of the time, Pallas kernels for 1%

profile of v10, /device:TPU:1, one launch (start us, length us, event | category | flops | bytes accessed | tf_op | source)
XLA Modules:
  0.0 116.9 jit_solution(9513689552625342146)
XLA Ops:
  0.6 0.8 mul.11
  1.5 15.1 %collective-permute-start.2 = (f32[9,4,128]{2,1,0:T(4,128)S(1)}, f32[9,4,128]{2,1,0:T(4,128)S(1)}, u32[]{:S(2)}, u32[]{:S(2)}) collective-permute-start(f32[9,4,128]{2,1,0:T(4,128)S(1)} %mul.12.mine), channel_id=1, source_target_pairs={{0,8},{1,9},{2,10},{3,11},{4,12},{5,13},{6,14},{7,15},{8,0},{9,1},... | collective-permute-start | bytes 55304 | tf_op jit(solution)/shard_map/ppermute | solution.py:538
  16.6 3.0 %collective-permute-start.1 = (f32[9,4,128]{2,1,0:T(4,128)S(1)}, f32[9,4,128]{2,1,0:T(4,128)S(1)}, u32[]{:S(2)}, u32[]{:S(2)}) collective-permute-start(f32[9,4,128]{2,1,0:T(4,128)S(1)} %mul.12.mine), channel_id=1, source_target_pairs={{0,1},{1,2},{2,3},{3,4},{4,5},{5,6},{6,7},{7,8},{8,9},{9,10},{10,1... | collective-permute-start | bytes 55304 | tf_op jit(solution)/shard_map/ppermute | solution.py:538
  19.6 0.7 fusion
  20.2 0.1 iota_add_fusion
  20.3 0.8 compare_reduce_fusion
  21.1 0.7 copy.32
  21.8 0.1 copy.31
  21.9 0.2 copy.30
  22.1 0.5 copy-done
  22.6 0.0 copy-done.1
  22.7 0.7 invert.1
  23.4 2.0 %apply_first.1 = (f32[160,128]{1,0:T(8,128)S(1)}, f32[144,128]{1,0:T(8,128)S(1)}) custom-call(f32[9,4,128]{2,1,0:T(4,128)S(1)} %mul.12.mine, f32[9,4,128]{2,1,0:T(4,128)S(1)} %collective-permute-done.after, f32[9,4,128]{2,1,0:T(4,128)S(1)} %collective-permute-done.1.before, f32[9,4,128]{2,1,0:T(4,128)S(1)} %collective-permute-done.2.across, ...), custom_call_target="tpu_custom_call" | custom-call | tf_op jit(solution)/shard_map/apply_first/pallas_call | solution.py:505
  25.3 17.4 %all_to_all.30 = f32[32,5,1,128]{3,2,1,0:T(1,128)S(1)} all-to-all(f32[32,5,1,128]{3,2,1,0:T(1,128)S(1)} %bitcast.36), channel_id=1, replica_groups=mesh['xa'=4,'xb'=2,'y'=8,'z'=8,'core'=2] {'xb','y','core'}, dimensions={0} | all-to-all | bytes 163840 | tf_op jit(solution)/shard_map/all_to_all | solution.py:520
  42.7 0.2 spread.1
  42.9 21.7 %all_to_all.31 = f32[32,7,1,128]{3,2,1,0:T(1,128)S(1)} all-to-all(f32[32,7,1,128]{3,2,1,0:T(1,128)S(1)} %bitcast.26), channel_id=1, replica_groups=mesh['xa'=4,'xb'=2,'y'=8,'z'=8,'core'=2] {'xa','z'}, dimensions={0} | all-to-all | bytes 229376 | tf_op jit(solution)/shard_map/all_to_all | solution.py:520
  64.6 0.2 combine.1
  64.7 13.1 %all_to_all.32 = f32[32,7,1,128]{3,2,1,0:T(1,128)S(1)} all-to-all(f32[32,7,1,128]{3,2,1,0:T(1,128)S(1)} %bitcast.28), channel_id=1, replica_groups=mesh['xa'=4,'xb'=2,'y'=8,'z'=8,'core'=2] {'xb','y','core'}, dimensions={0} | all-to-all | bytes 229376 | tf_op jit(solution)/shard_map/all_to_all | solution.py:520
  77.8 2.0 %apply_second.1 = (f32[160,128]{1,0:T(8,128)S(1)}, f32[144,128]{1,0:T(8,128)S(1)}, f32[144,128]{1,0:T(8,128)S(1)}) custom-call(f32[224,128]{1,0:T(8,128)S(1)} %bitcast.23, f32[144,128]{1,0:T(8,128)S(1)} %get-tuple-element.20.start, f32[180,128]{1,0:T(8,128)S(1)} %get-tuple-element.13.own, f32[18,4096]{1,0:T(8,128)S(1)} %bitcast.22, ...), custom_call_target="tpu_custom_call" | custom-call | tf_op jit(solution)/shard_map/apply_second/pallas_call | solution.py:505
  79.8 12.0 %all_to_all.33 = f32[32,5,1,128]{3,2,1,0:T(1,128)S(1)} all-to-all(f32[32,5,1,128]{3,2,1,0:T(1,128)S(1)} %bitcast.35), channel_id=1, replica_groups=mesh['xa'=4,'xb'=2,'y'=8,'z'=8,'core'=2] {'xb','y','core'}, dimensions={0} | all-to-all | bytes 163840 | tf_op jit(solution)/shard_map/all_to_all | solution.py:520
  91.8 0.1 own_block.1
  91.9 14.2 %all_to_all.34 = f32[32,3,1,128]{3,2,1,0:T(1,128)S(1)} all-to-all(f32[32,3,1,128]{3,2,1,0:T(1,128)S(1)} %bitcast.32), channel_id=1, replica_groups=mesh['xa'=4,'xb'=2,'y'=8,'z'=8,'core'=2] {'xa','z'}, dimensions={0} | all-to-all | bytes 98304 | tf_op jit(solution)/shard_map/all_to_all | solution.py:520
  106.2 9.9 %all_to_all.35 = f32[16,3,1,128]{3,2,1,0:T(1,128)S(1)} all-to-all(f32[16,3,1,128]{3,2,1,0:T(1,128)S(1)} %bitcast.34), channel_id=1, replica_groups=mesh['xa'=4,'xb'=2,'y'=8,'z'=8,'core'=2] {'xb','y'}, dimensions={0} | all-to-all | bytes 49152 | tf_op jit(solution)/shard_map/all_to_all | solution.py:520
  116.1 0.7 finish.1
  (20 shorter events, 0.1 us)
Async XLA Ops:
  0.6 21.2 %copy-start.6 = (f32[1,6,4096]{2,0,1:T(1,128)S(1)}, f32[1,6,4096]{2,0,1:T(1,128)}, u32[]{:S(2)}) copy-start(f32[1,6,4096]{2,0,1:T(1,128)} %param.14) | copy-start | bytes 294916
  0.6 21.2 %copy-start.5 = (f32[1,18,4096]{2,0,1:T(1,128)S(1)}, f32[1,18,4096]{2,0,1:T(1,128)}, u32[]{:S(2)}) copy-start(f32[1,18,4096]{2,0,1:T(1,128)} %param.13) | copy-start | bytes 884740
  1.5 21.9 %collective-permute-start.2 = (f32[9,4,128]{2,1,0:T(4,128)S(1)}, f32[9,4,128]{2,1,0:T(4,128)S(1)}, u32[]{:S(2)}, u32[]{:S(2)}) collective-permute-start(f32[9,4,128]{2,1,0:T(4,128)S(1)} %mul.12.mine), channel_id=1, source_target_pairs={{0,8},{1,9},{2,10},{3,11},{4,12},{5,13},{6,14},{7,15},{8,0},{9,1},... | collective-permute-start | bytes 55304 | tf_op jit(solution)/shard_map/ppermute | solution.py:538
  16.6 6.8 %collective-permute-start.1 = (f32[9,4,128]{2,1,0:T(4,128)S(1)}, f32[9,4,128]{2,1,0:T(4,128)S(1)}, u32[]{:S(2)}, u32[]{:S(2)}) collective-permute-start(f32[9,4,128]{2,1,0:T(4,128)S(1)} %mul.12.mine), channel_id=1, source_target_pairs={{0,1},{1,2},{2,3},{3,4},{4,5},{5,6},{6,7},{7,8},{8,9},{9,10},{10,1... | collective-permute-start | bytes 55304 | tf_op jit(solution)/shard_map/ppermute | solution.py:538
  19.6 3.8 %collective-permute-start = (f32[9,4,128]{2,1,0:T(4,128)S(1)}, f32[9,4,128]{2,1,0:T(4,128)S(1)}, u32[]{:S(2)}, u32[]{:S(2)}) collective-permute-start(f32[9,4,128]{2,1,0:T(4,128)S(1)} %mul.12.mine), channel_id=1, source_target_pairs={{0,15},{1,0},{2,1},{3,2},{4,3},{5,4},{6,5},{7,6},{8,7},{9,8},{10,9... | collective-permute-start | bytes 55304 | tf_op jit(solution)/shard_map/ppermute | solution.py:538
  21.9 0.8 copy-start
  21.9 0.8 copy-start.1
  21.9 0.8 copy-start.2
  21.9 0.8 copy-start.3
  21.9 0.8 copy-start.4

commit v11 on v10

--- a/solution.py
+++ b/solution.py
@@ -9,7 +9,8 @@
 
 LANES = 128
 BLOCKS = 4
-STEPS = (1, 2, 4, 8)
+STAGES = ((1, 2, 3), (4, 8, 12))
+STEPS = STAGES[0] + STAGES[1]
 CHUNK = 512
 FOLDS = 8
 QUARTER = 32
@@ -62,9 +63,13 @@
 def point_totals(value, masks):
     before = value
     after = value
-    for i, step in enumerate(STEPS):
-        before = before + part(masks, i) * shifted(before, step)
-        after = after + part(masks, len(STEPS) + i) * shifted(after, -step)
+    index = 0
+    for stage in STAGES:
+        earlier, later = before, after
+        for step in stage:
+            before = before + part(masks, index) * shifted(earlier, step)
+            after = after + part(masks, len(STEPS) + index) * shifted(later, -step)
+            index += 1
     return before + (after - value)
 
 
@@ -266,26 +271,26 @@
         thirds = [jnp.zeros((1, LANES), F32)] * BLOCKS
         for i in range(4):
             chunk = 4 * q + i
-            even = received[2 * chunk * TRIPLE : (2 * chunk + 1) * TRIPLE, :]
-            odds = received[(2 * chunk + 1) * TRIPLE : (2 * chunk + 2) * TRIPLE, :]
+            even = received[2 * chunk * PAIR : (2 * chunk + 1) * PAIR, :]
+            odds = received[(2 * chunk + 1) * PAIR : (2 * chunk + 2) * PAIR, :]
             same, other = jnp.where(odd, odds, even), jnp.where(odd, even, odds)
             near = jnp.where(odd, other[2:4], other[0:2])
             far = jnp.where(odd, other[0:2], other[2:4])
             rows = []
             for r in range(2):
-                rows += [same[r : r + 1], near[r : r + 1], far[r : r + 1], same[4 + r : 5 + r]]
+                rows += [same[r : r + 1], near[r : r + 1], far[r : r + 1], same[2 + r : 3 + r]]
             change[chunk * 8 : (chunk + 1) * 8, :] = jnp.concatenate(rows, axis=0)
 
             def moved(row, quarter):
                 by = (QUARTER * (i - quarter)) % LANES
                 return pltpu.roll(row, by, 1) if by else row
 
-            first, second = moved(other[6:7], 0), moved(other[6:7], 1)
+            first, second = moved(other[4:5], 0), moved(other[4:5], 1)
             pieces = (
-                moved(same[6:7], 0),
+                moved(same[4:5], 0),
                 jnp.where(odd, second, first),
                 jnp.where(odd, first, second),
-                moved(same[6:7], 2),
+                moved(same[4:5], 1),
             )
             thirds = [jnp.where(ids >= QUARTER * i, p, t) for p, t in zip(pieces, thirds)]
         at = (32 + q) * BLOCKS
@@ -296,8 +301,8 @@
                   send, step, change_ref, sums, hot, error):
     per = start.shape[0] // BLOCKS
     unpack(received, change_ref)
-    scalars = received[TRIPLE - 1 : TRIPLE, :]
-    alpha = scalar(scalars, FIRST_SCALARS + 1) / scalar(scalars, FIRST_SCALARS)
+    scalars = received[PAIR - 1 : PAIR, :]
+    alpha = scalar(scalars, SCALARS + 1) / scalar(scalars, SCALARS)
     step[...] = start[...] - alpha * change_ref[...]
     energy = schur(step[...], sums, jac_cam, folded, lane, slot, masks, inverse, hot, error)
     vector = step[pl.ds(0, per, stride=BLOCKS), :]
@@ -356,8 +361,8 @@
             third = jnp.where(ids >= QUARTER * i, row, third)
         sums[32 + q : 33 + q, :] = third
 
-    row = first[TRIPLE - 1 : TRIPLE, :]
-    curve, gamma = scalar(row, FIRST_SCALARS), scalar(row, FIRST_SCALARS + 1)
+    row = first[PAIR - 1 : PAIR, :]
+    curve, gamma = scalar(row, SCALARS), scalar(row, SCALARS + 1)
     row = second[OWN - 1 : OWN, :]
     energy, fresh, cross = (scalar(row, SCALARS + i) for i in range(3))
     alpha = gamma / curve
@@ -491,13 +496,19 @@
     mixed = received[TRIPLE - 1 : TRIPLE, :]
     for source in range(1, received.shape[0] // TRIPLE):
         mixed = mixed + received[(source + 1) * TRIPLE - 1 : (source + 1) * TRIPLE, :]
-    for u in (2, 1, 0):
-        third = changes[u][2:3]
-        third = pltpu.roll(third, QUARTER * u, 1) if u else third
-        mixed = jnp.where(ids < QUARTER * (u + 1), third, mixed)
-    joined = jnp.concatenate([change[0:2] for change in changes] + [mixed], axis=0)
-    for spot in range(send.shape[0] // TRIPLE):
-        send[spot * TRIPLE : (spot + 1) * TRIPLE, :] = joined
+    mixed = pltpu.roll(mixed, LANES + SCALARS - FIRST_SCALARS, 1)
+
+    def two(first, second):
+        row = jnp.where(ids < SCALARS, pltpu.roll(second[2:3], QUARTER, 1), mixed)
+        row = jnp.where(ids < QUARTER, first[2:3], row)
+        return jnp.concatenate([first[0:2], second[0:2], row], axis=0)
+
+    same, other = two(changes[0], changes[2]), two(changes[0], changes[1])
+    odd = lax.axis_index("core") == 1
+    to_even, to_odd = jnp.where(odd, other, same), jnp.where(odd, same, other)
+    for spot in range(0, send.shape[0] // PAIR, 2):
+        send[spot * PAIR : (spot + 1) * PAIR, :] = to_even
+        send[(spot + 1) * PAIR : (spot + 2) * PAIR, :] = to_odd
 
 
 def call(kernel, outs, *args, scratch=(), name=None):
@@ -543,7 +554,7 @@
     keep = 1.0 - jnp.any(anchors[:, None, None] == ids[None], axis=0).astype(F32)
     folds = [
         jax.ShapeDtypeStruct((count_of * FOLDS, CHUNK), kind)
-        for count_of, kind in ((6, F32), (8, F32), (6, F32), (1, jnp.int32), (1, jnp.int32))
+        for count_of, kind in ((6, F32), (2 * len(STEPS), F32), (6, F32), (1, jnp.int32), (1, jnp.int32))
     ]
     inverse, masks, folded, lane, slot, own = call(
         functools.partial(setup_kernel, owners),
@@ -566,8 +577,7 @@
     shape = jax.ShapeDtypeStruct((lax.axis_size(wide) * TRIPLE, LANES), F32)
     chunks = call(spread_kernel, shape, chunks, own, name="spread")
     chunks = swap(chunks, wide, 1)
-    shape = jax.ShapeDtypeStruct((lax.axis_size(near) * TRIPLE, LANES), F32)
-    chunks = call(combine_kernel, shape, chunks, own, name="combine")
+    chunks = call(combine_kernel, chunked, chunks, own, name="combine")
     first = swap(chunks, near, 1)
 
     send, step, change = call(

time: 118 us -> 118 us (level)
  no operation moved by 1% of the time
where the time goes in v11:
time: 118 us; the launch traced here: 116 us
  blocking collectives  87.8 us (74%)
  starting transfers between devices  18.1 us (15%)
  Pallas kernels  5.84 us (5%)
  other arithmetic  2.34 us (2%)
  local copies, waits for them, and re-layouts  1.55 us (1%)
    all_to_all x6, blocking collectives, swap(): return lax.all_to_all(chunks, axes, 0, 0).reshape(value.shape)  87.8 us
    ppermute x3, starting transfers between devices, on_device(): lax.ppermute(mine, cam, [(i, (i - d) % owners) for i in range(owners)])  18.1 us
    pallas_call x8, Pallas kernels, call(): pl.pallas_call(kernel, out_shape=outs, in_specs=[VMEM] * len(args), out_s...  5.84 us
  transfers between devices with their start and end apart: 3, of which 0 were waited for; matrix products, arithmetic and copies ran while one was open for 2% of the time, Pallas kernels for 1%

profile of v11, /device:TPU:1, one launch (start us, length us, event | category | flops | bytes accessed | tf_op | source)
XLA Modules:
  0.0 116.4 jit_solution(16216497869425199770)
XLA Ops:
  0.6 0.8 mul.11
  1.5 15.1 %collective-permute-start.2 = (f32[9,4,128]{2,1,0:T(4,128)S(1)}, f32[9,4,128]{2,1,0:T(4,128)S(1)}, u32[]{:S(2)}, u32[]{:S(2)}) collective-permute-start(f32[9,4,128]{2,1,0:T(4,128)S(1)} %mul.12.mine), channel_id=1, source_target_pairs={{0,8},{1,9},{2,10},{3,11},{4,12},{5,13},{6,14},{7,15},{8,0},{9,1},... | collective-permute-start | bytes 55304 | tf_op jit(solution)/shard_map/ppermute | solution.py:549
  16.6 3.0 %collective-permute-start.1 = (f32[9,4,128]{2,1,0:T(4,128)S(1)}, f32[9,4,128]{2,1,0:T(4,128)S(1)}, u32[]{:S(2)}, u32[]{:S(2)}) collective-permute-start(f32[9,4,128]{2,1,0:T(4,128)S(1)} %mul.12.mine), channel_id=1, source_target_pairs={{0,1},{1,2},{2,3},{3,4},{4,5},{5,6},{6,7},{7,8},{8,9},{9,10},{10,1... | collective-permute-start | bytes 55304 | tf_op jit(solution)/shard_map/ppermute | solution.py:549
  19.6 0.7 fusion
  20.2 0.1 iota_add_fusion
  20.3 0.8 compare_reduce_fusion
  21.1 0.7 copy.32
  21.8 0.1 copy.31
  21.9 0.2 copy.30
  22.1 0.5 copy-done
  22.6 0.0 copy-done.1
  22.7 0.8 invert.1
  23.6 1.9 %apply_first.1 = (f32[160,128]{1,0:T(8,128)S(1)}, f32[144,128]{1,0:T(8,128)S(1)}) custom-call(f32[9,4,128]{2,1,0:T(4,128)S(1)} %mul.12.mine, f32[9,4,128]{2,1,0:T(4,128)S(1)} %collective-permute-done.after, f32[9,4,128]{2,1,0:T(4,128)S(1)} %collective-permute-done.1.before, f32[9,4,128]{2,1,0:T(4,128)S(1)} %collective-permute-done.2.across, ...), custom_call_target="tpu_custom_call" | custom-call | tf_op jit(solution)/shard_map/apply_first/pallas_call | solution.py:516
  25.4 17.4 %all_to_all.30 = f32[32,5,1,128]{3,2,1,0:T(1,128)S(1)} all-to-all(f32[32,5,1,128]{3,2,1,0:T(1,128)S(1)} %bitcast.36), channel_id=1, replica_groups=mesh['xa'=4,'xb'=2,'y'=8,'z'=8,'core'=2] {'xb','y','core'}, dimensions={0} | all-to-all | bytes 163840 | tf_op jit(solution)/shard_map/all_to_all | solution.py:531
  42.8 0.2 spread.1
  43.0 21.7 %all_to_all.31 = f32[32,7,1,128]{3,2,1,0:T(1,128)S(1)} all-to-all(f32[32,7,1,128]{3,2,1,0:T(1,128)S(1)} %bitcast.26), channel_id=1, replica_groups=mesh['xa'=4,'xb'=2,'y'=8,'z'=8,'core'=2] {'xa','z'}, dimensions={0} | all-to-all | bytes 229376 | tf_op jit(solution)/shard_map/all_to_all | solution.py:531
  64.7 0.2 combine.1
  64.8 12.9 %all_to_all.32 = f32[32,5,1,128]{3,2,1,0:T(1,128)S(1)} all-to-all(f32[32,5,1,128]{3,2,1,0:T(1,128)S(1)} %bitcast.30), channel_id=1, replica_groups=mesh['xa'=4,'xb'=2,'y'=8,'z'=8,'core'=2] {'xb','y','core'}, dimensions={0} | all-to-all | bytes 163840 | tf_op jit(solution)/shard_map/all_to_all | solution.py:531
  77.8 1.9 %apply_second.1 = (f32[160,128]{1,0:T(8,128)S(1)}, f32[144,128]{1,0:T(8,128)S(1)}, f32[144,128]{1,0:T(8,128)S(1)}) custom-call(f32[160,128]{1,0:T(8,128)S(1)} %bitcast.23, f32[144,128]{1,0:T(8,128)S(1)} %get-tuple-element.20.start, f32[180,128]{1,0:T(8,128)S(1)} %get-tuple-element.13.own, f32[18,4096]{1,0:T(8,128)S(1)} %bitcast.22, ...), custom_call_target="tpu_custom_call" | custom-call | tf_op jit(solution)/shard_map/apply_second/pallas_call | solution.py:516
  79.7 11.7 %all_to_all.33 = f32[32,5,1,128]{3,2,1,0:T(1,128)S(1)} all-to-all(f32[32,5,1,128]{3,2,1,0:T(1,128)S(1)} %bitcast.35), channel_id=1, replica_groups=mesh['xa'=4,'xb'=2,'y'=8,'z'=8,'core'=2] {'xb','y','core'}, dimensions={0} | all-to-all | bytes 163840 | tf_op jit(solution)/shard_map/all_to_all | solution.py:531
  91.3 0.1 own_block.1
  91.4 14.2 %all_to_all.34 = f32[32,3,1,128]{3,2,1,0:T(1,128)S(1)} all-to-all(f32[32,3,1,128]{3,2,1,0:T(1,128)S(1)} %bitcast.32), channel_id=1, replica_groups=mesh['xa'=4,'xb'=2,'y'=8,'z'=8,'core'=2] {'xa','z'}, dimensions={0} | all-to-all | bytes 98304 | tf_op jit(solution)/shard_map/all_to_all | solution.py:531
  105.7 10.0 %all_to_all.35 = f32[16,3,1,128]{3,2,1,0:T(1,128)S(1)} all-to-all(f32[16,3,1,128]{3,2,1,0:T(1,128)S(1)} %bitcast.34), channel_id=1, replica_groups=mesh['xa'=4,'xb'=2,'y'=8,'z'=8,'core'=2] {'xb','y'}, dimensions={0} | all-to-all | bytes 49152 | tf_op jit(solution)/shard_map/all_to_all | solution.py:531
  115.7 0.7 finish.1
  (20 shorter events, 0.1 us)
Async XLA Ops:
  0.6 21.2 %copy-start.6 = (f32[1,6,4096]{2,0,1:T(1,128)S(1)}, f32[1,6,4096]{2,0,1:T(1,128)}, u32[]{:S(2)}) copy-start(f32[1,6,4096]{2,0,1:T(1,128)} %param.14) | copy-start | bytes 294916
  0.6 21.2 %copy-start.5 = (f32[1,18,4096]{2,0,1:T(1,128)S(1)}, f32[1,18,4096]{2,0,1:T(1,128)}, u32[]{:S(2)}) copy-start(f32[1,18,4096]{2,0,1:T(1,128)} %param.13) | copy-start | bytes 884740
  1.5 22.0 %collective-permute-start.2 = (f32[9,4,128]{2,1,0:T(4,128)S(1)}, f32[9,4,128]{2,1,0:T(4,128)S(1)}, u32[]{:S(2)}, u32[]{:S(2)}) collective-permute-start(f32[9,4,128]{2,1,0:T(4,128)S(1)} %mul.12.mine), channel_id=1, source_target_pairs={{0,8},{1,9},{2,10},{3,11},{4,12},{5,13},{6,14},{7,15},{8,0},{9,1},... | collective-permute-start | bytes 55304 | tf_op jit(solution)/shard_map/ppermute | solution.py:549
  16.6 6.9 %collective-permute-start.1 = (f32[9,4,128]{2,1,0:T(4,128)S(1)}, f32[9,4,128]{2,1,0:T(4,128)S(1)}, u32[]{:S(2)}, u32[]{:S(2)}) collective-permute-start(f32[9,4,128]{2,1,0:T(4,128)S(1)} %mul.12.mine), channel_id=1, source_target_pairs={{0,1},{1,2},{2,3},{3,4},{4,5},{5,6},{6,7},{7,8},{8,9},{9,10},{10,1... | collective-permute-start | bytes 55304 | tf_op jit(solution)/shard_map/ppermute | solution.py:549
  19.6 4.0 %collective-permute-start = (f32[9,4,128]{2,1,0:T(4,128)S(1)}, f32[9,4,128]{2,1,0:T(4,128)S(1)}, u32[]{:S(2)}, u32[]{:S(2)}) collective-permute-start(f32[9,4,128]{2,1,0:T(4,128)S(1)} %mul.12.mine), channel_id=1, source_target_pairs={{0,15},{1,0},{2,1},{3,2},{4,3},{5,4},{6,5},{7,6},{8,7},{9,8},{10,9... | collective-permute-start | bytes 55304 | tf_op jit(solution)/shard_map/ppermute | solution.py:549
  21.9 0.8 copy-start
  21.9 0.8 copy-start.1
  21.9 0.8 copy-start.2
  21.9 0.8 copy-start.3
  21.9 0.8 copy-start.4

commit v12 on v11

--- a/solution.py
+++ b/solution.py
@@ -31,11 +31,6 @@
 
 def cam_index():
     return lax.axis_index("z") * 2 + lax.axis_index("core")
-
-
-def pts_index():
-    x = lax.axis_index("xa") * 2 + lax.axis_index("xb")
-    return x * lax.axis_size("y") + lax.axis_index("y")
 
 
 def short_one_hot(row, count):
@@ -409,7 +404,7 @@
 
 def own_rows(own):
     per = own.shape[0] // 5
-    chunk = lax.axis_index("xb") * lax.axis_size("y") + lax.axis_index("y")
+    chunk = lax.axis_index("x") * lax.axis_size("yb") + lax.axis_index("yb")
     found = []
     for which in (WEIGHTS, PULL):
         two = own[pl.ds(which * per + 2 * chunk, 2), :]
@@ -534,8 +529,8 @@
 def on_device(right_side, camera_damping, preconditioner, jac_cam, jac_pt, camera_index,
               point_index, point_damping, anchors):
     params, width = right_side.shape
-    pts, cam = ("xa", "xb", "y"), ("z", "core")
-    near, wide, last = ("xb", "y", "core"), ("xa", "z"), ("xb", "y")
+    pts, cam = ("x", "ya", "yb"), ("z", "core")
+    near, wide, last = ("x", "yb", "core"), ("ya", "z"), ("x", "yb")
     owners, rows = lax.axis_size(cam), lax.axis_size(pts)
     per = params * width // LANES
     count = camera_index.shape[1]
@@ -604,8 +599,8 @@
     cores = 2
     high = mesh.shape["cam"] // cores
     side = int(mesh.shape["pts"] ** 0.5)
-    grid = mesh.devices.reshape(side // 2, 2, mesh.shape["pts"] // side, high, cores)
-    cam, whole = ("z", "core"), ("xa", "xb", "y", "z", "core")
+    grid = mesh.devices.reshape(side, mesh.shape["pts"] // side // 2, 2, high, cores)
+    cam, whole = ("z", "core"), ("x", "ya", "yb", "z", "core")
     mesh = Mesh(grid, whole)
     return jax.shard_map(
         on_device,

time: 118 us -> 118 us (level)
  no operation moved by 1% of the time
where the time goes in v12:
time: 118 us; the launch traced here: 117 us
  blocking collectives  88.5 us (75%)
  starting transfers between devices  18.1 us (15%)
  Pallas kernels  5.82 us (5%)
  other arithmetic  2.34 us (2%)
  local copies, waits for them, and re-layouts  1.55 us (1%)
    all_to_all x6, blocking collectives, swap(): return lax.all_to_all(chunks, axes, 0, 0).reshape(value.shape)  88.5 us
    ppermute x3, starting transfers between devices, on_device(): lax.ppermute(mine, cam, [(i, (i - d) % owners) for i in range(owners)])  18.1 us
    pallas_call x8, Pallas kernels, call(): pl.pallas_call(kernel, out_shape=outs, in_specs=[VMEM] * len(args), out_s...  5.82 us
  transfers between devices with their start and end apart: 3, of which 0 were waited for; matrix products, arithmetic and copies ran while one was open for 2% of the time, Pallas kernels for 1%

profile of v12, /device:TPU:1, one launch (start us, length us, event | category | flops | bytes accessed | tf_op | source)
XLA Modules:
  0.0 117.0 jit_solution(16985350610650703122)
XLA Ops:
  0.6 0.8 mul.11
  1.5 15.1 %collective-permute-start.2 = (f32[9,4,128]{2,1,0:T(4,128)S(1)}, f32[9,4,128]{2,1,0:T(4,128)S(1)}, u32[]{:S(2)}, u32[]{:S(2)}) collective-permute-start(f32[9,4,128]{2,1,0:T(4,128)S(1)} %mul.12.mine), channel_id=1, source_target_pairs={{0,8},{1,9},{2,10},{3,11},{4,12},{5,13},{6,14},{7,15},{8,0},{9,1},... | collective-permute-start | bytes 55304 | tf_op jit(solution)/shard_map/ppermute | solution.py:544
  16.6 3.0 %collective-permute-start.1 = (f32[9,4,128]{2,1,0:T(4,128)S(1)}, f32[9,4,128]{2,1,0:T(4,128)S(1)}, u32[]{:S(2)}, u32[]{:S(2)}) collective-permute-start(f32[9,4,128]{2,1,0:T(4,128)S(1)} %mul.12.mine), channel_id=1, source_target_pairs={{0,1},{1,2},{2,3},{3,4},{4,5},{5,6},{6,7},{7,8},{8,9},{9,10},{10,1... | collective-permute-start | bytes 55304 | tf_op jit(solution)/shard_map/ppermute | solution.py:544
  19.6 0.7 fusion
  20.2 0.1 iota_add_fusion
  20.3 0.8 compare_reduce_fusion
  21.1 0.7 copy.32
  21.8 0.1 copy.31
  21.9 0.2 copy.30
  22.1 0.5 copy-done
  22.6 0.0 copy-done.1
  22.7 0.8 invert.1
  23.6 1.9 %apply_first.1 = (f32[160,128]{1,0:T(8,128)S(1)}, f32[144,128]{1,0:T(8,128)S(1)}) custom-call(f32[9,4,128]{2,1,0:T(4,128)S(1)} %mul.12.mine, f32[9,4,128]{2,1,0:T(4,128)S(1)} %collective-permute-done.after, f32[9,4,128]{2,1,0:T(4,128)S(1)} %collective-permute-done.1.before, f32[9,4,128]{2,1,0:T(4,128)S(1)} %collective-permute-done.2.across, ...), custom_call_target="tpu_custom_call" | custom-call | tf_op jit(solution)/shard_map/apply_first/pallas_call | solution.py:511
  25.4 17.3 %all_to_all.30 = f32[32,5,1,128]{3,2,1,0:T(1,128)S(1)} all-to-all(f32[32,5,1,128]{3,2,1,0:T(1,128)S(1)} %bitcast.36), channel_id=1, replica_groups=mesh['x'=8,'ya'=4,'yb'=2,'z'=8,'core'=2] {'x','yb','core'}, dimensions={0} | all-to-all | bytes 163840 | tf_op jit(solution)/shard_map/all_to_all | solution.py:526
  42.8 0.2 spread.1
  42.9 22.3 %all_to_all.31 = f32[32,7,1,128]{3,2,1,0:T(1,128)S(1)} all-to-all(f32[32,7,1,128]{3,2,1,0:T(1,128)S(1)} %bitcast.26), channel_id=1, replica_groups=mesh['x'=8,'ya'=4,'yb'=2,'z'=8,'core'=2] {'ya','z'}, dimensions={0} | all-to-all | bytes 229376 | tf_op jit(solution)/shard_map/all_to_all | solution.py:526
  65.3 0.2 combine.1
  65.4 13.1 %all_to_all.32 = f32[32,5,1,128]{3,2,1,0:T(1,128)S(1)} all-to-all(f32[32,5,1,128]{3,2,1,0:T(1,128)S(1)} %bitcast.30), channel_id=1, replica_groups=mesh['x'=8,'ya'=4,'yb'=2,'z'=8,'core'=2] {'x','yb','core'}, dimensions={0} | all-to-all | bytes 163840 | tf_op jit(solution)/shard_map/all_to_all | solution.py:526
  78.5 1.9 %apply_second.1 = (f32[160,128]{1,0:T(8,128)S(1)}, f32[144,128]{1,0:T(8,128)S(1)}, f32[144,128]{1,0:T(8,128)S(1)}) custom-call(f32[160,128]{1,0:T(8,128)S(1)} %bitcast.23, f32[144,128]{1,0:T(8,128)S(1)} %get-tuple-element.20.start, f32[180,128]{1,0:T(8,128)S(1)} %get-tuple-element.13.own, f32[18,4096]{1,0:T(8,128)S(1)} %bitcast.22, ...), custom_call_target="tpu_custom_call" | custom-call | tf_op jit(solution)/shard_map/apply_second/pallas_call | solution.py:511
  80.4 11.5 %all_to_all.33 = f32[32,5,1,128]{3,2,1,0:T(1,128)S(1)} all-to-all(f32[32,5,1,128]{3,2,1,0:T(1,128)S(1)} %bitcast.35), channel_id=1, replica_groups=mesh['x'=8,'ya'=4,'yb'=2,'z'=8,'core'=2] {'x','yb','core'}, dimensions={0} | all-to-all | bytes 163840 | tf_op jit(solution)/shard_map/all_to_all | solution.py:526
  92.0 0.1 own_block.1
  92.0 14.2 %all_to_all.34 = f32[32,3,1,128]{3,2,1,0:T(1,128)S(1)} all-to-all(f32[32,3,1,128]{3,2,1,0:T(1,128)S(1)} %bitcast.32), channel_id=1, replica_groups=mesh['x'=8,'ya'=4,'yb'=2,'z'=8,'core'=2] {'ya','z'}, dimensions={0} | all-to-all | bytes 98304 | tf_op jit(solution)/shard_map/all_to_all | solution.py:526
  106.2 10.1 %all_to_all.35 = f32[16,3,1,128]{3,2,1,0:T(1,128)S(1)} all-to-all(f32[16,3,1,128]{3,2,1,0:T(1,128)S(1)} %bitcast.34), channel_id=1, replica_groups=mesh['x'=8,'ya'=4,'yb'=2,'z'=8,'core'=2] {'x','yb'}, dimensions={0} | all-to-all | bytes 49152 | tf_op jit(solution)/shard_map/all_to_all | solution.py:526
  116.3 0.7 finish.1
  (20 shorter events, 0.1 us)
Async XLA Ops:
  0.6 21.2 %copy-start.6 = (f32[1,6,4096]{2,0,1:T(1,128)S(1)}, f32[1,6,4096]{2,0,1:T(1,128)}, u32[]{:S(2)}) copy-start(f32[1,6,4096]{2,0,1:T(1,128)} %param.14) | copy-start | bytes 294916
  0.6 21.2 %copy-start.5 = (f32[1,18,4096]{2,0,1:T(1,128)S(1)}, f32[1,18,4096]{2,0,1:T(1,128)}, u32[]{:S(2)}) copy-start(f32[1,18,4096]{2,0,1:T(1,128)} %param.13) | copy-start | bytes 884740
  1.5 22.0 %collective-permute-start.2 = (f32[9,4,128]{2,1,0:T(4,128)S(1)}, f32[9,4,128]{2,1,0:T(4,128)S(1)}, u32[]{:S(2)}, u32[]{:S(2)}) collective-permute-start(f32[9,4,128]{2,1,0:T(4,128)S(1)} %mul.12.mine), channel_id=1, source_target_pairs={{0,8},{1,9},{2,10},{3,11},{4,12},{5,13},{6,14},{7,15},{8,0},{9,1},... | collective-permute-start | bytes 55304 | tf_op jit(solution)/shard_map/ppermute | solution.py:544
  16.6 6.9 %collective-permute-start.1 = (f32[9,4,128]{2,1,0:T(4,128)S(1)}, f32[9,4,128]{2,1,0:T(4,128)S(1)}, u32[]{:S(2)}, u32[]{:S(2)}) collective-permute-start(f32[9,4,128]{2,1,0:T(4,128)S(1)} %mul.12.mine), channel_id=1, source_target_pairs={{0,1},{1,2},{2,3},{3,4},{4,5},{5,6},{6,7},{7,8},{8,9},{9,10},{10,1... | collective-permute-start | bytes 55304 | tf_op jit(solution)/shard_map/ppermute | solution.py:544
  19.6 4.0 %collective-permute-start = (f32[9,4,128]{2,1,0:T(4,128)S(1)}, f32[9,4,128]{2,1,0:T(4,128)S(1)}, u32[]{:S(2)}, u32[]{:S(2)}) collective-permute-start(f32[9,4,128]{2,1,0:T(4,128)S(1)} %mul.12.mine), channel_id=1, source_target_pairs={{0,15},{1,0},{2,1},{3,2},{4,3},{5,4},{6,5},{7,6},{8,7},{9,8},{10,9... | collective-permute-start | bytes 55304 | tf_op jit(solution)/shard_map/ppermute | solution.py:544
  21.9 0.8 copy-start
  21.9 0.8 copy-start.1
  21.9 0.8 copy-start.2
  21.9 0.8 copy-start.3
  21.9 0.8 copy-start.4
